TPU v7x, 256 devices: a whole 4x4x8 slice. The times are simulated.
256 devices in a mesh: seq: 32 (over y, z), head: 8 (over x, core).
Axes of the slice: x: 4, y: 4, z: 8, core: 2. Of those that a mesh axis runs over, the one named last changes fastest.
Arguments:
- queries: bfloat16 [32768, 32, 128], P('seq', 'head'), may hold values from -6 to 6
- key_rows: bfloat16 [32768, 32, 128], P('seq', 'head'), may hold values from -6 to 6
- value_rows: bfloat16 [32768, 32, 128], P('seq', 'head'), may hold values from -6 to 6
- out_grad: bfloat16 [32768, 4096], P('seq', 'head'), may hold values from -6 to 6
- out_weight: bfloat16 [32, 128, 4096], P('head'), may hold values from -0.09375 to 0.09375
Outputs:
- query_grad: bfloat16 [32768, 32, 128], P('seq', 'head')
- key_grad: bfloat16 [32768, 32, 128], P('seq', 'head')
- value_grad: bfloat16 [32768, 32, 128], P('seq', 'head')
All inputs are finite; a program needn't handle non-finite values.
Results may differ from a plain program's by a relative error of at most 0.0058.
Values may be sent and summed in bfloat16 or wider, within the bound.
No kernel may reach another device: no remote copies, remote signals or barrier semaphores. Data moves between devices by JAX's collectives and lax.ppermute only.
A program may use at most 128 MiB of HBM per device.

v0:
```python
import math

import jax
import jax.numpy as jnp
from jax import lax
from jax.sharding import PartitionSpec as P

BLOCK = 256


def body(queries, key_rows, value_rows, out_grad, out_weight):
    tokens = queries.shape[0]
    heads = queries.shape[1]
    depth = queries.shape[2]
    blocks = tokens // BLOCK
    factor = 1.0 / math.sqrt(depth * tokens * lax.axis_size("seq"))
    attn_grad = jnp.einsum(
        "tm,hdm->thd",
        lax.all_gather(out_grad, "head", axis=1, tiled=True),
        out_weight,
        preferred_element_type=jnp.float32,
    ).astype(jnp.bfloat16)
    layout = (blocks, BLOCK, heads, depth)
    query_blocks = queries.reshape(layout)
    key_blocks = key_rows.reshape(layout)
    value_blocks = value_rows.reshape(layout)
    grad_blocks = attn_grad.reshape(layout)
    kv_parts = jnp.einsum(
        "bthd,bthe->bhde", key_blocks, value_blocks, preferred_element_type=jnp.float32
    )
    qg_parts = jnp.einsum(
        "bthd,bthe->bhde", query_blocks, grad_blocks, preferred_element_type=jnp.float32
    )
    kv_total = jnp.sum(kv_parts, 0)
    qg_total = jnp.sum(qg_parts, 0)
    shards = lax.axis_size("seq")
    stacked = jnp.stack([kv_total, qg_total]).reshape(2, shards, -1)
    pieces = lax.all_to_all(stacked, "seq", split_axis=1, concat_axis=1, tiled=True)
    forward_sums = jnp.cumsum(pieces[0], 0) - pieces[0]
    reverse_sums = jnp.cumsum(pieces[1][::-1], 0)[::-1] - pieces[1]
    totals = lax.all_to_all(
        jnp.stack([forward_sums, reverse_sums]), "seq", split_axis=1, concat_axis=1, tiled=True
    )
    totals = totals.reshape(2, heads, depth, depth)
    before = totals[0]
    after = totals[1]
    first_zero = jnp.zeros((1, heads, depth, depth), jnp.float32)
    running = jnp.cumsum(kv_parts, 0)
    prefix = before[None] + jnp.concatenate([first_zero, running[:-1]], 0)
    backward_sums = jnp.cumsum(qg_parts[::-1], 0)[::-1]
    suffix = after[None] + jnp.concatenate([backward_sums[1:], first_zero], 0)
    prefix_bf = prefix.astype(jnp.bfloat16)
    suffix_bf = suffix.astype(jnp.bfloat16)
    causal = jnp.tril(jnp.ones((BLOCK, BLOCK), bool))
    qk_scores = jnp.einsum(
        "bthd,bshd->bhts", query_blocks, key_blocks, preferred_element_type=jnp.float32
    )
    qk_scores = jnp.where(causal, qk_scores, 0.0).astype(jnp.bfloat16)
    grad_scores = jnp.einsum(
        "bthd,bshd->bhts", grad_blocks, value_blocks, preferred_element_type=jnp.float32
    )
    grad_scores = jnp.where(causal, grad_scores, 0.0).astype(jnp.bfloat16)
    query_grad = jnp.einsum(
        "bhts,bshd->bthd", grad_scores, key_blocks, preferred_element_type=jnp.float32
    )
    query_grad = query_grad + jnp.einsum(
        "bthe,bhde->bthd", grad_blocks, prefix_bf, preferred_element_type=jnp.float32
    )
    key_grad = jnp.einsum(
        "bhts,bthd->bshd", grad_scores, query_blocks, preferred_element_type=jnp.float32
    )
    key_grad = key_grad + jnp.einsum(
        "bshe,bhde->bshd", value_blocks, suffix_bf, preferred_element_type=jnp.float32
    )
    value_grad = jnp.einsum(
        "bhts,bthe->bshe", qk_scores, grad_blocks, preferred_element_type=jnp.float32
    )
    value_grad = value_grad + jnp.einsum(
        "bshd,bhde->bshe", key_blocks, suffix_bf, preferred_element_type=jnp.float32
    )
    final_shape = (tokens, heads, depth)
    return (
        (factor * query_grad).astype(jnp.bfloat16).reshape(final_shape),
        (factor * key_grad).astype(jnp.bfloat16).reshape(final_shape),
        (factor * value_grad).astype(jnp.bfloat16).reshape(final_shape),
    )


def solution(mesh):
    placed = (
        P("seq", "head", None),
        P("seq", "head", None),
        P("seq", "head", None),
        P("seq", "head"),
        P("head", None, None),
    )
    return jax.shard_map(
        body,
        mesh=mesh,
        in_specs=placed,
        out_specs=(P("seq", "head", None), P("seq", "head", None), P("seq", "head", None)),
        check_vma=False,
    )
```

profile of v0, /device:TPU:8, one launch (start us, length us, event | category | flops | bytes accessed | tf_op | source)
XLA Modules:
  0.0 153.2 jit_solution(7390798430991049583)
XLA Ops:
  7.2 0.0 all-gather.2.cloned.1.call-start
  7.2 0.7 all-gather.2.cloned.1.call-update
  7.9 2.1 %fusion.38 = (f32[4,128,128]{2,1,0:T(8,128)S(1)}, f32[4,4,128,128]{3,2,1,0:T(8,128)S(1)}) fusion(bf16[4,256,4,128]{3,2,1,0:T(4,128)(2,1)} %bitcast.53, bf16[4,256,4,128]{3,2,1,0:T(4,128)(2,1)} %bitcast.46), kind=kOutput, calls=%fused_computation.48 | convolution fusion | flops 134414336 | bytes 3407872 | tf_op jit(solution)/shard_map/bthd,bthe->bhde/dot_general | solution.py:28
  10.0 0.0 copy-start.4
  10.1 54.9 %all-gather.2.cloned.1.call-done = bf16[1024,4096]{1,0:T(8,128)(2,1)} async-done(((bf16[1024,512]{1,0:T(8,128)(2,1)}), bf16[1024,4096]{1,0:T(8,128)(2,1)}) %all-gather.2.cloned.1.call-update) | async-done | bytes 8388624 | tf_op jit(solution)/shard_map/all_gather | solution.py:19
  65.0 8.2 %fusion.7 = bf16[1024,4,128]{2,0,1:T(8,128)(2,1)S(1)} fusion(bf16[4,128,4096]{2,1,0:T(8,128)(2,1)} %param.9, bf16[1024,4096]{1,0:T(8,128)(2,1)} %all-gather.2.cloned.1.call-done), kind=kOutput, calls=%fused_computation.12 | convolution fusion | flops 4295491584 | bytes 13631488 | tf_op jit(solution)/shard_map/tm,hdm->thd/dot_general | solution.py:17
  73.2 0.0 copy-start.7
  73.2 0.0 copy-done.4
  73.2 1.2 fusion.37
  74.5 0.0 copy-done.7
  74.5 1.1 copy.83
  75.7 1.2 copy.84
  76.9 10.2 %all-to-all-start = ((f32[2,32,2048]{2,0,1:T(2,128)}), f32[2,32,2048]{2,0,1:T(2,128)}, u32[]{:S(2)}, u32[]{:S(2)}) async-start(f32[2,32,2048]{2,0,1:T(2,128)} %copy.84), calls=%async_computation | async-start | bytes 1048576 | tf_op jit(solution)/shard_map/all_to_all | solution.py:38
  87.1 0.8 fusion.39
  87.9 0.0 copy-start.9
  87.9 1.0 copy-done.9
  88.9 0.1 rev.12
  89.0 0.8 fusion.40
  89.7 0.0 copy-start.5
  89.8 0.1 slice.37
  89.8 0.9 slice.31
  90.8 0.5 copy-done.5
  91.3 1.9 %select_convert_fusion.1 = bf16[4,4,256,256]{3,2,1,0:T(8,128)(2,1)S(1)} fusion(pred[256,256]{1,0:T(8,128)(4,1)S(1)} %iota_compare_fusion, bf16[4,256,4,128]{3,2,1,0:T(4,128)(2,1)S(1)} %bitcast.54, bf16[4,256,4,128]{3,1,0,2:T(8,128)(2,1)} %bitcast.57), kind=kOutput, calls=%fused_computation.3 | convolution fusion | flops 270532608 | bytes 4259840 | tf_op jit(solution)/shard_map/bthd,bshd->bhts/dot_general | solution.py:59
  93.2 9.9 %all-to-all-done = f32[2,32,2048]{2,0,1:T(2,128)} async-done(((f32[2,32,2048]{2,0,1:T(2,128)}), f32[2,32,2048]{2,0,1:T(2,128)}, u32[]{:S(2)}, u32[]{:S(2)}) %all-to-all-start) | async-done | bytes 524320 | tf_op jit(solution)/shard_map/all_to_all | solution.py:38
  103.1 1.7 %fusion.36 = (f32[1,32,2048]{2,0,1:T(1,128)S(1)}, f32[1,32,2048]{2,0,1:T(1,128)S(1)}) fusion(f32[2,32,2048]{2,0,1:T(2,128)} %all-to-all-done), kind=kLoop, calls=%fused_computation.46 | loop fusion | bytes 1048576 | tf_op jit(solution)/shard_map/slice | solution.py:39
  104.9 0.1 copy.114
  105.0 0.2 reduce_window_sum.34
  105.2 0.1 copy_subtract_fusion
  105.3 0.1 copy.158
  105.4 0.3 rev.10
  105.7 0.2 reduce_window_sum.35
  105.9 0.3 rev.11
  106.2 0.1 subtract_bitcast_fusion
  106.4 1.2 copy.87
  107.6 7.0 %all-to-all-start.1 = ((f32[2,32,2048]{2,0,1:T(2,128)}), f32[2,32,2048]{2,0,1:T(2,128)}, u32[]{:S(2)}, u32[]{:S(2)}) async-start(f32[2,32,2048]{2,0,1:T(2,128)} %copy.87), calls=%async_computation.1 | async-start | bytes 1048576 | tf_op jit(solution)/shard_map/all_to_all | solution.py:41
  114.6 0.0 copy-start
  114.6 3.4 %fusion.13 = f32[4,4,256,128]{3,2,1,0:T(8,128)} fusion(bf16[4,4,256,256]{3,2,1,0:T(8,128)(2,1)S(1)} %select_convert_fusion.1, bf16[4,256,4,128]{3,2,1,0:T(4,128)(2,1)} %bitcast.50), kind=kOutput, calls=%fused_computation.18 | convolution fusion | flops 268435456 | bytes 5242880 | tf_op jit(solution)/shard_map/bhts,bthd->bshd/dot_general | solution.py:69
  118.0 0.0 copy-done
  118.0 2.1 %fusion.24 = f32[4,4,256,128]{3,2,1,0:T(8,128)} fusion(bf16[4,4,256,256]{3,2,1,0:T(8,128)(2,1)S(1)} %select_convert_fusion.1, bf16[4,256,4,128]{3,2,1,0:T(4,128)(2,1)S(1)} %bitcast.47), kind=kOutput, calls=%fused_computation.28 | convolution fusion | flops 268435456 | bytes 5242880 | tf_op jit(solution)/shard_map/bhts,bshd->bthd/dot_general | solution.py:63
  120.0 3.9 %fusion.6 = f32[4,4,128,256]{3,2,1,0:T(8,128)} fusion(pred[256,256]{1,0:T(8,128)(4,1)S(1)} %iota_compare_fusion, bf16[4,256,4,128]{3,2,1,0:T(4,128)(2,1)} %bitcast.51, bf16[4,256,4,128]{3,2,1,0:T(4,128)(2,1)S(1)} %bitcast.48, bf16[4,256,4,128]{3,1,0,2:T(8,128)(2,1)} %bitcast.58), kind=kOutput, calls=%fused_computation.11 | convolution fusion | flops 538968064 | bytes 5308416 | tf_op jit(solution)/shard_map/bhts,bthe->bshe/dot_general | solution.py:75
  123.9 0.0 copy-start.3
  123.9 6.0 %all-to-all-done.1 = f32[2,32,2048]{2,0,1:T(2,128)} async-done(((f32[2,32,2048]{2,0,1:T(2,128)}), f32[2,32,2048]{2,0,1:T(2,128)}, u32[]{:S(2)}, u32[]{:S(2)}) %all-to-all-start.1) | async-done | bytes 524320 | tf_op jit(solution)/shard_map/all_to_all | solution.py:41
  129.9 2.5 %fusion.35 = (f32[1,32,2048]{2,0,1:T(1,128)S(1)}, f32[1,32,2048]{2,0,1:T(1,128)}) fusion(f32[2,32,2048]{2,0,1:T(2,128)} %all-to-all-done.1), kind=kLoop, calls=%fused_computation.45 | loop fusion | bytes 1048576 | tf_op jit(solution)/shard_map/slice | solution.py:46
  132.4 0.1 copy.93
  132.5 0.0 copy-done.3
  132.5 3.0 %fusion.10 = bf16[4,256,4,128]{1,3,2,0:T(8,128)(2,1)} fusion(f32[4,4,128,256]{3,2,1,0:T(8,128)} %fusion.6, bf16[4,256,4,128]{3,2,1,0:T(4,128)(2,1)S(1)} %bitcast.49, f32[3,4,128,128]{2,3,1,0:T(8,128)S(1)} %copy-done.3, f32[4,128,128]{1,2,0:T(8,128)S(1)} %copy.93), kind=kOutput, calls=%fused_computation.13 | convolution fusion | flops 136314880 | bytes 5242880 | tf_op jit(solution)/shard_map/bshd,bhde->bshe/dot_general | solution.py:78
  135.5 2.4 %copy.102 = bf16[4,256,4,128]{3,1,0,2:T(8,128)(2,1)} copy(bf16[4,256,4,128]{1,3,2,0:T(8,128)(2,1)} %fusion.10) | data formatting | bytes 2097152 | tf_op jit(solution)/shard_map/convert_element_type | solution.py:85
  137.9 3.1 %copy.105 = bf16[1024,4,128]{2,1,0:T(4,128)(2,1)} copy(bf16[1024,4,128]{2,0,1:T(8,128)(2,1)} %bitcast.60) | data formatting | bytes 2097152
  141.0 0.0 copy-done.2
  141.0 0.0 copy-done.6
  141.0 0.5 fusion.3
  141.5 0.0 copy-start.1
  141.5 0.0 copy-start.8
  141.6 0.0 slice-start
  141.6 0.0 copy-start.10
  141.6 0.1 copy.97
  141.7 1.8 %copy.104 = bf16[1024,4,128]{2,1,0:T(4,128)(2,1)} copy(bf16[1024,4,128]{2,0,1:T(8,128)(2,1)S(1)} %bitcast.61) | data formatting | bytes 2097152
  143.5 0.0 copy-done.1
  143.5 0.0 copy-done.8
  143.5 0.5 slice-done
  144.0 0.1 copy-done.10
  144.1 0.4 fusion.5
  144.5 0.1 copy.90
  144.6 1.8 %copy.103 = bf16[1024,4,128]{2,1,0:T(4,128)(2,1)} copy(bf16[1024,4,128]{2,0,1:T(8,128)(2,1)S(1)} %bitcast.62) | data formatting | bytes 2097152
  (7 shorter events, 0.2 us)
Async XLA Ops:
  7.2 57.8 %all-gather.2.cloned.1.call-start = ((), (), s32[]{:S(2)}) async-start(), calls=%async_computation.2 | async-start | bytes 9437184 | tf_op jit(solution)/shard_map/all_gather | solution.py:19
  10.0 63.2 %copy-start.4 = (bf16[1024,4,128]{2,1,0:T(4,128)(2,1)S(1)}, bf16[1024,4,128]{2,1,0:T(4,128)(2,1)}, u32[]{:S(2)}) copy-start(bf16[1024,4,128]{2,1,0:T(4,128)(2,1)} %param.5) | copy-start | bytes 3145732
  73.2 1.3 copy-start.7
  76.9 26.3 %all-to-all-start = ((f32[2,32,2048]{2,0,1:T(2,128)}), f32[2,32,2048]{2,0,1:T(2,128)}, u32[]{:S(2)}, u32[]{:S(2)}) async-start(f32[2,32,2048]{2,0,1:T(2,128)} %copy.84), calls=%async_computation | async-start | bytes 1048576 | tf_op jit(solution)/shard_map/all_to_all | solution.py:38
  87.9 1.0 copy-start.9
  89.7 1.5 copy-start.5
  107.6 22.3 %all-to-all-start.1 = ((f32[2,32,2048]{2,0,1:T(2,128)}), f32[2,32,2048]{2,0,1:T(2,128)}, u32[]{:S(2)}, u32[]{:S(2)}) async-start(f32[2,32,2048]{2,0,1:T(2,128)} %copy.87), calls=%async_computation.1 | async-start | bytes 1048576 | tf_op jit(solution)/shard_map/all_to_all | solution.py:41
  114.6 3.4 %copy-start = (bf16[1024,4,128]{2,1,0:T(4,128)(2,1)S(1)}, bf16[1024,4,128]{2,1,0:T(4,128)(2,1)}, u32[]{:S(2)}) copy-start(bf16[1024,4,128]{2,1,0:T(4,128)(2,1)} %param.6) | copy-start | bytes 3145732
  123.9 8.6 %copy-start.3 = (f32[3,4,128,128]{2,3,1,0:T(8,128)S(1)}, f32[3,4,128,128]{2,3,1,0:T(8,128)}, u32[]{:S(2)}) copy-start(f32[3,4,128,128]{2,3,1,0:T(8,128)} %slice.31) | copy-start | bytes 2359300
  135.5 5.5 %copy-start.2 = (f32[4,4,256,128]{3,2,1,0:T(8,128)S(1)}, f32[4,4,256,128]{3,2,1,0:T(8,128)}, u32[]{:S(2)}) copy-start(f32[4,4,256,128]{3,2,1,0:T(8,128)} %fusion.13) | copy-start | bytes 6291460
  137.9 3.1 %copy-start.6 = (bf16[1024,4,128]{2,1,0:T(4,128)(2,1)S(1)}, bf16[1024,4,128]{2,1,0:T(4,128)(2,1)}, u32[]{:S(2)}) copy-start(bf16[1024,4,128]{2,1,0:T(4,128)(2,1)} %param.7) | copy-start | bytes 3145732
  141.5 1.9 %copy-start.1 = (f32[4,4,256,128]{3,2,1,0:T(8,128)S(1)}, f32[4,4,256,128]{3,2,1,0:T(8,128)}, u32[]{:S(2)}) copy-start(f32[4,4,256,128]{3,2,1,0:T(8,128)} %fusion.24) | copy-start | bytes 6291460
  141.5 1.9 %copy-start.8 = (bf16[1024,4,128]{2,0,1:T(8,128)(2,1)S(1)}, bf16[1024,4,128]{2,0,1:T(8,128)(2,1)}, u32[]{:S(2)}) copy-start(bf16[1024,4,128]{2,0,1:T(8,128)(2,1)} %copy-done.7) | copy-start | bytes 3145732
  141.6 2.4 %slice-start = ((f32[4,4,128,128]{3,2,1,0:T(8,128)}), f32[3,4,128,128]{3,2,1,0:T(8,128)S(1)}, s32[]{:S(2)}) async-start(f32[4,4,128,128]{3,2,1,0:T(8,128)} %copy-done.9), calls=%async_computation.3 | async-start | bytes 1572864 | tf_op jit(solution)/shard_map/slice | solution.py:49
  141.6 2.5 %copy-start.10 = (f32[1,32,2048]{2,0,1:T(1,128)S(1)}, f32[1,32,2048]{2,0,1:T(1,128)}, u32[]{:S(2)}) copy-start(f32[1,32,2048]{2,0,1:T(1,128)} %get-tuple-element.13) | copy-start | bytes 786436
Sparse Core Ops, SparseCore 0:
  9.8 55.1 all-gather.1
where the time goes:
time: 156 us; the launch traced here: 153 us
  waiting for transfers between devices  71.5 us (46%)
  matrix products  26.8 us (17%)
  local copies, waits for them, and re-layouts  21.1 us (14%)
  starting transfers between devices  17.2 us (11%)
  between operations  14.3 us (9%)
  other arithmetic  2.3 us (1%)
    all_gather x1, waiting for transfers between devices, body(): lax.all_gather(out_grad, 'head', axis=1, tiled=True)  54.9 us
    all_to_all x1, starting transfers between devices, body(): lax.all_to_all(stacked, 'seq', split_axis=1, concat_axis=1, tiled=True)  10.2 us
    all_to_all x1, waiting for transfers between devices, body(): lax.all_to_all(stacked, 'seq', split_axis=1, concat_axis=1, tiled=True)  9.93 us
    unnamed x27, local copies, waits for them, and re-layouts  8.39 us
    dot_general x1, matrix products, body(): jnp.einsum('tm,hdm->thd', lax.all_gather(out_grad, 'head', axis=1, tiled=...  8.22 us
    all_to_all x1, starting transfers between devices, body(): lax.all_to_all(jnp.stack([forward_sums, reverse_sums]), 'seq', split_axis...  6.97 us
    all_to_all x1, waiting for transfers between devices, body(): lax.all_to_all(jnp.stack([forward_sums, reverse_sums]), 'seq', split_axis...  5.98 us
    dot_general x1, matrix products, body(): jnp.einsum('bhts,bthe->bshe', qk_scores, grad_blocks, preferred_element_t...  3.89 us
  transfers between devices with their start and end apart: 3, of which 3 were waited for; matrix products, arithmetic and copies ran while one was open for 10% of the time, Pallas kernels for 0%

commit v1 on v0

v1 whole, which is shorter than its diff:
```python
import math

import jax
import jax.numpy as jnp
from jax import lax
from jax.experimental import pallas as pl
from jax.experimental.pallas import tpu as pltpu
from jax.sharding import PartitionSpec as P

BLOCK = 256
F32 = jnp.float32
BF16 = jnp.bfloat16


def dot(a, b, ca, cb):
    return lax.dot_general(a, b, (((ca,), (cb,)), ((), ())), preferred_element_type=F32)


def params(mib=40):
    return pltpu.CompilerParams(vmem_limit_bytes=mib * 1024 * 1024)


def kv_kernel(heads, k_ref, v_ref, before_ref, total_ref, run):
    step = pl.program_id(0)

    @pl.when(step == 0)
    def _():
        run[...] = jnp.zeros_like(run)

    before_ref[0] = run[...]
    for h in range(heads):
        run[h] += dot(k_ref[h], v_ref[h], 0, 0)
    total_ref[...] = run[...].astype(BF16)


def kv_states(k, v):
    heads, tokens, depth = k.shape
    blocks = tokens // BLOCK
    spec = pl.BlockSpec((heads, BLOCK, depth), lambda b: (0, b, 0))
    return pl.pallas_call(
        lambda *refs: kv_kernel(heads, *refs),
        grid=(blocks,),
        in_specs=[spec, spec],
        out_specs=[
            pl.BlockSpec((1, heads, depth, depth), lambda b: (b, 0, 0, 0)),
            pl.BlockSpec((heads, depth, depth), lambda b: (0, 0, 0)),
        ],
        out_shape=[
            jax.ShapeDtypeStruct((blocks, heads, depth, depth), F32),
            jax.ShapeDtypeStruct((heads, depth, depth), BF16),
        ],
        scratch_shapes=[pltpu.VMEM((heads, depth, depth), F32)],
        compiler_params=params(),
        name="kv_states",
    )(k, v)


def attn_first_kernel(width, index_ref, *refs):
    pieces, w_ref, acc_ref = refs[:-2], refs[-2], refs[-1]
    total = None
    for i, piece in enumerate(pieces):
        start = pl.multiple_of(index_ref[i] * width, 128)
        part = dot(piece[...], w_ref[:, pl.ds(start, width)], 1, 1)
        total = part if total is None else total + part
    acc_ref[...] = total


def attn_first(pieces, index, w):
    tokens, width = pieces[0].shape
    rows = w.shape[0]
    spec = pl.BlockSpec((BLOCK, width), lambda b, i: (b, 0))
    return pl.pallas_call(
        lambda *refs: attn_first_kernel(width, *refs),
        grid_spec=pltpu.PrefetchScalarGridSpec(
            num_scalar_prefetch=1,
            grid=(tokens // BLOCK,),
            in_specs=[spec] * len(pieces) + [pl.BlockSpec(w.shape, lambda b, i: (0, 0))],
            out_specs=pl.BlockSpec((BLOCK, rows), lambda b, i: (b, 0)),
        ),
        out_shape=jax.ShapeDtypeStruct((tokens, rows), F32),
        compiler_params=params(),
        name="attn_first",
    )(index, *pieces, w)


def attn_last_kernel(heads, index_ref, a_ref, b_ref, wa_ref, wb_ref, acc_ref, qt_ref, g_ref, after_ref, total_ref, run):
    step = pl.program_id(0)
    depth = qt_ref.shape[1]

    @pl.when(step == 0)
    def _():
        run[...] = jnp.zeros_like(run)

    total = acc_ref[...] + dot(a_ref[...], wa_ref[...], 1, 1)
    total = (total + dot(b_ref[...], wb_ref[...], 1, 1)).astype(BF16)
    g_ref[...] = total
    after_ref[0] = run[...]
    for h in range(heads):
        run[h] += dot(qt_ref[h], total[:, h * depth : (h + 1) * depth], 1, 0)
    total_ref[...] = run[...].astype(BF16)


def attn_last(a, b, index, w, acc, qt):
    tokens, width = a.shape
    rows = w.shape[0]
    heads, depth, _ = qt.shape
    blocks = tokens // BLOCK
    last = blocks - 1
    piece = pl.BlockSpec((BLOCK, width), lambda s, i: (last - s, 0))
    wide = pl.BlockSpec((BLOCK, rows), lambda s, i: (last - s, 0))
    return pl.pallas_call(
        lambda *refs: attn_last_kernel(heads, *refs),
        grid_spec=pltpu.PrefetchScalarGridSpec(
            num_scalar_prefetch=1,
            grid=(blocks,),
            in_specs=[
                piece,
                piece,
                pl.BlockSpec((rows, width), lambda s, i: (0, i[0])),
                pl.BlockSpec((rows, width), lambda s, i: (0, i[1])),
                wide,
                pl.BlockSpec((heads, depth, BLOCK), lambda s, i: (0, 0, last - s)),
            ],
            out_specs=[
                wide,
                pl.BlockSpec((1, heads, depth, depth), lambda s, i: (last - s, 0, 0, 0)),
                pl.BlockSpec((heads, depth, depth), lambda s, i: (0, 0, 0)),
            ],
            scratch_shapes=[pltpu.VMEM((heads, depth, depth), F32)],
        ),
        out_shape=[
            jax.ShapeDtypeStruct((tokens, rows), BF16),
            jax.ShapeDtypeStruct((blocks, heads, depth, depth), F32),
            jax.ShapeDtypeStruct((heads, depth, depth), BF16),
        ],
        compiler_params=params(),
        name="attn_last",
    )(index, a, b, w, w, acc, qt)


def inner_kernel(heads, q_ref, k_ref, v_ref, g_ref, qi_ref, ki_ref, vi_ref):
    depth = q_ref.shape[2]
    row = lax.broadcasted_iota(jnp.int32, (BLOCK, BLOCK), 0)
    col = lax.broadcasted_iota(jnp.int32, (BLOCK, BLOCK), 1)
    for h in range(heads):
        lanes = slice(h * depth, (h + 1) * depth)
        q, k, v, g = q_ref[h], k_ref[h], v_ref[h], g_ref[:, lanes]
        grad = jnp.where(col <= row, dot(g, v, 1, 1), 0.0).astype(BF16)
        grad_t = jnp.where(row <= col, dot(v, g, 1, 1), 0.0).astype(BF16)
        score_t = jnp.where(row <= col, dot(k, q, 1, 1), 0.0).astype(BF16)
        qi_ref[:, lanes] = dot(grad, k, 1, 0)
        ki_ref[:, lanes] = dot(grad_t, q, 1, 0)
        vi_ref[:, lanes] = dot(score_t, g, 1, 0)


def inner(q, k, v, g):
    heads, tokens, depth = q.shape
    rows = heads * depth
    split = pl.BlockSpec((heads, BLOCK, depth), lambda b: (0, b, 0))
    wide = pl.BlockSpec((BLOCK, rows), lambda b: (b, 0))
    return pl.pallas_call(
        lambda *refs: inner_kernel(heads, *refs),
        grid=(tokens // BLOCK,),
        in_specs=[split, split, split, wide],
        out_specs=[wide] * 3,
        out_shape=[jax.ShapeDtypeStruct((tokens, rows), F32)] * 3,
        compiler_params=params(),
        name="inner",
    )(q, k, v, g)


def query_kernel(heads, factor, g_ref, qi_ref, local_ref, far_ref, out_ref, flat):
    depth = far_ref.shape[1]
    for h in range(heads):
        lanes = slice(h * depth, (h + 1) * depth)
        state = (far_ref[h].astype(F32) + local_ref[0, h]).astype(BF16)
        flat[:, h, :] = factor * (qi_ref[:, lanes] + dot(g_ref[:, lanes], state, 1, 1))
    out_ref[...] = flat[...].astype(BF16)


def query_out(g, qi, local, far, factor):
    tokens, rows = g.shape
    heads, depth, _ = far.shape
    wide = pl.BlockSpec((BLOCK, rows), lambda b: (b, 0))
    return pl.pallas_call(
        lambda *refs: query_kernel(heads, factor, *refs),
        grid=(tokens // BLOCK,),
        in_specs=[
            wide,
            wide,
            pl.BlockSpec((1, heads, depth, depth), lambda b: (b, 0, 0, 0)),
            pl.BlockSpec((heads, depth, depth), lambda b: (0, 0, 0)),
        ],
        out_specs=pl.BlockSpec((BLOCK, heads, depth), lambda b: (b, 0, 0)),
        out_shape=jax.ShapeDtypeStruct((tokens, heads, depth), BF16),
        scratch_shapes=[pltpu.VMEM((BLOCK, heads, depth), F32)],
        compiler_params=params(),
        name="query_out",
    )(g, qi, local, far)


def key_value_kernel(heads, factor, k_ref, v_ref, ki_ref, vi_ref, local_ref, far_ref, ko_ref, vo_ref, kf, vf):
    depth = far_ref.shape[1]
    for h in range(heads):
        lanes = slice(h * depth, (h + 1) * depth)
        state = (far_ref[h].astype(F32) + local_ref[0, h]).astype(BF16)
        kf[:, h, :] = factor * (ki_ref[:, lanes] + dot(v_ref[h], state, 1, 1))
        vf[:, h, :] = factor * (vi_ref[:, lanes] + dot(k_ref[h], state, 1, 0))
    ko_ref[...] = kf[...].astype(BF16)
    vo_ref[...] = vf[...].astype(BF16)


def key_value_out(k, v, ki, vi, local, far, factor):
    tokens, rows = ki.shape
    heads, depth, _ = far.shape
    split = pl.BlockSpec((heads, BLOCK, depth), lambda b: (0, b, 0))
    wide = pl.BlockSpec((BLOCK, rows), lambda b: (b, 0))
    out = pl.BlockSpec((BLOCK, heads, depth), lambda b: (b, 0, 0))
    return pl.pallas_call(
        lambda *refs: key_value_kernel(heads, factor, *refs),
        grid=(tokens // BLOCK,),
        in_specs=[
            split,
            split,
            wide,
            wide,
            pl.BlockSpec((1, heads, depth, depth), lambda b: (b, 0, 0, 0)),
            pl.BlockSpec((heads, depth, depth), lambda b: (0, 0, 0)),
        ],
        out_specs=[out, out],
        out_shape=[jax.ShapeDtypeStruct((tokens, heads, depth), BF16)] * 2,
        scratch_shapes=[pltpu.VMEM((BLOCK, heads, depth), F32)] * 2,
        compiler_params=params(),
        name="key_value_out",
    )(k, v, ki, vi, local, far)


def body(queries, key_rows, value_rows, out_grad, out_weight):
    tokens, heads, depth = queries.shape
    shards = lax.axis_size("seq")
    columns = lax.axis_size("head")
    chips = columns // 2
    factor = 1.0 / math.sqrt(depth * tokens * shards)

    def along(shift):
        return [(2 * x + c, 2 * ((x + shift) % chips) + c) for x in range(chips) for c in range(2)]

    def send(array, pairs):
        return lax.ppermute(array, "head", pairs)

    swap = [(i, i ^ 1) for i in range(columns)]
    right, left = along(1), along(-1)
    half = tokens // 2
    from_left = send(out_grad, right)
    from_right = send(out_grad, left)
    twin = send(out_grad, swap)
    far_top = send(from_left[:half], right)
    far_bottom = send(from_right[half:], left)
    from_left_twin = send(from_left, swap)
    from_right_twin = send(from_right, swap)
    far_top_twin = send(far_top, swap)
    far_bottom_twin = send(far_bottom, swap)

    me = lax.axis_index("head")
    chip, core = me // 2, me % 2

    def column(shift, other):
        return 2 * ((chip + shift) % chips) + (1 - core if other else core)

    w = out_weight.reshape(heads * depth, -1)

    q = queries.transpose(1, 0, 2)
    k = key_rows.transpose(1, 0, 2)
    v = value_rows.transpose(1, 0, 2)
    qt = queries.transpose(1, 2, 0)

    kv_local, kv_total = kv_states(k, v)
    rows = heads * depth // shards
    kv_pieces = lax.all_to_all(kv_total.reshape(shards, rows, depth), "seq", 0, 0, tiled=True)
    earlier = jnp.tril(jnp.ones((shards, shards), BF16), -1)
    later = jnp.triu(jnp.ones((shards, shards), BF16), 1)

    def scan(mask, pieces):
        sums = dot(mask, pieces.reshape(shards, rows * depth), 1, 0)
        return sums.astype(BF16).reshape(shards, rows, depth)

    kv_sums = scan(earlier, kv_pieces)

    index = jnp.stack(
        [column(0, 0), column(0, 1), column(-1, 0), column(-1, 1), column(1, 0), column(1, 1)]
    ).astype(jnp.int32)
    acc = attn_first(
        [out_grad, twin, from_left, from_left_twin, from_right, from_right_twin], index, w
    )
    far = jnp.concatenate([far_top, far_bottom], 0)
    far_twin = jnp.concatenate([far_top_twin, far_bottom_twin], 0)
    far_index = jnp.stack([column(2, 0), column(2, 1)]).astype(jnp.int32)
    grad, qg_local, qg_total = attn_last(far, far_twin, far_index, w, acc, qt)

    both = jnp.concatenate([qg_total.reshape(shards, rows, depth), kv_sums], 1)
    both = lax.all_to_all(both, "seq", 0, 0, tiled=True)
    qg_sums = scan(later, both[:, :rows])
    before = both[:, rows:].reshape(heads, depth, depth)
    after = lax.all_to_all(qg_sums, "seq", 0, 0, tiled=True).reshape(heads, depth, depth)

    qi, ki, vi = inner(q, k, v, grad)
    query_grad = query_out(grad, qi, kv_local, before, factor)
    key_grad, value_grad = key_value_out(k, v, ki, vi, qg_local, after, factor)
    return query_grad, key_grad, value_grad


def solution(mesh):
    placed = (
        P("seq", "head", None),
        P("seq", "head", None),
        P("seq", "head", None),
        P("seq", "head"),
        P("head", None, None),
    )
    return jax.shard_map(
        body,
        mesh=mesh,
        in_specs=placed,
        out_specs=(P("seq", "head", None), P("seq", "head", None), P("seq", "head", None)),
        check_vma=False,
    )
```

time: 156 us -> 127 us (0.81); the launches traced: 153 us -> 127 us
  waiting for transfers between devices: 71.5 us -> 43 us
  matrix products: 26.8 us -> 0.38 us
  Pallas kernels: 0 us -> 24.5 us
  blocking collectives: 0 us -> 15.6 us
  between operations: 14.3 us -> 0.96 us
  starting transfers between devices: 17.2 us -> 24.7 us
  local copies, waits for them, and re-layouts: 21.1 us -> 15 us
    all_gather x1 -> x0, waiting for transfers between devices: 54.9 us -> none  [body(): lax.all_gather(out_grad, 'head', axis=1, tiled=True)]
    ppermute x0 -> x9, waiting for transfers between devices: none -> 35.9 us  [send(): return lax.ppermute(array, 'head', pairs)]
    dot_general x10 -> x2, matrix products: 26.8 us -> 0.38 us  [dot(): lax.dot_general(a, b, (((ca,), (cb,)), ((), ())), preferred_element_type=...]
    pallas_call x0 -> x6, Pallas kernels: none -> 24.5 us  [the longest x1 6.24 us: attn_first(): pl.pallas_call(lambda *refs: attn_first_kernel(width, *refs), grid_spec=p...]
    all_to_all x0 -> x1, blocking collectives: none -> 15.6 us  [body(): both = lax.all_to_all(both, 'seq', 0, 0, tiled=True)]
    all_to_all x2, waiting for transfers between devices: 15.9 us -> 7.1 us  [the longest x1 7.1 us: body(): lax.all_to_all(kv_total.reshape(shards, rows, depth), 'seq', 0, 0, tiled=...]
    ppermute x0 -> x9, starting transfers between devices: none -> 7.28 us  [send(): return lax.ppermute(array, 'head', pairs)]
    unnamed x27 -> x28, local copies, waits for them, and re-layouts: 8.39 us -> 13.5 us
  transfers between devices with their start and end apart: 3 -> 11, of which waited for: 3 -> 4; matrix products, arithmetic and copies ran while one was open for 10% -> 7% of each run, Pallas kernels for 0% -> 8%
where the time goes in v1:
time: 127 us
  waiting for transfers between devices  43 us (34%)
  starting transfers between devices  24.7 us (19%)
  Pallas kernels  24.5 us (19%)
  blocking collectives  15.6 us (12%)
  local copies, waits for them, and re-layouts  15 us (12%)
  other arithmetic  2.9 us (2%)
    ppermute x9, waiting for transfers between devices, send(): return lax.ppermute(array, 'head', pairs)  35.9 us
    all_to_all x1, blocking collectives, body(): both = lax.all_to_all(both, 'seq', 0, 0, tiled=True)  15.6 us
    unnamed x28, local copies, waits for them, and re-layouts  13.5 us
    all_to_all x1, starting transfers between devices, body(): lax.all_to_all(kv_total.reshape(shards, rows, depth), 'seq', 0, 0, tiled=...  11.7 us
    ppermute x9, starting transfers between devices, send(): return lax.ppermute(array, 'head', pairs)  7.28 us
    all_to_all x1, waiting for transfers between devices, body(): lax.all_to_all(kv_total.reshape(shards, rows, depth), 'seq', 0, 0, tiled=...  7.1 us
    pallas_call x1, Pallas kernels, attn_first(): pl.pallas_call(lambda *refs: attn_first_kernel(width, *refs), grid_spec=p...  6.24 us
    all_to_all x1, starting transfers between devices, body(): lax.all_to_all(qg_sums, 'seq', 0, 0, tiled=True)  5.7 us
  transfers between devices with their start and end apart: 11, of which 4 were waited for; matrix products, arithmetic and copies ran while one was open for 7% of the time, Pallas kernels for 8%

profile of v1, /device:TPU:8, one launch (start us, length us, event | category | flops | bytes accessed | tf_op | source)
XLA Modules:
  0.0 126.9 jit_solution(12102522312519124196)
XLA Ops:
  0.6 0.0 copy-start.10
  0.6 0.0 copy-start.11
  0.7 2.8 %collective-permute-start.2 = (bf16[1024,512]{1,0:T(8,128)(2,1)}, bf16[1024,512]{1,0:T(8,128)(2,1)S(1)}, u32[]{:S(2)}, u32[]{:S(2)}) collective-permute-start(bf16[1024,512]{1,0:T(8,128)(2,1)} %refs_1_.1), channel_id=1, source_target_pairs={{0,6},{1,7},{2,0},{3,1},{4,2},{5,3},{6,4},{7,5},{8,14},{9,15},{10,... | collective-permute-start | bytes 3145736 | tf_op jit(solution)/shard_map/ppermute | solution.py:249
  3.5 0.0 collective-permute-start
  3.5 22.7 %collective-permute-done.2.refs_5_ = bf16[1024,512]{1,0:T(8,128)(2,1)S(1)} collective-permute-done((bf16[1024,512]{1,0:T(8,128)(2,1)}, bf16[1024,512]{1,0:T(8,128)(2,1)S(1)}, u32[]{:S(2)}, u32[]{:S(2)}) %collective-permute-start.2) | collective-permute-done | bytes 1048608 | tf_op jit(solution)/shard_map/ppermute | solution.py:249
  26.3 3.7 %collective-permute-start.3 = (bf16[512,512]{1,0:T(8,128)(2,1)S(1)}, bf16[512,512]{1,0:T(8,128)(2,1)}, u32[]{:S(2)}, u32[]{:S(2)}) collective-permute-start(bf16[512,512]{1,0:T(8,128)(2,1)S(1)} %slice.17), channel_id=1, source_target_pairs={{0,6},{1,7},{2,0},{3,1},{4,2},{5,3},{6,4},{7,5},{8,14},{9,15},{10,... | collective-permute-start | bytes 1572872 | tf_op jit(solution)/shard_map/ppermute | solution.py:249
  29.9 0.0 collective-permute-done.refs_3_
  29.9 1.1 slice.16
  31.0 0.1 collective-permute-start.1
  31.1 0.1 collective-permute-start.6
  31.2 0.5 collective-permute-start.7
  31.7 0.1 collective-permute-start.8
  31.8 8.4 %collective-permute-done.3 = bf16[512,512]{1,0:T(8,128)(2,1)} collective-permute-done((bf16[512,512]{1,0:T(8,128)(2,1)S(1)}, bf16[512,512]{1,0:T(8,128)(2,1)}, u32[]{:S(2)}, u32[]{:S(2)}) %collective-permute-start.3) | collective-permute-done | bytes 524320 | tf_op jit(solution)/shard_map/ppermute | solution.py:249
  40.2 0.0 collective-permute-start.5
  40.2 4.7 %collective-permute-done.1 = bf16[512,512]{1,0:T(8,128)(2,1)} collective-permute-done((bf16[512,512]{1,0:T(8,128)(2,1)S(1)}, bf16[512,512]{1,0:T(8,128)(2,1)}, u32[]{:S(2)}, u32[]{:S(2)}) %collective-permute-start.1) | collective-permute-done | bytes 524320 | tf_op jit(solution)/shard_map/ppermute | solution.py:249
  44.9 0.0 collective-permute-start.4
  44.9 0.0 copy-done.10
  44.9 0.0 copy-done.11
  44.9 0.3 copy_bitcast_fusion
  45.2 2.0 %kv_states.1 = (f32[4,4,128,128]{3,2,1,0:T(8,128)S(1)}, bf16[4,128,128]{2,1,0:T(8,128)(2,1)}) custom-call(bf16[4,1024,128]{2,1,0:T(8,128)(2,1)S(1)} %get-tuple-element.26.refs_1_.refs_0_, bf16[4,1024,128]{2,1,0:T(8,128)(2,1)S(1)} %get-tuple-element.25.refs_2_.refs_1_), custom_call_target="tpu_custom_call" | custom-call | tf_op jit(solution)/shard_map/kv_states/pallas_call | solution.py:40
  47.2 0.0 copy-start.8
  47.2 1.0 copy-done.8
  48.2 11.7 %all-to-all-start = ((bf16[32,16,128]{2,1,0:T(8,128)(2,1)}), bf16[32,16,128]{2,1,0:T(8,128)(2,1)S(1)}, u32[]{:S(2)}, u32[]{:S(2)}) async-start(bf16[32,16,128]{2,1,0:T(8,128)(2,1)} %bitcast.14), calls=%async_computation | async-start | bytes 262144 | tf_op jit(solution)/shard_map/all_to_all | solution.py:279
  60.0 2.4 %copy.8 = bf16[1024,4,128]{0,2,1:T(8,128)(2,1)} copy(bf16[1024,4,128]{2,1,0:T(4,128)(2,1)} %param.5) | data formatting | bytes 2097152 | tf_op args[0]
  62.4 0.1 stack.39.refs_0_
  62.5 0.1 pad_add_fusion.refs_0_
  62.5 7.1 %all-to-all-done = bf16[32,16,128]{2,1,0:T(8,128)(2,1)S(1)} async-done(((bf16[32,16,128]{2,1,0:T(8,128)(2,1)}), bf16[32,16,128]{2,1,0:T(8,128)(2,1)S(1)}, u32[]{:S(2)}, u32[]{:S(2)}) %all-to-all-start) | async-done | bytes 131104 | tf_op jit(solution)/shard_map/all_to_all | solution.py:279
  69.6 0.2 fusion
  69.9 0.0 copy-start
  69.9 1.4 %pad_maximum_fusion.refs_1_ = bf16[1024,512]{1,0:T(8,128)(2,1)S(1)} fusion(bf16[512,512]{1,0:T(8,128)(2,1)} %collective-permute-done.3, bf16[512,512]{1,0:T(8,128)(2,1)} %collective-permute-done.1), kind=kLoop, calls=%fused_computation.4 | loop fusion | flops 2097152 | bytes 2097152 | tf_op jit(solution)/shard_map/concatenate | solution.py:295
  71.3 0.0 collective-permute-done.5
  71.3 0.0 collective-permute-done.4
  71.3 1.4 %pad_maximum_fusion.1.refs_2_ = bf16[1024,512]{1,0:T(8,128)(2,1)S(1)} fusion(bf16[512,512]{1,0:T(8,128)(2,1)} %collective-permute-done.5, bf16[512,512]{1,0:T(8,128)(2,1)} %collective-permute-done.4), kind=kLoop, calls=%fused_computation.5 | loop fusion | flops 2097152 | bytes 2097152 | tf_op jit(solution)/shard_map/concatenate | solution.py:296
  72.7 0.0 collective-permute-done.6.refs_2_
  72.8 0.0 collective-permute-done.7.refs_4_
  72.8 0.0 collective-permute-done.8.refs_6_
  72.8 0.0 copy-done
  72.8 0.0 copy-start.1
  72.8 6.2 %attn_first.1.refs_5_ = f32[1024,512]{1,0:T(8,128)S(1)} custom-call(s32[6]{0:T(128)S(1)} %stack.39.refs_0_, bf16[1024,512]{1,0:T(8,128)(2,1)} %refs_1_.1, bf16[1024,512]{1,0:T(8,128)(2,1)} %collective-permute-done.6.refs_2_, bf16[1024,512]{1,0:T(8,128)(2,1)} %collective-permute-done.refs_3_, bf16[1024,512]{1,0:T(8,128)(2,1)} %collective-permute-done.7.refs_4_, ...), custom_call_target="tpu_custom_call" | custom-call | tf_op jit(solution)/shard_map/attn_first/pallas_call | solution.py:72
  79.0 0.0 copy-done.1
  79.1 3.6 %attn_last.1 = (bf16[1024,512]{1,0:T(8,128)(2,1)S(1)}, f32[4,4,128,128]{3,2,1,0:T(8,128)S(1)}, bf16[4,128,128]{2,1,0:T(8,128)(2,1)S(1)}) custom-call(s32[2]{0:T(128)S(1)} %pad_add_fusion.refs_0_, bf16[1024,512]{1,0:T(8,128)(2,1)S(1)} %pad_maximum_fusion.refs_1_, bf16[1024,512]{1,0:T(8,128)(2,1)S(1)} %pad_maximum_fusion.1.refs_2_, ...), custom_call_target="tpu_custom_call" | custom-call | tf_op jit(solution)/shard_map/attn_last/pallas_call | solution.py:111
  82.7 0.0 copy-start.6
  82.7 1.0 copy-done.6
  83.7 15.6 %all_to_all.15 = bf16[32,32,128]{2,1,0:T(8,128)(2,1)S(1)} all-to-all(bf16[32,32,128]{2,1,0:T(8,128)(2,1)S(1)} %pad_maximum_fusion.2), channel_id=1, replica_groups=mesh['seq'=32,'head'=8] {'seq'}, dimensions={0} | all-to-all | bytes 524288 | tf_op jit(solution)/shard_map/all_to_all | solution.py:301
  99.3 0.2 fusion.1
  99.4 0.7 copy.15
  100.1 5.7 %all-to-all-start.2 = ((bf16[32,16,128]{2,1,0:T(8,128)(2,1)}), bf16[32,16,128]{2,1,0:T(8,128)(2,1)S(1)}, u32[]{:S(2)}, u32[]{:S(2)}) async-start(bf16[32,16,128]{2,1,0:T(8,128)(2,1)} %bitcast.24), calls=%async_computation.2 | async-start | bytes 262144 | tf_op jit(solution)/shard_map/all_to_all | solution.py:304
  105.8 1.4 %copy.27 = bf16[1024,4,128]{2,0,1:T(8,128)(2,1)S(1)} copy(bf16[1024,4,128]{2,1,0:T(4,128)(2,1)} %param.5) | data formatting | bytes 2097152 | tf_op args[0]
  107.2 0.0 copy-start.9
  107.2 4.6 %inner.1 = (f32[1024,512]{1,0:T(8,128)S(1)}, f32[1024,512]{1,0:T(8,128)S(1)}, f32[1024,512]{1,0:T(8,128)S(1)}) custom-call(bf16[4,1024,128]{2,1,0:T(8,128)(2,1)S(1)} %bitcast.38, bf16[4,1024,128]{2,1,0:T(8,128)(2,1)S(1)} %get-tuple-element.26.refs_1_.refs_0_, bf16[4,1024,128]{2,1,0:T(8,128)(2,1)S(1)} %get-tuple-element.25.refs_2_.refs_1_, ...), custom_call_target="tpu_custom_call" | custom-call | tf_op jit(solution)/shard_map/inner/pallas_call | solution.py:161
  111.8 0.0 copy-start.2
  111.8 1.3 %copy-done.2 = f32[1024,512]{1,0:T(8,128)} copy-done((f32[1024,512]{1,0:T(8,128)}, f32[1024,512]{1,0:T(8,128)S(1)}, u32[]{:S(2)}) %copy-start.2) | copy-done | bytes 2097176
  113.1 0.0 copy-start.4
  113.1 1.3 %copy-done.4 = f32[1024,512]{1,0:T(8,128)} copy-done((f32[1024,512]{1,0:T(8,128)}, f32[1024,512]{1,0:T(8,128)S(1)}, u32[]{:S(2)}) %copy-start.4) | copy-done | bytes 2097176
  114.4 0.0 copy-done.9
  114.4 3.2 %query_out.1 = bf16[1024,4,128]{2,1,0:T(4,128)(2,1)} custom-call(bf16[1024,512]{1,0:T(8,128)(2,1)S(1)} %get-tuple-element.13.refs_3_.refs_0_, f32[1024,512]{1,0:T(8,128)S(1)} %get-tuple-element.14.refs_1_, f32[4,4,128,128]{3,2,1,0:T(8,128)S(1)} %copy-done.9, bf16[4,128,128]{2,1,0:T(8,128)(2,1)S(1)} %bitcast.41), custom_call_target="tpu_custom_call" | custom-call | tf_op jit(solution)/shard_map/query_out/pallas_call | solution.py:185
  117.7 0.0 all-to-all-done.2
  117.7 0.0 copy-start.3
  117.7 1.6 %copy-done.3 = f32[1024,512]{1,0:T(8,128)S(1)} copy-done((f32[1024,512]{1,0:T(8,128)S(1)}, f32[1024,512]{1,0:T(8,128)}, u32[]{:S(2)}) %copy-start.3) | copy-done | bytes 2097176
  119.3 0.0 copy-start.5
  119.3 1.6 %copy-done.5 = f32[1024,512]{1,0:T(8,128)S(1)} copy-done((f32[1024,512]{1,0:T(8,128)S(1)}, f32[1024,512]{1,0:T(8,128)}, u32[]{:S(2)}) %copy-start.5) | copy-done | bytes 2097176
  120.8 0.0 copy-start.7
  120.9 1.2 copy-done.7
  122.1 4.9 %key_value_out.1 = (bf16[1024,4,128]{2,1,0:T(4,128)(2,1)}, bf16[1024,4,128]{2,1,0:T(4,128)(2,1)}) custom-call(bf16[4,1024,128]{2,1,0:T(8,128)(2,1)S(1)} %get-tuple-element.26.refs_1_.refs_0_, bf16[4,1024,128]{2,1,0:T(8,128)(2,1)S(1)} %get-tuple-element.25.refs_2_.refs_1_, f32[1024,512]{1,0:T(8,128)S(1)} %copy-done.3, f32[1024,512]{1,0:T(8,128)S(1)} %copy-done.5, ...), custom_call_target="tpu_custom_call" | custom-call | tf_op jit(solution)/shard_map/key_value_out/pallas_call | solution.py:219
  (5 shorter events, 0.1 us)
Async XLA Ops:
  0.6 44.3 %copy-start.10 = (bf16[1024,4,128]{2,1,0:T(4,128)(2,1)S(1)}, bf16[1024,4,128]{2,1,0:T(4,128)(2,1)}, u32[]{:S(2)}) copy-start(bf16[1024,4,128]{2,1,0:T(4,128)(2,1)} %param.7) | copy-start | bytes 3145732
  0.6 44.3 %copy-start.11 = (bf16[1024,4,128]{2,1,0:T(4,128)(2,1)S(1)}, bf16[1024,4,128]{2,1,0:T(4,128)(2,1)}, u32[]{:S(2)}) copy-start(bf16[1024,4,128]{2,1,0:T(4,128)(2,1)} %param.6) | copy-start | bytes 3145732
  0.7 25.6 %collective-permute-start.2 = (bf16[1024,512]{1,0:T(8,128)(2,1)}, bf16[1024,512]{1,0:T(8,128)(2,1)S(1)}, u32[]{:S(2)}, u32[]{:S(2)}) collective-permute-start(bf16[1024,512]{1,0:T(8,128)(2,1)} %refs_1_.1), channel_id=1, source_target_pairs={{0,6},{1,7},{2,0},{3,1},{4,2},{5,3},{6,4},{7,5},{8,14},{9,15},{10,... | collective-permute-start | bytes 3145736 | tf_op jit(solution)/shard_map/ppermute | solution.py:249
  3.5 26.4 %collective-permute-start = (bf16[1024,512]{1,0:T(8,128)(2,1)}, bf16[1024,512]{1,0:T(8,128)(2,1)}, u32[]{:S(2)}, u32[]{:S(2)}) collective-permute-start(bf16[1024,512]{1,0:T(8,128)(2,1)} %refs_1_.1), channel_id=1, source_target_pairs={{0,2},{1,3},{2,4},{3,5},{4,6},{5,7},{6,0},{7,1},{8,10},{9,11},{10,... | collective-permute-start | bytes 3145736 | tf_op jit(solution)/shard_map/ppermute | solution.py:249
  26.3 14.0 %collective-permute-start.3 = (bf16[512,512]{1,0:T(8,128)(2,1)S(1)}, bf16[512,512]{1,0:T(8,128)(2,1)}, u32[]{:S(2)}, u32[]{:S(2)}) collective-permute-start(bf16[512,512]{1,0:T(8,128)(2,1)S(1)} %slice.17), channel_id=1, source_target_pairs={{0,6},{1,7},{2,0},{3,1},{4,2},{5,3},{6,4},{7,5},{8,14},{9,15},{10,... | collective-permute-start | bytes 1572872 | tf_op jit(solution)/shard_map/ppermute | solution.py:249
  31.0 13.9 %collective-permute-start.1 = (bf16[512,512]{1,0:T(8,128)(2,1)S(1)}, bf16[512,512]{1,0:T(8,128)(2,1)}, u32[]{:S(2)}, u32[]{:S(2)}) collective-permute-start(bf16[512,512]{1,0:T(8,128)(2,1)S(1)} %slice.16), channel_id=1, source_target_pairs={{0,2},{1,3},{2,4},{3,5},{4,6},{5,7},{6,0},{7,1},{8,10},{9,11},{10,... | collective-permute-start | bytes 1572872 | tf_op jit(solution)/shard_map/ppermute | solution.py:249
  31.1 41.6 %collective-permute-start.6 = (bf16[1024,512]{1,0:T(8,128)(2,1)}, bf16[1024,512]{1,0:T(8,128)(2,1)}, u32[]{:S(2)}, u32[]{:S(2)}) collective-permute-start(bf16[1024,512]{1,0:T(8,128)(2,1)} %refs_1_.1), channel_id=1, source_target_pairs={{0,1},{1,0},{2,3},{3,2},{4,5},{5,4},{6,7},{7,6},{8,9},{9,8},{10,11... | collective-permute-start | bytes 3145736 | tf_op jit(solution)/shard_map/ppermute | solution.py:249
  31.2 41.6 %collective-permute-start.7 = (bf16[1024,512]{1,0:T(8,128)(2,1)}, bf16[1024,512]{1,0:T(8,128)(2,1)}, u32[]{:S(2)}, u32[]{:S(2)}) collective-permute-start(bf16[1024,512]{1,0:T(8,128)(2,1)} %collective-permute-done.refs_3_), channel_id=1, source_target_pairs={{0,1},{1,0},{2,3},{3,2},{4,5},{5,4},{6,7},{7,6},{8,9},{9,8},{10,11... | collective-permute-start | bytes 3145736 | tf_op jit(solution)/shard_map/ppermute | solution.py:249
  31.7 41.1 %collective-permute-start.8 = (bf16[1024,512]{1,0:T(8,128)(2,1)S(1)}, bf16[1024,512]{1,0:T(8,128)(2,1)}, u32[]{:S(2)}, u32[]{:S(2)}) collective-permute-start(bf16[1024,512]{1,0:T(8,128)(2,1)S(1)} %collective-permute-done.2.refs_5_), channel_id=1, source_target_pairs={{0,1},{1,0},{2,3},{3,2},{4,5},{5,4},{6,7},{7,6},{8,9},{9,8},{10,11... | collective-permute-start | bytes 3145736 | tf_op jit(solution)/shard_map/ppermute | solution.py:249
  40.2 31.1 %collective-permute-start.5 = (bf16[512,512]{1,0:T(8,128)(2,1)}, bf16[512,512]{1,0:T(8,128)(2,1)}, u32[]{:S(2)}, u32[]{:S(2)}) collective-permute-start(bf16[512,512]{1,0:T(8,128)(2,1)} %collective-permute-done.3), channel_id=1, source_target_pairs={{0,1},{1,0},{2,3},{3,2},{4,5},{5,4},{6,7},{7,6},{8,9},{9,8},{10,11... | collective-permute-start | bytes 1572872 | tf_op jit(solution)/shard_map/ppermute | solution.py:249
  44.9 26.4 %collective-permute-start.4 = (bf16[512,512]{1,0:T(8,128)(2,1)}, bf16[512,512]{1,0:T(8,128)(2,1)}, u32[]{:S(2)}, u32[]{:S(2)}) collective-permute-start(bf16[512,512]{1,0:T(8,128)(2,1)} %collective-permute-done.1), channel_id=1, source_target_pairs={{0,1},{1,0},{2,3},{3,2},{4,5},{5,4},{6,7},{7,6},{8,9},{9,8},{10,11... | collective-permute-start | bytes 1572872 | tf_op jit(solution)/shard_map/ppermute | solution.py:249
  47.2 1.0 copy-start.8
  48.2 21.5 %all-to-all-start = ((bf16[32,16,128]{2,1,0:T(8,128)(2,1)}), bf16[32,16,128]{2,1,0:T(8,128)(2,1)S(1)}, u32[]{:S(2)}, u32[]{:S(2)}) async-start(bf16[32,16,128]{2,1,0:T(8,128)(2,1)} %bitcast.14), calls=%async_computation | async-start | bytes 262144 | tf_op jit(solution)/shard_map/all_to_all | solution.py:279
  69.9 2.9 %copy-start = (bf16[4,128,4096]{2,1,0:T(8,128)(2,1)S(1)}, bf16[4,128,4096]{2,1,0:T(8,128)(2,1)}, u32[]{:S(2)}) copy-start(bf16[4,128,4096]{2,1,0:T(8,128)(2,1)} %param.9) | copy-start | bytes 12582916
  72.8 6.3 %copy-start.1 = (bf16[1024,4,128]{0,2,1:T(8,128)(2,1)S(1)}, bf16[1024,4,128]{0,2,1:T(8,128)(2,1)}, u32[]{:S(2)}) copy-start(bf16[1024,4,128]{0,2,1:T(8,128)(2,1)} %copy.8) | copy-start | bytes 3145732
  82.7 1.0 copy-start.6
  100.1 17.6 %all-to-all-start.2 = ((bf16[32,16,128]{2,1,0:T(8,128)(2,1)}), bf16[32,16,128]{2,1,0:T(8,128)(2,1)S(1)}, u32[]{:S(2)}, u32[]{:S(2)}) async-start(bf16[32,16,128]{2,1,0:T(8,128)(2,1)} %bitcast.24), calls=%async_computation.2 | async-start | bytes 262144 | tf_op jit(solution)/shard_map/all_to_all | solution.py:304
  107.2 7.3 %copy-start.9 = (f32[4,4,128,128]{3,2,1,0:T(8,128)S(1)}, f32[4,4,128,128]{3,2,1,0:T(8,128)}, u32[]{:S(2)}) copy-start(f32[4,4,128,128]{3,2,1,0:T(8,128)} %copy-done.8) | copy-start | bytes 3145732
  111.8 1.4 %copy-start.2 = (f32[1024,512]{1,0:T(8,128)}, f32[1024,512]{1,0:T(8,128)S(1)}, u32[]{:S(2)}) copy-start(f32[1024,512]{1,0:T(8,128)S(1)} %get-tuple-element.18.refs_2_) | copy-start | bytes 6291460
  113.1 1.3 %copy-start.4 = (f32[1024,512]{1,0:T(8,128)}, f32[1024,512]{1,0:T(8,128)S(1)}, u32[]{:S(2)}) copy-start(f32[1024,512]{1,0:T(8,128)S(1)} %get-tuple-element.19.refs_3_) | copy-start | bytes 6291460
  117.7 1.6 %copy-start.3 = (f32[1024,512]{1,0:T(8,128)S(1)}, f32[1024,512]{1,0:T(8,128)}, u32[]{:S(2)}) copy-start(f32[1024,512]{1,0:T(8,128)} %copy-done.2) | copy-start | bytes 6291460
  119.3 1.6 %copy-start.5 = (f32[1024,512]{1,0:T(8,128)S(1)}, f32[1024,512]{1,0:T(8,128)}, u32[]{:S(2)}) copy-start(f32[1024,512]{1,0:T(8,128)} %copy-done.4) | copy-start | bytes 6291460
  120.8 1.2 copy-start.7

commit v2 on v1

v2 whole, which is shorter than its diff:
```python
import math

import jax
import jax.numpy as jnp
from jax import lax
from jax.experimental import pallas as pl
from jax.experimental.pallas import tpu as pltpu
from jax.sharding import PartitionSpec as P

BLOCK = 256
STEP = 512
F32 = jnp.float32
BF16 = jnp.bfloat16


def dot(a, b, ca, cb):
    return lax.dot_general(a, b, (((ca,), (cb,)), ((), ())), preferred_element_type=F32)


def params(mib):
    return pltpu.CompilerParams(vmem_limit_bytes=mib * 1024 * 1024)


def in_hbm(array):
    return pltpu.with_memory_space_constraint(array, pltpu.HBM)


def cost(flops, moved):
    return pl.CostEstimate(flops=flops, bytes_accessed=moved, transcendentals=0)


def kv_kernel(heads, k_ref, v_ref, before_ref, total_ref, run):
    step = pl.program_id(0)

    @pl.when(step == 0)
    def _():
        run[...] = jnp.zeros_like(run)

    before_ref[0] = run[...]
    for h in range(heads):
        run[h] += dot(k_ref[h], v_ref[h], 0, 0)
    total_ref[...] = run[...].astype(BF16)


def kv_states(k, v):
    heads, tokens, depth = k.shape
    blocks = tokens // BLOCK
    spec = pl.BlockSpec((heads, BLOCK, depth), lambda b: (0, b, 0))
    return pl.pallas_call(
        lambda *refs: kv_kernel(heads, *refs),
        grid=(blocks,),
        in_specs=[spec, spec],
        out_specs=[
            pl.BlockSpec((1, heads, depth, depth), lambda b: (b, 0, 0, 0)),
            pl.BlockSpec((heads, depth, depth), lambda b: (0, 0, 0)),
        ],
        out_shape=[
            pltpu.HBM((blocks, heads, depth, depth), F32),
            jax.ShapeDtypeStruct((heads, depth, depth), BF16),
        ],
        scratch_shapes=[pltpu.VMEM((heads, depth, depth), F32)],
        compiler_params=params(6),
        name="kv_states",
    )(k, v)


def attn_add_kernel(count, acc_ref, *refs):
    total = None if acc_ref is None else acc_ref[...]
    for i in range(count):
        part = dot(refs[i][...], refs[count + i][...], 1, 1)
        total = part if total is None else total + part
    refs[-1][...] = total


def attn_add(acc, pieces, index, w, name):
    tokens, width = pieces[0].shape
    rows = w.shape[0]
    count = len(pieces)
    spec = pl.BlockSpec((BLOCK, width), lambda b, i: (b, 0))
    wide = pl.BlockSpec((BLOCK, rows), lambda b, i: (b, 0))
    weights = [pl.BlockSpec((rows, width), lambda b, i, j=j: (0, i[j])) for j in range(count)]
    first = [] if acc is None else [acc]
    return pl.pallas_call(
        lambda i, *refs: attn_add_kernel(count, *(refs if first else (None, *refs))),
        grid_spec=pltpu.PrefetchScalarGridSpec(
            num_scalar_prefetch=1,
            grid=(tokens // BLOCK,),
            in_specs=[wide] * len(first) + [spec] * count + weights,
            out_specs=wide,
        ),
        out_shape=jax.ShapeDtypeStruct((tokens, rows), F32),
        compiler_params=params(6 + 3 * count),
        cost_estimate=cost(2 * tokens * rows * width * count, 4 * tokens * rows),
        name=name,
    )(index, *first, *pieces, *([w] * count))


def attn_last_kernel(heads, i_ref, a_ref, b_ref, wa_ref, wb_ref, acc_ref, q_ref, g_ref, after_ref, total_ref, run):
    depth = q_ref.shape[2]

    @pl.when(pl.program_id(0) == 0)
    def _():
        run[...] = jnp.zeros_like(run)

    total = acc_ref[...] + dot(a_ref[...], wa_ref[...], 1, 1)
    total = (total + dot(b_ref[...], wb_ref[...], 1, 1)).astype(BF16)
    g_ref[...] = total
    for j in reversed(range(a_ref.shape[0] // BLOCK)):
        part = slice(j * BLOCK, (j + 1) * BLOCK)
        after_ref[j] = run[...]
        for h in range(heads):
            run[h] += dot(q_ref[h, part, :], total[part, h * depth : (h + 1) * depth], 0, 0)
    total_ref[...] = run[...].astype(BF16)


def attn_last(a, b, index, w, acc, q):
    tokens, width = a.shape
    rows = w.shape[0]
    heads, _, depth = q.shape
    steps = tokens // STEP
    last = steps - 1
    blocks = STEP // BLOCK
    piece = pl.BlockSpec((STEP, width), lambda s, i: (last - s, 0))
    wide = pl.BlockSpec((STEP, rows), lambda s, i: (last - s, 0))
    return pl.pallas_call(
        lambda *refs: attn_last_kernel(heads, *refs),
        grid_spec=pltpu.PrefetchScalarGridSpec(
            num_scalar_prefetch=1,
            grid=(steps,),
            in_specs=[
                piece,
                piece,
                pl.BlockSpec((rows, width), lambda s, i: (0, i[0])),
                pl.BlockSpec((rows, width), lambda s, i: (0, i[1])),
                wide,
                pl.BlockSpec((heads, STEP, depth), lambda s, i: (0, last - s, 0)),
            ],
            out_specs=[
                wide,
                pl.BlockSpec((blocks, heads, depth, depth), lambda s, i: (last - s, 0, 0, 0)),
                pl.BlockSpec((heads, depth, depth), lambda s, i: (0, 0, 0)),
            ],
            scratch_shapes=[pltpu.VMEM((heads, depth, depth), F32)],
        ),
        out_shape=[
            pltpu.HBM((tokens, rows), BF16),
            pltpu.HBM((tokens // BLOCK, heads, depth, depth), F32),
            jax.ShapeDtypeStruct((heads, depth, depth), BF16),
        ],
        compiler_params=params(18),
        cost_estimate=cost(5 * tokens * rows * width, 4 * tokens * rows),
        name="attn_last",
    )(index, a, b, w, w, acc, q)


def inner_kernel(heads, q_ref, k_ref, v_ref, g_ref, qi_ref, ki_ref, vi_ref):
    depth = q_ref.shape[2]
    row = lax.broadcasted_iota(jnp.int32, (BLOCK, BLOCK), 0)
    col = lax.broadcasted_iota(jnp.int32, (BLOCK, BLOCK), 1)
    for h in range(heads):
        lanes = slice(h * depth, (h + 1) * depth)
        q, k, v, g = q_ref[h], k_ref[h], v_ref[h], g_ref[:, lanes]
        grad = jnp.where(col <= row, dot(g, v, 1, 1), 0.0).astype(BF16)
        grad_t = jnp.where(row <= col, dot(v, g, 1, 1), 0.0).astype(BF16)
        score_t = jnp.where(row <= col, dot(k, q, 1, 1), 0.0).astype(BF16)
        qi_ref[:, lanes] = dot(grad, k, 1, 0)
        ki_ref[:, lanes] = dot(grad_t, q, 1, 0)
        vi_ref[:, lanes] = dot(score_t, g, 1, 0)


def inner(q, k, v, g):
    heads, tokens, depth = q.shape
    rows = heads * depth
    split = pl.BlockSpec((heads, BLOCK, depth), lambda b: (0, b, 0))
    wide = pl.BlockSpec((BLOCK, rows), lambda b: (b, 0))
    return pl.pallas_call(
        lambda *refs: inner_kernel(heads, *refs),
        grid=(tokens // BLOCK,),
        in_specs=[split, split, split, wide],
        out_specs=[wide] * 3,
        out_shape=[jax.ShapeDtypeStruct((tokens, rows), F32)] + [pltpu.HBM((tokens, rows), F32)] * 2,
        compiler_params=params(10),
        name="inner",
    )(q, k, v, g)


def query_kernel(heads, factor, g_ref, qi_ref, local_ref, far_ref, out_ref):
    depth = far_ref.shape[1]
    for j in range(g_ref.shape[0] // BLOCK):
        rows = slice(j * BLOCK, (j + 1) * BLOCK)
        parts = []
        for h in range(heads):
            lanes = slice(h * depth, (h + 1) * depth)
            state = (far_ref[h].astype(F32) + local_ref[j, h]).astype(BF16)
            parts.append(factor * (qi_ref[rows, lanes] + dot(g_ref[rows, lanes], state, 1, 1)))
        out_ref[rows] = jnp.concatenate(parts, 1).astype(BF16).reshape(BLOCK, heads, depth)


def query_out(g, qi, local, far, factor):
    tokens, rows = g.shape
    heads, depth, _ = far.shape
    step = STEP
    wide = pl.BlockSpec((step, rows), lambda b: (b, 0))
    return pl.pallas_call(
        lambda *refs: query_kernel(heads, factor, *refs),
        grid=(tokens // step,),
        in_specs=[
            wide,
            wide,
            pl.BlockSpec((step // BLOCK, heads, depth, depth), lambda b: (b, 0, 0, 0)),
            pl.BlockSpec((heads, depth, depth), lambda b: (0, 0, 0)),
        ],
        out_specs=pl.BlockSpec((step, heads, depth), lambda b: (b, 0, 0)),
        out_shape=jax.ShapeDtypeStruct((tokens, heads, depth), BF16),
        compiler_params=params(12),
        name="query_out",
    )(g, qi, local, far)


def key_value_kernel(heads, factor, k_ref, v_ref, ki_ref, vi_ref, local_ref, far_ref, ko_ref, vo_ref):
    depth = far_ref.shape[1]
    for j in range(ki_ref.shape[0] // BLOCK):
        rows = slice(j * BLOCK, (j + 1) * BLOCK)
        keys, values = [], []
        for h in range(heads):
            lanes = slice(h * depth, (h + 1) * depth)
            state = (far_ref[h].astype(F32) + local_ref[j, h]).astype(BF16)
            keys.append(factor * (ki_ref[rows, lanes] + dot(v_ref[h, rows, :], state, 1, 1)))
            values.append(factor * (vi_ref[rows, lanes] + dot(k_ref[h, rows, :], state, 1, 0)))
        ko_ref[rows] = jnp.concatenate(keys, 1).astype(BF16).reshape(BLOCK, heads, depth)
        vo_ref[rows] = jnp.concatenate(values, 1).astype(BF16).reshape(BLOCK, heads, depth)


def key_value_out(k, v, ki, vi, local, far, factor):
    tokens, rows = ki.shape
    heads, depth, _ = far.shape
    split = pl.BlockSpec((heads, STEP, depth), lambda b: (0, b, 0))
    step = STEP
    wide = pl.BlockSpec((step, rows), lambda b: (b, 0))
    out = pl.BlockSpec((step, heads, depth), lambda b: (b, 0, 0))
    return pl.pallas_call(
        lambda *refs: key_value_kernel(heads, factor, *refs),
        grid=(tokens // step,),
        in_specs=[
            split,
            split,
            wide,
            wide,
            pl.BlockSpec((step // BLOCK, heads, depth, depth), lambda b: (b, 0, 0, 0)),
            pl.BlockSpec((heads, depth, depth), lambda b: (0, 0, 0)),
        ],
        out_specs=[out, out],
        out_shape=[jax.ShapeDtypeStruct((tokens, heads, depth), BF16)] * 2,
        compiler_params=params(18),
        name="key_value_out",
    )(k, v, ki, vi, local, far)


def body(queries, key_rows, value_rows, out_grad, out_weight):
    tokens, heads, depth = queries.shape
    shards = lax.axis_size("seq")
    columns = lax.axis_size("head")
    chips = columns // 2
    factor = 1.0 / math.sqrt(depth * tokens * shards)

    def along(shift):
        return [(2 * x + c, 2 * ((x + shift) % chips) + c) for x in range(chips) for c in range(2)]

    def send(array, pairs):
        return lax.ppermute(array, "head", pairs)

    swap = [(i, i ^ 1) for i in range(columns)]
    right, left = along(1), along(-1)
    half = tokens // 2

    me = lax.axis_index("head")
    chip, core = me // 2, me % 2

    def column(shift, other):
        return 2 * ((chip + shift) % chips) + (1 - core if other else core)

    w = out_weight.reshape(heads * depth, -1)

    def columns_of(*shifts):
        return jnp.stack([column(s, other) for s in shifts for other in (False, True)]).astype(jnp.int32)

    own_columns, near_columns, far_columns, out_grad = lax.optimization_barrier(
        (columns_of(0), columns_of(-1, 1), columns_of(2), out_grad)
    )
    from_left = send(out_grad, right)
    from_right = send(out_grad, left)

    q = queries.transpose(1, 0, 2)
    k = key_rows.transpose(1, 0, 2)
    v = value_rows.transpose(1, 0, 2)

    kv_local, kv_total = kv_states(k, v)
    kv_total, q, k, v = lax.optimization_barrier((kv_total, q, k, v))
    rows = heads * depth // shards
    kv_pieces = lax.all_to_all(kv_total.reshape(shards, rows, depth), "seq", 0, 0, tiled=True)
    earlier = jnp.tril(jnp.ones((shards, shards), BF16), -1)
    later = jnp.triu(jnp.ones((shards, shards), BF16), 1)

    def scan(mask, pieces):
        sums = dot(mask, pieces.reshape(shards, rows * depth), 1, 0)
        return sums.astype(BF16).reshape(shards, rows, depth)

    kv_sums = scan(earlier, kv_pieces)
    from_left, from_right, out_grad, kv_sums, q, k, v = lax.optimization_barrier(
        (from_left, from_right, out_grad, kv_sums, q, k, v)
    )
    far_top = send(from_left[:half], right)
    far_bottom = send(from_right[half:], left)
    from_left_twin = send(from_left, swap)
    from_right_twin = send(from_right, swap)
    twin = send(out_grad, swap)
    acc = attn_add(None, [out_grad, twin], own_columns, w, "attn_own")
    acc = attn_add(
        acc,
        [from_left, from_left_twin, from_right, from_right_twin],
        near_columns,
        w,
        "attn_near",
    )
    far_top, far_bottom, acc = lax.optimization_barrier((far_top, far_bottom, acc))
    far_top_twin = send(far_top, swap)
    far_bottom_twin = send(far_bottom, swap)
    far = jnp.concatenate([far_top, far_bottom], 0)
    far_twin = jnp.concatenate([far_top_twin, far_bottom_twin], 0)
    grad, qg_local, qg_total = attn_last(far, far_twin, far_columns, w, acc, q)

    both = jnp.concatenate([qg_total.reshape(shards, rows, depth), kv_sums], 1)
    both = lax.all_to_all(both, "seq", 0, 0, tiled=True)
    qg_sums = scan(later, both[:, :rows])
    before = both[:, rows:].reshape(heads, depth, depth)
    after = lax.all_to_all(qg_sums, "seq", 0, 0, tiled=True).reshape(heads, depth, depth)

    qi, ki, vi = inner(q, k, v, grad)
    ki, vi, qg_local = in_hbm(ki), in_hbm(vi), in_hbm(qg_local)
    query_grad = query_out(grad, qi, kv_local, before, factor)
    key_grad, value_grad = key_value_out(k, v, ki, vi, qg_local, after, factor)
    return query_grad, key_grad, value_grad


def solution(mesh):
    placed = (
        P("seq", "head", None),
        P("seq", "head", None),
        P("seq", "head", None),
        P("seq", "head"),
        P("head", None, None),
    )
    return jax.shard_map(
        body,
        mesh=mesh,
        in_specs=placed,
        out_specs=(P("seq", "head", None), P("seq", "head", None), P("seq", "head", None)),
        check_vma=False,
    )
```

time: 127 us -> 96.4 us (0.76); the launches traced: 127 us -> 94.7 us
  waiting for transfers between devices: 43 us -> 14.8 us
  local copies, waits for them, and re-layouts: 15 us -> 7.93 us
  blocking collectives: 15.6 us -> 20.9 us
  other arithmetic: 2.9 us -> 0.31 us
    ppermute x9, waiting for transfers between devices: 35.9 us -> 4.55 us  [send(): return lax.ppermute(array, 'head', pairs)]
    unnamed x28 -> x19, local copies, waits for them, and re-layouts: 13.5 us -> 5.48 us
    all_to_all x1, blocking collectives: 15.6 us -> 20.9 us  [body(): both = lax.all_to_all(both, 'seq', 0, 0, tiled=True)]
    all_to_all x1, waiting for transfers between devices: 7.1 us -> 9.26 us  [body(): lax.all_to_all(kv_total.reshape(shards, rows, depth), 'seq', 0, 0, tiled=...]
    pallas_call x1, Pallas kernels: 3.23 us -> 1.45 us  [query_out(): pl.pallas_call(lambda *refs: query_kernel(heads, factor, *refs), grid=(to...]
    concatenate x1, other arithmetic: 1.42 us -> 0.07 us  [body(): far = jnp.concatenate([far_top, far_bottom], 0)]
    concatenate x1, other arithmetic: 1.39 us -> 0.07 us  [body(): far_twin = jnp.concatenate([far_top_twin, far_bottom_twin], 0)]
    pallas_call x1 -> x2, Pallas kernels: 6.24 us -> 7.53 us  [attn_add(): pl.pallas_call(lambda i, *refs: attn_add_kernel(count, *(refs if first el...]
  transfers between devices with their start and end apart: 11 -> 11, of which waited for: 4 -> 5; matrix products, arithmetic and copies ran while one was open for 7% -> 4% of each run, Pallas kernels for 8% -> 18%
where the time goes in v2:
time: 96.4 us; the launch traced here: 94.7 us
  starting transfers between devices  25.1 us (26%)
  Pallas kernels  24.3 us (25%)
  blocking collectives  20.9 us (22%)
  waiting for transfers between devices  14.8 us (15%)
  local copies, waits for them, and re-layouts  7.93 us (8%)
    all_to_all x1, blocking collectives, body(): both = lax.all_to_all(both, 'seq', 0, 0, tiled=True)  20.9 us
    all_to_all x1, starting transfers between devices, body(): lax.all_to_all(kv_total.reshape(shards, rows, depth), 'seq', 0, 0, tiled=...  11.7 us
    all_to_all x1, waiting for transfers between devices, body(): lax.all_to_all(kv_total.reshape(shards, rows, depth), 'seq', 0, 0, tiled=...  9.26 us
    ppermute x9, starting transfers between devices, send(): return lax.ppermute(array, 'head', pairs)  7.77 us
    pallas_call x2, Pallas kernels, attn_add(): pl.pallas_call(lambda i, *refs: attn_add_kernel(count, *(refs if first el...  7.53 us
    all_to_all x1, starting transfers between devices, body(): lax.all_to_all(qg_sums, 'seq', 0, 0, tiled=True)  5.62 us
    pallas_call x1, Pallas kernels, inner(): pl.pallas_call(lambda *refs: inner_kernel(heads, *refs), grid=(tokens //...  5.51 us
    unnamed x19, local copies, waits for them, and re-layouts  5.48 us
  transfers between devices with their start and end apart: 11, of which 5 were waited for; matrix products, arithmetic and copies ran while one was open for 4% of the time, Pallas kernels for 18%

profile of v2, /device:TPU:8, one launch (start us, length us, event | category | flops | bytes accessed | tf_op | source)
XLA Modules:
  0.0 94.7 jit_solution(3441004762271596529)
XLA Ops:
  0.7 0.0 copy-start.6
  0.7 0.0 copy-start.7
  0.7 0.1 pad_add_fusion
  0.8 0.1 pad_add_fusion.1.i
  0.9 1.5 %collective-permute-start = (bf16[1024,512]{1,0:T(8,128)(2,1)}, bf16[1024,512]{1,0:T(8,128)(2,1)}, u32[]{:S(2)}, u32[]{:S(2)}) collective-permute-start(bf16[1024,512]{1,0:T(8,128)(2,1)} %refs_0_), channel_id=1, source_target_pairs={{0,2},{1,3},{2,4},{3,5},{4,6},{5,7},{6,0},{7,1},{8,10},{9,11},{10,... | collective-permute-start | bytes 3145736 | tf_op jit(solution)/shard_map/ppermute | solution.py:270
  2.4 1.7 %collective-permute-start.1 = (bf16[1024,512]{1,0:T(8,128)(2,1)}, bf16[1024,512]{1,0:T(8,128)(2,1)}, u32[]{:S(2)}, u32[]{:S(2)}) collective-permute-start(bf16[1024,512]{1,0:T(8,128)(2,1)} %refs_0_), channel_id=1, source_target_pairs={{0,6},{1,7},{2,0},{3,1},{4,2},{5,3},{6,4},{7,5},{8,14},{9,15},{10,... | collective-permute-start | bytes 3145736 | tf_op jit(solution)/shard_map/ppermute | solution.py:270
  4.1 1.4 %copy.26 = bf16[1024,4,128]{2,0,1:T(8,128)(2,1)S(1)} copy(bf16[1024,4,128]{2,1,0:T(4,128)(2,1)} %param.5) | data formatting | bytes 2097152 | tf_op args[0]
  5.5 0.0 copy-done.6
  5.5 0.0 copy-done.7
  5.5 0.3 copy_bitcast_fusion.1
  5.8 2.3 %kv_states.1 = (f32[4,4,128,128]{3,2,1,0:T(8,128)}, bf16[4,128,128]{2,1,0:T(8,128)(2,1)}) custom-call(bf16[4,1024,128]{2,1,0:T(8,128)(2,1)S(1)} %get-tuple-element.48.refs_0_.refs_1_, bf16[4,1024,128]{2,1,0:T(8,128)(2,1)S(1)} %get-tuple-element.49.refs_1_.refs_2_), custom_call_target="tpu_custom_call" | custom-call | tf_op jit(solution)/shard_map/kv_states/pallas_call | solution.py:49
  8.1 11.7 %all-to-all-start = ((bf16[32,16,128]{2,1,0:T(8,128)(2,1)}), bf16[32,16,128]{2,1,0:T(8,128)(2,1)S(1)}, u32[]{:S(2)}, u32[]{:S(2)}) async-start(bf16[32,16,128]{2,1,0:T(8,128)(2,1)} %bitcast.11), calls=%async_computation | async-start | bytes 262144 | tf_op jit(solution)/shard_map/all_to_all | solution.py:300
  19.8 9.3 %all-to-all-done = bf16[32,16,128]{2,1,0:T(8,128)(2,1)S(1)} async-done(((bf16[32,16,128]{2,1,0:T(8,128)(2,1)}), bf16[32,16,128]{2,1,0:T(8,128)(2,1)S(1)}, u32[]{:S(2)}, u32[]{:S(2)}) %all-to-all-start) | async-done | bytes 131104 | tf_op jit(solution)/shard_map/all_to_all | solution.py:300
  29.0 0.0 copy-start.4
  29.0 0.2 fusion
  29.3 0.0 collective-permute-done.refs_1_
  29.3 0.0 collective-permute-done.1.refs_3_
  29.3 0.1 collective-permute-start.4
  29.4 0.5 collective-permute-start.5
  29.9 0.1 collective-permute-start.6
  30.0 1.1 %slice.12 = bf16[512,512]{1,0:T(8,128)(2,1)S(1)} slice(bf16[1024,512]{1,0:T(8,128)(2,1)} %collective-permute-done.refs_1_), slice={[0:512], [0:512]} | slice | bytes 1048576 | tf_op jit(solution)/shard_map/slice | solution.py:312
  31.1 1.1 %slice.13 = bf16[512,512]{1,0:T(8,128)(2,1)S(1)} slice(bf16[1024,512]{1,0:T(8,128)(2,1)} %collective-permute-done.1.refs_3_), slice={[512:1024], [0:512]} | slice | bytes 1048576 | tf_op jit(solution)/shard_map/slice | solution.py:313
  32.2 0.4 collective-permute-start.2
  32.5 3.0 %collective-permute-start.3 = (bf16[512,512]{1,0:T(8,128)(2,1)S(1)}, bf16[512,512]{1,0:T(8,128)(2,1)S(1)}, u32[]{:S(2)}, u32[]{:S(2)}) collective-permute-start(bf16[512,512]{1,0:T(8,128)(2,1)S(1)} %slice.13), channel_id=1, source_target_pairs={{0,6},{1,7},{2,0},{3,1},{4,2},{5,3},{6,4},{7,5},{8,14},{9,15},{10,... | collective-permute-start | bytes 1572872 | tf_op jit(solution)/shard_map/ppermute | solution.py:270
  35.5 0.0 collective-permute-done.4.refs_1_
  35.5 0.0 copy-done.4
  35.5 0.0 copy-start
  35.5 2.2 %copy-done = bf16[4,128,4096]{2,1,0:T(8,128)(2,1)S(1)} copy-done((bf16[4,128,4096]{2,1,0:T(8,128)(2,1)S(1)}, bf16[4,128,4096]{2,1,0:T(8,128)(2,1)}, u32[]{:S(2)}) %copy-start) | copy-done | bytes 4194328
  37.7 0.0 copy-start.1
  37.7 2.6 %attn_own.1.refs_0_ = f32[1024,512]{1,0:T(8,128)S(1)} custom-call(s32[2]{0:T(128)S(1)} %get-tuple-element.41.i, bf16[1024,512]{1,0:T(8,128)(2,1)S(1)} %copy-done.4, bf16[1024,512]{1,0:T(8,128)(2,1)S(1)} %collective-permute-done.4.refs_1_, bf16[512,4096]{1,0:T(8,128)(2,1)S(1)} %bitcast.34, bf16[512,4096]{1,0:T(8,128)(2,1)S(1)} %bitcast.35), custom_call_target="tpu_custom_call" | custom-call | flops 1073741824 | bytes 2097152 | tf_op jit(solution)/shard_map/attn_own/pallas_call | solution.py:83
  40.3 0.0 collective-permute-done.5.refs_2_
  40.3 0.0 collective-permute-done.6.refs_4_
  40.3 0.0 copy-done.1
  40.3 5.0 %attn_near.1.refs_5_ = f32[1024,512]{1,0:T(8,128)S(1)} custom-call(s32[4]{0:T(128)S(1)} %pad_add_fusion.1.i, f32[1024,512]{1,0:T(8,128)S(1)} %attn_own.1.refs_0_, bf16[1024,512]{1,0:T(8,128)(2,1)} %collective-permute-done.refs_1_, bf16[1024,512]{1,0:T(8,128)(2,1)S(1)} %collective-permute-done.5.refs_2_, bf16[1024,512]{1,0:T(8,128)(2,1)} %collective-permute-done.1.refs_3_, ...), custom_call_target="tpu_custom_call" | custom-call | flops 2147483648 | bytes 2097152 | tf_op jit(solution)/shard_map/attn_near/pallas_call | solution.py:83
  45.3 2.5 %collective-permute-done.2 = bf16[512,512]{1,0:T(8,128)(2,1)S(1)} collective-permute-done((bf16[512,512]{1,0:T(8,128)(2,1)S(1)}, bf16[512,512]{1,0:T(8,128)(2,1)S(1)}, u32[]{:S(2)}, u32[]{:S(2)}) %collective-permute-start.2) | collective-permute-done | bytes 524320 | tf_op jit(solution)/shard_map/ppermute | solution.py:270
  47.7 0.0 collective-permute-done.3
  47.7 0.0 collective-permute-start.8
  47.7 0.5 collective-permute-start.7
  48.3 0.1 pad_maximum_fusion.refs_1_
  48.3 1.3 %collective-permute-done.8 = bf16[512,512]{1,0:T(8,128)(2,1)S(1)} collective-permute-done((bf16[512,512]{1,0:T(8,128)(2,1)S(1)}, bf16[512,512]{1,0:T(8,128)(2,1)S(1)}, u32[]{:S(2)}, u32[]{:S(2)}) %collective-permute-start.8) | collective-permute-done | bytes 524320 | tf_op jit(solution)/shard_map/ppermute | solution.py:270
  49.7 0.7 collective-permute-done.7
  50.4 0.1 pad_maximum_fusion.1.refs_2_
  50.5 3.6 %attn_last.1 = (bf16[1024,512]{1,0:T(8,128)(2,1)}, f32[4,4,128,128]{3,2,1,0:T(8,128)}, bf16[4,128,128]{2,1,0:T(8,128)(2,1)S(1)}) custom-call(s32[2]{0:T(128)S(1)} %get-tuple-element.31.refs_0_, bf16[1024,512]{1,0:T(8,128)(2,1)S(1)} %pad_maximum_fusion.refs_1_, bf16[1024,512]{1,0:T(8,128)(2,1)S(1)} %pad_maximum_fusion.1.refs_2_, ...), custom_call_target="tpu_custom_call" | custom-call | flops 1342177280 | bytes 2097152 | tf_op jit(solution)/shard_map/attn_last/pallas_call | solution.py:125
  54.1 20.9 %all_to_all.15 = bf16[32,32,128]{2,1,0:T(8,128)(2,1)S(1)} all-to-all(bf16[32,32,128]{2,1,0:T(8,128)(2,1)S(1)} %pad_maximum_fusion.2), channel_id=1, replica_groups=mesh['seq'=32,'head'=8] {'seq'}, dimensions={0} | all-to-all | bytes 524288 | tf_op jit(solution)/shard_map/all_to_all | solution.py:333
  75.1 0.2 fusion.1
  75.2 0.7 copy.14
  75.9 5.6 %all-to-all-start.2 = ((bf16[32,16,128]{2,1,0:T(8,128)(2,1)}), bf16[32,16,128]{2,1,0:T(8,128)(2,1)S(1)}, u32[]{:S(2)}, u32[]{:S(2)}) async-start(bf16[32,16,128]{2,1,0:T(8,128)(2,1)} %bitcast.23), calls=%async_computation.2 | async-start | bytes 262144 | tf_op jit(solution)/shard_map/all_to_all | solution.py:336
  81.5 0.0 copy-start.2
  81.5 1.2 %copy-done.2 = bf16[1024,512]{1,0:T(8,128)(2,1)S(1)} copy-done((bf16[1024,512]{1,0:T(8,128)(2,1)S(1)}, bf16[1024,512]{1,0:T(8,128)(2,1)}, u32[]{:S(2)}) %copy-start.2) | copy-done | bytes 1048600
  82.8 0.0 copy-start.3
  82.8 0.0 copy-start.5
  82.8 5.5 %inner.1 = (f32[1024,512]{1,0:T(8,128)S(1)}, f32[1024,512]{1,0:T(8,128)}, f32[1024,512]{1,0:T(8,128)}) custom-call(bf16[4,1024,128]{2,1,0:T(8,128)(2,1)S(1)} %bitcast.43, bf16[4,1024,128]{2,1,0:T(8,128)(2,1)S(1)} %get-tuple-element.48.refs_0_.refs_1_, bf16[4,1024,128]{2,1,0:T(8,128)(2,1)S(1)} %get-tuple-element.49.refs_1_.refs_2_, ...), custom_call_target="tpu_custom_call" | custom-call | tf_op jit(solution)/shard_map/inner/pallas_call | solution.py:176
  88.3 0.0 copy-done.3
  88.3 0.0 copy-done.5
  88.3 1.4 %query_out.1 = bf16[1024,4,128]{2,1,0:T(4,128)(2,1)} custom-call(bf16[1024,512]{1,0:T(8,128)(2,1)S(1)} %copy-done.3, f32[1024,512]{1,0:T(8,128)S(1)} %get-tuple-element.50.refs_1_, f32[4,4,128,128]{3,2,1,0:T(8,128)S(1)} %copy-done.5, bf16[4,128,128]{2,1,0:T(8,128)(2,1)S(1)} %bitcast.45), custom_call_target="tpu_custom_call" | custom-call | tf_op jit(solution)/shard_map/query_out/pallas_call | solution.py:204
  89.7 1.0 %all-to-all-done.2 = bf16[32,16,128]{2,1,0:T(8,128)(2,1)S(1)} async-done(((bf16[32,16,128]{2,1,0:T(8,128)(2,1)}), bf16[32,16,128]{2,1,0:T(8,128)(2,1)S(1)}, u32[]{:S(2)}, u32[]{:S(2)}) %all-to-all-start.2) | async-done | bytes 131104 | tf_op jit(solution)/shard_map/all_to_all | solution.py:336
  90.8 4.0 %key_value_out.1 = (bf16[1024,4,128]{2,1,0:T(4,128)(2,1)}, bf16[1024,4,128]{2,1,0:T(4,128)(2,1)}) custom-call(bf16[4,1024,128]{2,1,0:T(8,128)(2,1)S(1)} %get-tuple-element.48.refs_0_.refs_1_, bf16[4,1024,128]{2,1,0:T(8,128)(2,1)S(1)} %get-tuple-element.49.refs_1_.refs_2_, f32[1024,512]{1,0:T(8,128)} %get-tuple-element.54.refs_2_, ...), custom_call_target="tpu_custom_call" | custom-call | tf_op jit(solution)/shard_map/key_value_out/pallas_call | solution.py:241
  (4 shorter events, 0.1 us)
Async XLA Ops:
  0.7 4.8 %copy-start.6 = (bf16[1024,4,128]{2,1,0:T(4,128)(2,1)S(1)}, bf16[1024,4,128]{2,1,0:T(4,128)(2,1)}, u32[]{:S(2)}) copy-start(bf16[1024,4,128]{2,1,0:T(4,128)(2,1)} %param.7) | copy-start | bytes 3145732
  0.7 4.8 %copy-start.7 = (bf16[1024,4,128]{2,1,0:T(4,128)(2,1)S(1)}, bf16[1024,4,128]{2,1,0:T(4,128)(2,1)}, u32[]{:S(2)}) copy-start(bf16[1024,4,128]{2,1,0:T(4,128)(2,1)} %param.6) | copy-start | bytes 3145732
  0.9 28.4 %collective-permute-start = (bf16[1024,512]{1,0:T(8,128)(2,1)}, bf16[1024,512]{1,0:T(8,128)(2,1)}, u32[]{:S(2)}, u32[]{:S(2)}) collective-permute-start(bf16[1024,512]{1,0:T(8,128)(2,1)} %refs_0_), channel_id=1, source_target_pairs={{0,2},{1,3},{2,4},{3,5},{4,6},{5,7},{6,0},{7,1},{8,10},{9,11},{10,... | collective-permute-start | bytes 3145736 | tf_op jit(solution)/shard_map/ppermute | solution.py:270
  2.4 26.9 %collective-permute-start.1 = (bf16[1024,512]{1,0:T(8,128)(2,1)}, bf16[1024,512]{1,0:T(8,128)(2,1)}, u32[]{:S(2)}, u32[]{:S(2)}) collective-permute-start(bf16[1024,512]{1,0:T(8,128)(2,1)} %refs_0_), channel_id=1, source_target_pairs={{0,6},{1,7},{2,0},{3,1},{4,2},{5,3},{6,4},{7,5},{8,14},{9,15},{10,... | collective-permute-start | bytes 3145736 | tf_op jit(solution)/shard_map/ppermute | solution.py:270
  8.1 21.0 %all-to-all-start = ((bf16[32,16,128]{2,1,0:T(8,128)(2,1)}), bf16[32,16,128]{2,1,0:T(8,128)(2,1)S(1)}, u32[]{:S(2)}, u32[]{:S(2)}) async-start(bf16[32,16,128]{2,1,0:T(8,128)(2,1)} %bitcast.11), calls=%async_computation | async-start | bytes 262144 | tf_op jit(solution)/shard_map/all_to_all | solution.py:300
  29.0 6.5 %copy-start.4 = (bf16[1024,512]{1,0:T(8,128)(2,1)S(1)}, bf16[1024,512]{1,0:T(8,128)(2,1)}, u32[]{:S(2)}) copy-start(bf16[1024,512]{1,0:T(8,128)(2,1)} %refs_0_) | copy-start | bytes 3145732
  29.3 6.2 %collective-permute-start.4 = (bf16[1024,512]{1,0:T(8,128)(2,1)}, bf16[1024,512]{1,0:T(8,128)(2,1)S(1)}, u32[]{:S(2)}, u32[]{:S(2)}) collective-permute-start(bf16[1024,512]{1,0:T(8,128)(2,1)} %refs_0_), channel_id=1, source_target_pairs={{0,1},{1,0},{2,3},{3,2},{4,5},{5,4},{6,7},{7,6},{8,9},{9,8},{10,11... | collective-permute-start | bytes 3145736 | tf_op jit(solution)/shard_map/ppermute | solution.py:270
  29.4 10.8 %collective-permute-start.5 = (bf16[1024,512]{1,0:T(8,128)(2,1)}, bf16[1024,512]{1,0:T(8,128)(2,1)S(1)}, u32[]{:S(2)}, u32[]{:S(2)}) collective-permute-start(bf16[1024,512]{1,0:T(8,128)(2,1)} %collective-permute-done.refs_1_), channel_id=1, source_target_pairs={{0,1},{1,0},{2,3},{3,2},{4,5},{5,4},{6,7},{7,6},{8,9},{9,8},{10,11... | collective-permute-start | bytes 3145736 | tf_op jit(solution)/shard_map/ppermute | solution.py:270
  29.9 10.4 %collective-permute-start.6 = (bf16[1024,512]{1,0:T(8,128)(2,1)}, bf16[1024,512]{1,0:T(8,128)(2,1)S(1)}, u32[]{:S(2)}, u32[]{:S(2)}) collective-permute-start(bf16[1024,512]{1,0:T(8,128)(2,1)} %collective-permute-done.1.refs_3_), channel_id=1, source_target_pairs={{0,1},{1,0},{2,3},{3,2},{4,5},{5,4},{6,7},{7,6},{8,9},{9,8},{10,11... | collective-permute-start | bytes 3145736 | tf_op jit(solution)/shard_map/ppermute | solution.py:270
  32.2 15.5 %collective-permute-start.2 = (bf16[512,512]{1,0:T(8,128)(2,1)S(1)}, bf16[512,512]{1,0:T(8,128)(2,1)S(1)}, u32[]{:S(2)}, u32[]{:S(2)}) collective-permute-start(bf16[512,512]{1,0:T(8,128)(2,1)S(1)} %slice.12), channel_id=1, source_target_pairs={{0,2},{1,3},{2,4},{3,5},{4,6},{5,7},{6,0},{7,1},{8,10},{9,11},{10,... | collective-permute-start | bytes 1572872 | tf_op jit(solution)/shard_map/ppermute | solution.py:270
  32.5 15.2 %collective-permute-start.3 = (bf16[512,512]{1,0:T(8,128)(2,1)S(1)}, bf16[512,512]{1,0:T(8,128)(2,1)S(1)}, u32[]{:S(2)}, u32[]{:S(2)}) collective-permute-start(bf16[512,512]{1,0:T(8,128)(2,1)S(1)} %slice.13), channel_id=1, source_target_pairs={{0,6},{1,7},{2,0},{3,1},{4,2},{5,3},{6,4},{7,5},{8,14},{9,15},{10,... | collective-permute-start | bytes 1572872 | tf_op jit(solution)/shard_map/ppermute | solution.py:270
  35.5 2.2 %copy-start = (bf16[4,128,4096]{2,1,0:T(8,128)(2,1)S(1)}, bf16[4,128,4096]{2,1,0:T(8,128)(2,1)}, u32[]{:S(2)}) copy-start(bf16[4,128,4096]{2,1,0:T(8,128)(2,1)} %param.9) | copy-start | bytes 12582916
  37.7 2.6 %copy-start.1 = (bf16[4,128,4096]{2,1,0:T(8,128)(2,1)S(1)}, bf16[4,128,4096]{2,1,0:T(8,128)(2,1)}, u32[]{:S(2)}) copy-start(bf16[4,128,4096]{2,1,0:T(8,128)(2,1)} %param.9) | copy-start | bytes 12582916
  47.7 1.9 %collective-permute-start.8 = (bf16[512,512]{1,0:T(8,128)(2,1)S(1)}, bf16[512,512]{1,0:T(8,128)(2,1)S(1)}, u32[]{:S(2)}, u32[]{:S(2)}) collective-permute-start(bf16[512,512]{1,0:T(8,128)(2,1)S(1)} %collective-permute-done.3), channel_id=1, source_target_pairs={{0,1},{1,0},{2,3},{3,2},{4,5},{5,4},{6,7},{7,6},{8,9},{9,8},{10,11... | collective-permute-start | bytes 1572872 | tf_op jit(solution)/shard_map/ppermute | solution.py:270
  47.7 2.7 %collective-permute-start.7 = (bf16[512,512]{1,0:T(8,128)(2,1)S(1)}, bf16[512,512]{1,0:T(8,128)(2,1)S(1)}, u32[]{:S(2)}, u32[]{:S(2)}) collective-permute-start(bf16[512,512]{1,0:T(8,128)(2,1)S(1)} %collective-permute-done.2), channel_id=1, source_target_pairs={{0,1},{1,0},{2,3},{3,2},{4,5},{5,4},{6,7},{7,6},{8,9},{9,8},{10,11... | collective-permute-start | bytes 1572872 | tf_op jit(solution)/shard_map/ppermute | solution.py:270
  75.9 14.9 %all-to-all-start.2 = ((bf16[32,16,128]{2,1,0:T(8,128)(2,1)}), bf16[32,16,128]{2,1,0:T(8,128)(2,1)S(1)}, u32[]{:S(2)}, u32[]{:S(2)}) async-start(bf16[32,16,128]{2,1,0:T(8,128)(2,1)} %bitcast.23), calls=%async_computation.2 | async-start | bytes 262144 | tf_op jit(solution)/shard_map/all_to_all | solution.py:336
  81.5 1.2 %copy-start.2 = (bf16[1024,512]{1,0:T(8,128)(2,1)S(1)}, bf16[1024,512]{1,0:T(8,128)(2,1)}, u32[]{:S(2)}) copy-start(bf16[1024,512]{1,0:T(8,128)(2,1)} %get-tuple-element.47.refs_3_.refs_0_) | copy-start | bytes 3145732
  82.8 5.5 %copy-start.3 = (bf16[1024,512]{1,0:T(8,128)(2,1)S(1)}, bf16[1024,512]{1,0:T(8,128)(2,1)}, u32[]{:S(2)}) copy-start(bf16[1024,512]{1,0:T(8,128)(2,1)} %get-tuple-element.47.refs_3_.refs_0_) | copy-start | bytes 3145732
  82.8 5.5 %copy-start.5 = (f32[4,4,128,128]{3,2,1,0:T(8,128)S(1)}, f32[4,4,128,128]{3,2,1,0:T(8,128)}, u32[]{:S(2)}) copy-start(f32[4,4,128,128]{3,2,1,0:T(8,128)} %get-tuple-element.51.refs_2_) | copy-start | bytes 3145732

commit v3 on v2

--- a/solution.py
+++ b/solution.py
@@ -95,25 +95,24 @@
     )(index, *first, *pieces, *([w] * count))
 
 
-def attn_last_kernel(heads, i_ref, a_ref, b_ref, wa_ref, wb_ref, acc_ref, q_ref, g_ref, after_ref, total_ref, run):
+def attn_last_kernel(heads, i_ref, a_ref, wa_ref, acc_ref, q_ref, g_ref, after_ref, total_ref, run):
     depth = q_ref.shape[2]
 
     @pl.when(pl.program_id(0) == 0)
     def _():
         run[...] = jnp.zeros_like(run)
 
-    total = acc_ref[...] + dot(a_ref[...], wa_ref[...], 1, 1)
-    total = (total + dot(b_ref[...], wb_ref[...], 1, 1)).astype(BF16)
+    total = (acc_ref[...] + dot(a_ref[...], wa_ref[...], 1, 1)).astype(BF16)
     g_ref[...] = total
     for j in reversed(range(a_ref.shape[0] // BLOCK)):
         part = slice(j * BLOCK, (j + 1) * BLOCK)
-        after_ref[j] = run[...]
+        after_ref[j] = run[...].astype(BF16)
         for h in range(heads):
             run[h] += dot(q_ref[h, part, :], total[part, h * depth : (h + 1) * depth], 0, 0)
     total_ref[...] = run[...].astype(BF16)
 
 
-def attn_last(a, b, index, w, acc, q):
+def attn_last(a, index, w, acc, q):
     tokens, width = a.shape
     rows = w.shape[0]
     heads, _, depth = q.shape
@@ -129,9 +128,7 @@
             grid=(steps,),
             in_specs=[
                 piece,
-                piece,
                 pl.BlockSpec((rows, width), lambda s, i: (0, i[0])),
-                pl.BlockSpec((rows, width), lambda s, i: (0, i[1])),
                 wide,
                 pl.BlockSpec((heads, STEP, depth), lambda s, i: (0, last - s, 0)),
             ],
@@ -144,16 +141,16 @@
         ),
         out_shape=[
             pltpu.HBM((tokens, rows), BF16),
-            pltpu.HBM((tokens // BLOCK, heads, depth, depth), F32),
+            pltpu.HBM((tokens // BLOCK, heads, depth, depth), BF16),
             jax.ShapeDtypeStruct((heads, depth, depth), BF16),
         ],
         compiler_params=params(18),
         cost_estimate=cost(5 * tokens * rows * width, 4 * tokens * rows),
         name="attn_last",
-    )(index, a, b, w, w, acc, q)
-
-
-def inner_kernel(heads, q_ref, k_ref, v_ref, g_ref, qi_ref, ki_ref, vi_ref):
+    )(index, a, w, acc, q)
+
+
+def inner_kernel(heads, q_ref, k_ref, v_ref, g_ref, local_ref, qi_ref, ki_ref, vi_ref):
     depth = q_ref.shape[2]
     row = lax.broadcasted_iota(jnp.int32, (BLOCK, BLOCK), 0)
     col = lax.broadcasted_iota(jnp.int32, (BLOCK, BLOCK), 1)
@@ -164,11 +161,12 @@
         grad_t = jnp.where(row <= col, dot(v, g, 1, 1), 0.0).astype(BF16)
         score_t = jnp.where(row <= col, dot(k, q, 1, 1), 0.0).astype(BF16)
         qi_ref[:, lanes] = dot(grad, k, 1, 0)
-        ki_ref[:, lanes] = dot(grad_t, q, 1, 0)
-        vi_ref[:, lanes] = dot(score_t, g, 1, 0)
-
-
-def inner(q, k, v, g):
+        local = local_ref[0, h]
+        ki_ref[:, lanes] = (dot(grad_t, q, 1, 0) + dot(v, local, 1, 1)).astype(BF16)
+        vi_ref[:, lanes] = (dot(score_t, g, 1, 0) + dot(k, local, 1, 0)).astype(BF16)
+
+
+def inner(q, k, v, g, local):
     heads, tokens, depth = q.shape
     rows = heads * depth
     split = pl.BlockSpec((heads, BLOCK, depth), lambda b: (0, b, 0))
@@ -176,12 +174,18 @@
     return pl.pallas_call(
         lambda *refs: inner_kernel(heads, *refs),
         grid=(tokens // BLOCK,),
-        in_specs=[split, split, split, wide],
+        in_specs=[
+            split,
+            split,
+            split,
+            wide,
+            pl.BlockSpec((1, heads, depth, depth), lambda b: (b, 0, 0, 0)),
+        ],
         out_specs=[wide] * 3,
-        out_shape=[jax.ShapeDtypeStruct((tokens, rows), F32)] + [pltpu.HBM((tokens, rows), F32)] * 2,
+        out_shape=[jax.ShapeDtypeStruct((tokens, rows), F32)] + [pltpu.HBM((tokens, rows), BF16)] * 2,
         compiler_params=params(10),
         name="inner",
-    )(q, k, v, g)
+    )(q, k, v, g, local)
 
 
 def query_kernel(heads, factor, g_ref, qi_ref, local_ref, far_ref, out_ref):
@@ -217,25 +221,22 @@
     )(g, qi, local, far)
 
 
-def key_value_kernel(heads, factor, k_ref, v_ref, ki_ref, vi_ref, local_ref, far_ref, ko_ref, vo_ref):
+def key_value_kernel(heads, factor, k_ref, v_ref, ki_ref, vi_ref, far_ref, ko_ref, vo_ref):
     depth = far_ref.shape[1]
-    for j in range(ki_ref.shape[0] // BLOCK):
-        rows = slice(j * BLOCK, (j + 1) * BLOCK)
-        keys, values = [], []
-        for h in range(heads):
-            lanes = slice(h * depth, (h + 1) * depth)
-            state = (far_ref[h].astype(F32) + local_ref[j, h]).astype(BF16)
-            keys.append(factor * (ki_ref[rows, lanes] + dot(v_ref[h, rows, :], state, 1, 1)))
-            values.append(factor * (vi_ref[rows, lanes] + dot(k_ref[h, rows, :], state, 1, 0)))
-        ko_ref[rows] = jnp.concatenate(keys, 1).astype(BF16).reshape(BLOCK, heads, depth)
-        vo_ref[rows] = jnp.concatenate(values, 1).astype(BF16).reshape(BLOCK, heads, depth)
-
-
-def key_value_out(k, v, ki, vi, local, far, factor):
+    keys, values = [], []
+    for h in range(heads):
+        lanes = slice(h * depth, (h + 1) * depth)
+        state = far_ref[h]
+        keys.append(factor * (ki_ref[:, lanes].astype(F32) + dot(v_ref[h], state, 1, 1)))
+        values.append(factor * (vi_ref[:, lanes].astype(F32) + dot(k_ref[h], state, 1, 0)))
+    ko_ref[...] = jnp.concatenate(keys, 1).astype(BF16).reshape(ko_ref.shape)
+    vo_ref[...] = jnp.concatenate(values, 1).astype(BF16).reshape(vo_ref.shape)
+
+
+def key_value_out(k, v, ki, vi, far, factor, step=STEP):
     tokens, rows = ki.shape
     heads, depth, _ = far.shape
-    split = pl.BlockSpec((heads, STEP, depth), lambda b: (0, b, 0))
-    step = STEP
+    split = pl.BlockSpec((heads, step, depth), lambda b: (0, b, 0))
     wide = pl.BlockSpec((step, rows), lambda b: (b, 0))
     out = pl.BlockSpec((step, heads, depth), lambda b: (b, 0, 0))
     return pl.pallas_call(
@@ -246,14 +247,13 @@
             split,
             wide,
             wide,
-            pl.BlockSpec((step // BLOCK, heads, depth, depth), lambda b: (b, 0, 0, 0)),
             pl.BlockSpec((heads, depth, depth), lambda b: (0, 0, 0)),
         ],
         out_specs=[out, out],
         out_shape=[jax.ShapeDtypeStruct((tokens, heads, depth), BF16)] * 2,
         compiler_params=params(18),
         name="key_value_out",
-    )(k, v, ki, vi, local, far)
+    )(k, v, ki, vi, far)
 
 
 def body(queries, key_rows, value_rows, out_grad, out_weight):
@@ -284,50 +284,55 @@
     def columns_of(*shifts):
         return jnp.stack([column(s, other) for s in shifts for other in (False, True)]).astype(jnp.int32)
 
-    own_columns, near_columns, far_columns, out_grad = lax.optimization_barrier(
-        (columns_of(0), columns_of(-1, 1), columns_of(2), out_grad)
+    near_columns, far_columns, out_grad = lax.optimization_barrier(
+        (columns_of(0, -1, 1), (columns_of(2)[:1], columns_of(2)[1:]), out_grad)
     )
     from_left = send(out_grad, right)
     from_right = send(out_grad, left)
-
-    q = queries.transpose(1, 0, 2)
+    twin = send(out_grad, swap)
+
     k = key_rows.transpose(1, 0, 2)
     v = value_rows.transpose(1, 0, 2)
 
     kv_local, kv_total = kv_states(k, v)
-    kv_total, q, k, v = lax.optimization_barrier((kv_total, q, k, v))
+    order = jnp.arange(shards)
+    later = (order[:, None] < order[None, :]).astype(BF16)
+    earlier = (order[:, None] > order[None, :]).astype(BF16)
+    kv_total, k, v, later, earlier, queries, twin = lax.optimization_barrier(
+        (kv_total, k, v, later, earlier, queries, twin)
+    )
     rows = heads * depth // shards
     kv_pieces = lax.all_to_all(kv_total.reshape(shards, rows, depth), "seq", 0, 0, tiled=True)
-    earlier = jnp.tril(jnp.ones((shards, shards), BF16), -1)
-    later = jnp.triu(jnp.ones((shards, shards), BF16), 1)
 
     def scan(mask, pieces):
         sums = dot(mask, pieces.reshape(shards, rows * depth), 1, 0)
         return sums.astype(BF16).reshape(shards, rows, depth)
 
     kv_sums = scan(earlier, kv_pieces)
-    from_left, from_right, out_grad, kv_sums, q, k, v = lax.optimization_barrier(
-        (from_left, from_right, out_grad, kv_sums, q, k, v)
-    )
-    far_top = send(from_left[:half], right)
-    far_bottom = send(from_right[half:], left)
-    from_left_twin = send(from_left, swap)
-    from_right_twin = send(from_right, swap)
-    twin = send(out_grad, swap)
-    acc = attn_add(None, [out_grad, twin], own_columns, w, "attn_own")
+    from_left, from_right, kv_sums, queries, k, v = lax.optimization_barrier(
+        (from_left, from_right, kv_sums, queries, k, v)
+    )
+    q = queries.transpose(1, 0, 2)
+    to_right, to_left, near_left, near_right = lax.optimization_barrier(
+        (from_left[:half], from_right[half:], from_left, from_right)
+    )
+    far_top = send(to_right, right)
+    far_bottom = send(to_left, left)
+    from_left_twin = send(near_left, swap)
+    from_right_twin = send(near_right, swap)
     acc = attn_add(
-        acc,
-        [from_left, from_left_twin, from_right, from_right_twin],
+        None,
+        [out_grad, twin, from_left, from_left_twin, from_right, from_right_twin],
         near_columns,
         w,
         "attn_near",
     )
-    far_top, far_bottom, acc = lax.optimization_barrier((far_top, far_bottom, acc))
-    far_top_twin = send(far_top, swap)
-    far_bottom_twin = send(far_bottom, swap)
+    far_top, far_bottom, acc, q = lax.optimization_barrier((far_top, far_bottom, acc, q))
     far = jnp.concatenate([far_top, far_bottom], 0)
-    far_twin = jnp.concatenate([far_top_twin, far_bottom_twin], 0)
-    grad, qg_local, qg_total = attn_last(far, far_twin, far_columns, w, acc, q)
+    far_twin = send(far, swap)
+    acc = attn_add(acc, [far], far_columns[0], w, "attn_far")
+    far_twin, acc = lax.optimization_barrier((far_twin, acc))
+    grad, qg_local, qg_total = attn_last(far_twin, far_columns[1], w, acc, q)
 
     both = jnp.concatenate([qg_total.reshape(shards, rows, depth), kv_sums], 1)
     both = lax.all_to_all(both, "seq", 0, 0, tiled=True)
@@ -335,10 +340,10 @@
     before = both[:, rows:].reshape(heads, depth, depth)
     after = lax.all_to_all(qg_sums, "seq", 0, 0, tiled=True).reshape(heads, depth, depth)
 
-    qi, ki, vi = inner(q, k, v, grad)
-    ki, vi, qg_local = in_hbm(ki), in_hbm(vi), in_hbm(qg_local)
+    qi, ki, vi = inner(q, k, v, grad, qg_local)
+    ki, vi = in_hbm(ki), in_hbm(vi)
     query_grad = query_out(grad, qi, kv_local, before, factor)
-    key_grad, value_grad = key_value_out(k, v, ki, vi, qg_local, after, factor)
+    key_grad, value_grad = key_value_out(k, v, ki, vi, after, factor)
     return query_grad, key_grad, value_grad
 
 

time: 96.4 us -> 92.4 us (0.959)
  blocking collectives: 20.9 us -> 42.5 us
  starting transfers between devices: 25.1 us -> 12.9 us
  waiting for transfers between devices: 14.8 us -> 7.98 us
  Pallas kernels: 24.3 us -> 21.4 us
  local copies, waits for them, and re-layouts: 7.93 us -> 5.17 us
    all_to_all x0 -> x1, blocking collectives: none -> 20.6 us  [body(): lax.all_to_all(kv_total.reshape(shards, rows, depth), 'seq', 0, 0, tiled=...]
    all_to_all x1 -> x0, starting transfers between devices: 11.7 us -> none  [body(): lax.all_to_all(kv_total.reshape(shards, rows, depth), 'seq', 0, 0, tiled=...]
    all_to_all x1 -> x0, waiting for transfers between devices: 9.26 us -> none  [body(): lax.all_to_all(kv_total.reshape(shards, rows, depth), 'seq', 0, 0, tiled=...]
    ppermute x9 -> x8, waiting for transfers between devices: 4.55 us -> 7.98 us  [send(): return lax.ppermute(array, 'head', pairs)]
    unnamed x19 -> x17, local copies, waits for them, and re-layouts: 5.48 us -> 3.01 us
    slice x2, local copies, waits for them, and re-layouts: 2.15 us -> 0.07 us  [the longest x1 0.04 us: body(): from_left[:half]]
    transpose x1, local copies, waits for them, and re-layouts: 0.27 us -> 1.81 us  [body(): v = value_rows.transpose(1, 0, 2)]
    pallas_call x1, Pallas kernels: 3.61 us -> 2.37 us  [attn_last(): pl.pallas_call(lambda *refs: attn_last_kernel(heads, *refs), grid_spec=pl...]
  transfers between devices with their start and end apart: 11 -> 9, of which waited for: 5 -> 3; matrix products, arithmetic and copies ran while one was open for 4% -> 2% of each run, Pallas kernels for 18% -> 17%
where the time goes in v3:
time: 92.4 us; the launch traced here: 91.2 us
  blocking collectives  42.5 us (46%)
  Pallas kernels  21.4 us (23%)
  starting transfers between devices  12.9 us (14%)
  waiting for transfers between devices  7.98 us (9%)
  local copies, waits for them, and re-layouts  5.17 us (6%)
    all_to_all x1, blocking collectives, body(): both = lax.all_to_all(both, 'seq', 0, 0, tiled=True)  21.9 us
    all_to_all x1, blocking collectives, body(): lax.all_to_all(kv_total.reshape(shards, rows, depth), 'seq', 0, 0, tiled=...  20.6 us
    ppermute x8, waiting for transfers between devices, send(): return lax.ppermute(array, 'head', pairs)  7.98 us
    ppermute x8, starting transfers between devices, send(): return lax.ppermute(array, 'head', pairs)  7.26 us
    pallas_call x2, Pallas kernels, attn_add(): pl.pallas_call(lambda i, *refs: attn_add_kernel(count, *(refs if first el...  6.41 us
    pallas_call x1, Pallas kernels, inner(): pl.pallas_call(lambda *refs: inner_kernel(heads, *refs), grid=(tokens //...  5.78 us
    all_to_all x1, starting transfers between devices, body(): lax.all_to_all(qg_sums, 'seq', 0, 0, tiled=True)  5.61 us
    pallas_call x1, Pallas kernels, key_value_out(): pl.pallas_call(lambda *refs: key_value_kernel(heads, factor, *refs), grid...  3.25 us
  transfers between devices with their start and end apart: 9, of which 3 were waited for; matrix products, arithmetic and copies ran while one was open for 2% of the time, Pallas kernels for 17%

profile of v3, /device:TPU:8, one launch (start us, length us, event | category | flops | bytes accessed | tf_op | source)
XLA Modules:
  0.0 91.2 jit_solution(7670232206999686996)
XLA Ops:
  0.7 0.1 stack.33.i
  0.8 0.0 collective-permute-start.2
  0.8 1.6 %collective-permute-start = (bf16[1024,512]{1,0:T(8,128)(2,1)}, bf16[1024,512]{1,0:T(8,128)(2,1)S(1)}, u32[]{:S(2)}, u32[]{:S(2)}) collective-permute-start(bf16[1024,512]{1,0:T(8,128)(2,1)} %refs_0_), channel_id=1, source_target_pairs={{0,2},{1,3},{2,4},{3,5},{4,6},{5,7},{6,0},{7,1},{8,10},{9,11},{10,... | collective-permute-start | bytes 3145736 | tf_op jit(solution)/shard_map/ppermute | solution.py:270
  2.4 1.7 %collective-permute-start.1 = (bf16[1024,512]{1,0:T(8,128)(2,1)}, bf16[1024,512]{1,0:T(8,128)(2,1)S(1)}, u32[]{:S(2)}, u32[]{:S(2)}) collective-permute-start(bf16[1024,512]{1,0:T(8,128)(2,1)} %refs_0_), channel_id=1, source_target_pairs={{0,6},{1,7},{2,0},{3,1},{4,2},{5,3},{6,4},{7,5},{8,14},{9,15},{10,... | collective-permute-start | bytes 3145736 | tf_op jit(solution)/shard_map/ppermute | solution.py:270
  4.2 1.8 %copy_bitcast_fusion.1 = (bf16[4,1024,128]{2,1,0:T(8,128)(2,1)S(1)}, bf16[4,1024,128]{2,1,0:T(8,128)(2,1)S(1)}) fusion(bf16[1024,4,128]{2,1,0:T(4,128)(2,1)} %param.7, bf16[1024,4,128]{2,1,0:T(4,128)(2,1)} %param.6), kind=kLoop, calls=%fused_computation.5 | loop fusion | bytes 4194304 | tf_op jit(solution)/shard_map/transpose | solution.py:295
  6.0 0.0 copy-start.6
  6.0 0.0 copy-start.3
  6.0 2.2 %kv_states.1 = (f32[4,4,128,128]{3,2,1,0:T(8,128)}, bf16[4,128,128]{2,1,0:T(8,128)(2,1)S(1)}) custom-call(bf16[4,1024,128]{2,1,0:T(8,128)(2,1)S(1)} %get-tuple-element.65.refs_0_.refs_1_, bf16[4,1024,128]{2,1,0:T(8,128)(2,1)S(1)} %get-tuple-element.66.refs_1_.refs_2_), custom_call_target="tpu_custom_call" | custom-call | tf_op jit(solution)/shard_map/kv_states/pallas_call | solution.py:49
  8.2 0.0 collective-permute-done.2.refs_1_
  8.2 20.6 %all_to_all.15 = bf16[32,16,128]{2,1,0:T(8,128)(2,1)S(1)} all-to-all(bf16[32,16,128]{2,1,0:T(8,128)(2,1)S(1)} %bitcast.48), channel_id=1, replica_groups=mesh['seq'=32,'head'=8] {'seq'}, dimensions={0} | all-to-all | bytes 262144 | tf_op jit(solution)/shard_map/all_to_all | solution.py:305
  28.8 0.2 fusion
  29.0 0.0 collective-permute-done.refs_2_
  29.0 0.0 collective-permute-done.1.refs_4_
  29.0 0.0 copy-start
  29.1 0.1 collective-permute-start.5
  29.2 0.5 collective-permute-start.6
  29.7 0.3 collective-permute-start.3
  30.0 2.9 %collective-permute-start.4 = (bf16[512,512]{1,0:T(8,128)(2,1)S(1)}, bf16[512,512]{1,0:T(8,128)(2,1)S(1)}, u32[]{:S(2)}, u32[]{:S(2)}) collective-permute-start(bf16[512,512]{1,0:T(8,128)(2,1)S(1)} %slice.13), channel_id=1, source_target_pairs={{0,6},{1,7},{2,0},{3,1},{4,2},{5,3},{6,4},{7,5},{8,14},{9,15},{10,... | collective-permute-start | bytes 1572872 | tf_op jit(solution)/shard_map/ppermute | solution.py:270
  32.9 0.0 copy-done.6
  32.9 0.1 copy.26
  33.1 0.0 collective-permute-done.5.refs_3_
  33.1 0.3 collective-permute-done.6.refs_5_
  33.4 0.0 copy-done.3
  33.4 0.0 copy-done
  33.4 5.0 %attn_near.1.refs_0_ = f32[1024,512]{1,0:T(8,128)S(1)} custom-call(s32[6]{0:T(128)S(1)} %stack.33.i, bf16[1024,512]{1,0:T(8,128)(2,1)S(1)} %copy-done.3, bf16[1024,512]{1,0:T(8,128)(2,1)S(1)} %collective-permute-done.2.refs_1_, bf16[1024,512]{1,0:T(8,128)(2,1)S(1)} %collective-permute-done.refs_2_, bf16[1024,512]{1,0:T(8,128)(2,1)S(1)} %collective-permute-done.5.refs_3_, ...), custom_call_target="tpu_custom_call" | custom-call | flops 3221225472 | bytes 2097152 | tf_op jit(solution)/shard_map/attn_near/pallas_call | solution.py:83
  38.3 6.5 %collective-permute-done.3 = bf16[512,512]{1,0:T(8,128)(2,1)S(1)} collective-permute-done((bf16[512,512]{1,0:T(8,128)(2,1)S(1)}, bf16[512,512]{1,0:T(8,128)(2,1)S(1)}, u32[]{:S(2)}, u32[]{:S(2)}) %collective-permute-start.3) | collective-permute-done | bytes 524320 | tf_op jit(solution)/shard_map/ppermute | solution.py:270
  44.8 0.0 collective-permute-done.4
  44.9 0.1 collective-permute-start.7
  45.0 1.5 %attn_far.1.refs_3_ = f32[1024,512]{1,0:T(8,128)S(1)} custom-call(s32[1]{0:T(128)} %bitcast.6.i, f32[1024,512]{1,0:T(8,128)S(1)} %attn_near.1.refs_0_, bf16[1024,512]{1,0:T(8,128)(2,1)S(1)} %constant_dynamic-update-slice_fusion.refs_1_, bf16[512,4096]{1,0:T(8,128)(2,1)S(1)} %bitcast.42), custom_call_target="tpu_custom_call" | custom-call | flops 536870912 | bytes 2097152 | tf_op jit(solution)/shard_map/attn_far/pallas_call | solution.py:83
  46.5 1.2 %collective-permute-done.7.refs_1_ = bf16[1024,512]{1,0:T(8,128)(2,1)S(1)} collective-permute-done((bf16[1024,512]{1,0:T(8,128)(2,1)S(1)}, bf16[1024,512]{1,0:T(8,128)(2,1)S(1)}, u32[]{:S(2)}, u32[]{:S(2)}) %collective-permute-start.7) | collective-permute-done | bytes 1048608 | tf_op jit(solution)/shard_map/ppermute | solution.py:270
  47.7 2.4 %attn_last.1 = (bf16[1024,512]{1,0:T(8,128)(2,1)}, bf16[4,4,128,128]{3,2,1,0:T(8,128)(2,1)}, bf16[4,128,128]{2,1,0:T(8,128)(2,1)S(1)}) custom-call(s32[1]{0:T(128)} %bitcast.7.refs_0_, bf16[1024,512]{1,0:T(8,128)(2,1)S(1)} %collective-permute-done.7.refs_1_, bf16[512,4096]{1,0:T(8,128)(2,1)S(1)} %bitcast.43, f32[1024,512]{1,0:T(8,128)S(1)} %attn_far.1.refs_3_, ...), custom_call_target="tpu_custom_call" | custom-call | flops 1342177280 | bytes 2097152 | tf_op jit(solution)/shard_map/attn_last/pallas_call | solution.py:124
  50.1 21.9 %all_to_all.16 = bf16[32,32,128]{2,1,0:T(8,128)(2,1)S(1)} all-to-all(bf16[32,32,128]{2,1,0:T(8,128)(2,1)S(1)} %pad_maximum_fusion), channel_id=1, replica_groups=mesh['seq'=32,'head'=8] {'seq'}, dimensions={0} | all-to-all | bytes 524288 | tf_op jit(solution)/shard_map/all_to_all | solution.py:338
  72.0 0.2 fusion.1
  72.1 0.7 copy.14
  72.8 5.6 %all-to-all-start.2 = ((bf16[32,16,128]{2,1,0:T(8,128)(2,1)}), bf16[32,16,128]{2,1,0:T(8,128)(2,1)S(1)}, u32[]{:S(2)}, u32[]{:S(2)}) async-start(bf16[32,16,128]{2,1,0:T(8,128)(2,1)} %bitcast.23), calls=%async_computation.2 | async-start | bytes 262144 | tf_op jit(solution)/shard_map/all_to_all | solution.py:341
  78.4 0.0 copy-start.1
  78.4 1.2 %copy-done.1 = bf16[1024,512]{1,0:T(8,128)(2,1)S(1)} copy-done((bf16[1024,512]{1,0:T(8,128)(2,1)S(1)}, bf16[1024,512]{1,0:T(8,128)(2,1)}, u32[]{:S(2)}) %copy-start.1) | copy-done | bytes 1048600
  79.7 0.0 copy-start.5
  79.7 1.0 %copy-done.5 = bf16[4,4,128,128]{3,2,1,0:T(8,128)(2,1)S(1)} copy-done((bf16[4,4,128,128]{3,2,1,0:T(8,128)(2,1)S(1)}, bf16[4,4,128,128]{3,2,1,0:T(8,128)(2,1)}, u32[]{:S(2)}) %copy-start.5) | copy-done | bytes 524312
  80.7 0.0 copy-start.2
  80.7 0.0 copy-start.4
  80.7 5.8 %inner.1 = (f32[1024,512]{1,0:T(8,128)S(1)}, bf16[1024,512]{1,0:T(8,128)(2,1)}, bf16[1024,512]{1,0:T(8,128)(2,1)}) custom-call(bf16[4,1024,128]{2,1,0:T(8,128)(2,1)S(1)} %bitcast.45, bf16[4,1024,128]{2,1,0:T(8,128)(2,1)S(1)} %get-tuple-element.65.refs_0_.refs_1_, bf16[4,1024,128]{2,1,0:T(8,128)(2,1)S(1)} %get-tuple-element.66.refs_1_.refs_2_, ...), custom_call_target="tpu_custom_call" | custom-call | tf_op jit(solution)/shard_map/inner/pallas_call | solution.py:174
  86.5 0.0 copy-done.2
  86.5 0.0 copy-done.4
  86.5 1.4 %query_out.1 = bf16[1024,4,128]{2,1,0:T(4,128)(2,1)} custom-call(bf16[1024,512]{1,0:T(8,128)(2,1)S(1)} %copy-done.2, f32[1024,512]{1,0:T(8,128)S(1)} %get-tuple-element.68.refs_1_, f32[4,4,128,128]{3,2,1,0:T(8,128)S(1)} %copy-done.4, bf16[4,128,128]{2,1,0:T(8,128)(2,1)S(1)} %bitcast.47), custom_call_target="tpu_custom_call" | custom-call | tf_op jit(solution)/shard_map/query_out/pallas_call | solution.py:208
  87.9 0.0 all-to-all-done.2
  87.9 3.3 %key_value_out.1 = (bf16[1024,4,128]{2,1,0:T(4,128)(2,1)}, bf16[1024,4,128]{2,1,0:T(4,128)(2,1)}) custom-call(bf16[4,1024,128]{2,1,0:T(8,128)(2,1)S(1)} %get-tuple-element.65.refs_0_.refs_1_, bf16[4,1024,128]{2,1,0:T(8,128)(2,1)S(1)} %get-tuple-element.66.refs_1_.refs_2_, bf16[1024,512]{1,0:T(8,128)(2,1)} %get-tuple-element.72.refs_2_, ...), custom_call_target="tpu_custom_call" | custom-call | tf_op jit(solution)/shard_map/key_value_out/pallas_call | solution.py:242
  (8 shorter events, 0.2 us)
Async XLA Ops:
  0.8 7.4 %collective-permute-start.2 = (bf16[1024,512]{1,0:T(8,128)(2,1)}, bf16[1024,512]{1,0:T(8,128)(2,1)S(1)}, u32[]{:S(2)}, u32[]{:S(2)}) collective-permute-start(bf16[1024,512]{1,0:T(8,128)(2,1)} %refs_0_), channel_id=1, source_target_pairs={{0,1},{1,0},{2,3},{3,2},{4,5},{5,4},{6,7},{7,6},{8,9},{9,8},{10,11... | collective-permute-start | bytes 3145736 | tf_op jit(solution)/shard_map/ppermute | solution.py:270
  0.8 28.2 %collective-permute-start = (bf16[1024,512]{1,0:T(8,128)(2,1)}, bf16[1024,512]{1,0:T(8,128)(2,1)S(1)}, u32[]{:S(2)}, u32[]{:S(2)}) collective-permute-start(bf16[1024,512]{1,0:T(8,128)(2,1)} %refs_0_), channel_id=1, source_target_pairs={{0,2},{1,3},{2,4},{3,5},{4,6},{5,7},{6,0},{7,1},{8,10},{9,11},{10,... | collective-permute-start | bytes 3145736 | tf_op jit(solution)/shard_map/ppermute | solution.py:270
  2.4 26.6 %collective-permute-start.1 = (bf16[1024,512]{1,0:T(8,128)(2,1)}, bf16[1024,512]{1,0:T(8,128)(2,1)S(1)}, u32[]{:S(2)}, u32[]{:S(2)}) collective-permute-start(bf16[1024,512]{1,0:T(8,128)(2,1)} %refs_0_), channel_id=1, source_target_pairs={{0,6},{1,7},{2,0},{3,1},{4,2},{5,3},{6,4},{7,5},{8,14},{9,15},{10,... | collective-permute-start | bytes 3145736 | tf_op jit(solution)/shard_map/ppermute | solution.py:270
  6.0 27.0 %copy-start.6 = (bf16[1024,4,128]{2,1,0:T(4,128)(2,1)S(1)}, bf16[1024,4,128]{2,1,0:T(4,128)(2,1)}, u32[]{:S(2)}) copy-start(bf16[1024,4,128]{2,1,0:T(4,128)(2,1)} %param.5) | copy-start | bytes 3145732
  6.0 27.4 %copy-start.3 = (bf16[1024,512]{1,0:T(8,128)(2,1)S(1)}, bf16[1024,512]{1,0:T(8,128)(2,1)}, u32[]{:S(2)}) copy-start(bf16[1024,512]{1,0:T(8,128)(2,1)} %refs_0_) | copy-start | bytes 3145732
  29.0 4.4 %copy-start = (bf16[4,128,4096]{2,1,0:T(8,128)(2,1)S(1)}, bf16[4,128,4096]{2,1,0:T(8,128)(2,1)}, u32[]{:S(2)}) copy-start(bf16[4,128,4096]{2,1,0:T(8,128)(2,1)} %param.9) | copy-start | bytes 12582916
  29.1 4.0 %collective-permute-start.5 = (bf16[1024,512]{1,0:T(8,128)(2,1)S(1)}, bf16[1024,512]{1,0:T(8,128)(2,1)S(1)}, u32[]{:S(2)}, u32[]{:S(2)}) collective-permute-start(bf16[1024,512]{1,0:T(8,128)(2,1)S(1)} %collective-permute-done.refs_2_), channel_id=1, source_target_pairs={{0,1},{1,0},{2,3},{3,2},{4,5},{5,4},{6,7},{7,6},{8,9},{9,8},{10,11... | collective-permute-start | bytes 3145736 | tf_op jit(solution)/shard_map/ppermute | solution.py:270
  29.2 4.1 %collective-permute-start.6 = (bf16[1024,512]{1,0:T(8,128)(2,1)S(1)}, bf16[1024,512]{1,0:T(8,128)(2,1)S(1)}, u32[]{:S(2)}, u32[]{:S(2)}) collective-permute-start(bf16[1024,512]{1,0:T(8,128)(2,1)S(1)} %collective-permute-done.1.refs_4_), channel_id=1, source_target_pairs={{0,1},{1,0},{2,3},{3,2},{4,5},{5,4},{6,7},{7,6},{8,9},{9,8},{10,11... | collective-permute-start | bytes 3145736 | tf_op jit(solution)/shard_map/ppermute | solution.py:270
  29.7 15.1 %collective-permute-start.3 = (bf16[512,512]{1,0:T(8,128)(2,1)S(1)}, bf16[512,512]{1,0:T(8,128)(2,1)S(1)}, u32[]{:S(2)}, u32[]{:S(2)}) collective-permute-start(bf16[512,512]{1,0:T(8,128)(2,1)S(1)} %slice.12), channel_id=1, source_target_pairs={{0,2},{1,3},{2,4},{3,5},{4,6},{5,7},{6,0},{7,1},{8,10},{9,11},{10,... | collective-permute-start | bytes 1572872 | tf_op jit(solution)/shard_map/ppermute | solution.py:270
  30.0 14.8 %collective-permute-start.4 = (bf16[512,512]{1,0:T(8,128)(2,1)S(1)}, bf16[512,512]{1,0:T(8,128)(2,1)S(1)}, u32[]{:S(2)}, u32[]{:S(2)}) collective-permute-start(bf16[512,512]{1,0:T(8,128)(2,1)S(1)} %slice.13), channel_id=1, source_target_pairs={{0,6},{1,7},{2,0},{3,1},{4,2},{5,3},{6,4},{7,5},{8,14},{9,15},{10,... | collective-permute-start | bytes 1572872 | tf_op jit(solution)/shard_map/ppermute | solution.py:270
  44.9 2.7 %collective-permute-start.7 = (bf16[1024,512]{1,0:T(8,128)(2,1)S(1)}, bf16[1024,512]{1,0:T(8,128)(2,1)S(1)}, u32[]{:S(2)}, u32[]{:S(2)}) collective-permute-start(bf16[1024,512]{1,0:T(8,128)(2,1)S(1)} %constant_dynamic-update-slice_fusion.refs_1_), channel_id=1, source_target_pairs={{0,1},{1,0},{2,3},{3,2},{4,5},{5,4},{6,7},{7,6},{8,9},{9,8},{10,11... | collective-permute-start | bytes 3145736 | tf_op jit(solution)/shard_map/ppermute | solution.py:270
  72.8 15.1 %all-to-all-start.2 = ((bf16[32,16,128]{2,1,0:T(8,128)(2,1)}), bf16[32,16,128]{2,1,0:T(8,128)(2,1)S(1)}, u32[]{:S(2)}, u32[]{:S(2)}) async-start(bf16[32,16,128]{2,1,0:T(8,128)(2,1)} %bitcast.23), calls=%async_computation.2 | async-start | bytes 262144 | tf_op jit(solution)/shard_map/all_to_all | solution.py:341
  78.4 1.2 %copy-start.1 = (bf16[1024,512]{1,0:T(8,128)(2,1)S(1)}, bf16[1024,512]{1,0:T(8,128)(2,1)}, u32[]{:S(2)}) copy-start(bf16[1024,512]{1,0:T(8,128)(2,1)} %get-tuple-element.64.refs_3_.refs_0_) | copy-start | bytes 3145732
  79.7 1.0 %copy-start.5 = (bf16[4,4,128,128]{3,2,1,0:T(8,128)(2,1)S(1)}, bf16[4,4,128,128]{3,2,1,0:T(8,128)(2,1)}, u32[]{:S(2)}) copy-start(bf16[4,4,128,128]{3,2,1,0:T(8,128)(2,1)} %get-tuple-element.67.refs_4_) | copy-start | bytes 1572868
  80.7 5.8 %copy-start.2 = (bf16[1024,512]{1,0:T(8,128)(2,1)S(1)}, bf16[1024,512]{1,0:T(8,128)(2,1)}, u32[]{:S(2)}) copy-start(bf16[1024,512]{1,0:T(8,128)(2,1)} %get-tuple-element.64.refs_3_.refs_0_) | copy-start | bytes 3145732
  80.7 5.8 %copy-start.4 = (f32[4,4,128,128]{3,2,1,0:T(8,128)S(1)}, f32[4,4,128,128]{3,2,1,0:T(8,128)}, u32[]{:S(2)}) copy-start(f32[4,4,128,128]{3,2,1,0:T(8,128)} %get-tuple-element.69.refs_2_) | copy-start | bytes 3145732

commit v4 on v3

--- a/solution.py
+++ b/solution.py
@@ -64,6 +64,13 @@
     )(k, v)
 
 
+def column_at(shift, other):
+    me = lax.axis_index("head")
+    count = lax.axis_size("head")
+    twin = 1 - 2 * lax.rem(me, 2) if other else 0
+    return lax.rem(me + twin + (2 * shift + count), count)
+
+
 def attn_add_kernel(count, acc_ref, *refs):
     total = None if acc_ref is None else acc_ref[...]
     for i in range(count):
@@ -72,30 +79,27 @@
     refs[-1][...] = total
 
 
-def attn_add(acc, pieces, index, w, name):
+def attn_add(acc, pieces, places, w, name):
     tokens, width = pieces[0].shape
     rows = w.shape[0]
     count = len(pieces)
-    spec = pl.BlockSpec((BLOCK, width), lambda b, i: (b, 0))
-    wide = pl.BlockSpec((BLOCK, rows), lambda b, i: (b, 0))
-    weights = [pl.BlockSpec((rows, width), lambda b, i, j=j: (0, i[j])) for j in range(count)]
+    spec = pl.BlockSpec((BLOCK, width), lambda b: (b, 0))
+    wide = pl.BlockSpec((BLOCK, rows), lambda b: (b, 0))
+    weights = [pl.BlockSpec((rows, width), lambda b, p=p: (0, column_at(*p))) for p in places]
     first = [] if acc is None else [acc]
     return pl.pallas_call(
-        lambda i, *refs: attn_add_kernel(count, *(refs if first else (None, *refs))),
-        grid_spec=pltpu.PrefetchScalarGridSpec(
-            num_scalar_prefetch=1,
-            grid=(tokens // BLOCK,),
-            in_specs=[wide] * len(first) + [spec] * count + weights,
-            out_specs=wide,
-        ),
+        lambda *refs: attn_add_kernel(count, *(refs if first else (None, *refs))),
+        grid=(tokens // BLOCK,),
+        in_specs=[wide] * len(first) + [spec] * count + weights,
+        out_specs=wide,
         out_shape=jax.ShapeDtypeStruct((tokens, rows), F32),
         compiler_params=params(6 + 3 * count),
         cost_estimate=cost(2 * tokens * rows * width * count, 4 * tokens * rows),
         name=name,
-    )(index, *first, *pieces, *([w] * count))
-
-
-def attn_last_kernel(heads, i_ref, a_ref, wa_ref, acc_ref, q_ref, g_ref, after_ref, total_ref, run):
+    )(*first, *pieces, *([w] * count))
+
+
+def attn_last_kernel(heads, a_ref, wa_ref, acc_ref, q_ref, g_ref, after_ref, total_ref, run):
     depth = q_ref.shape[2]
 
     @pl.when(pl.program_id(0) == 0)
@@ -112,33 +116,30 @@
     total_ref[...] = run[...].astype(BF16)
 
 
-def attn_last(a, index, w, acc, q):
+def attn_last(a, place, w, acc, q):
     tokens, width = a.shape
     rows = w.shape[0]
     heads, _, depth = q.shape
     steps = tokens // STEP
     last = steps - 1
     blocks = STEP // BLOCK
-    piece = pl.BlockSpec((STEP, width), lambda s, i: (last - s, 0))
-    wide = pl.BlockSpec((STEP, rows), lambda s, i: (last - s, 0))
+    piece = pl.BlockSpec((STEP, width), lambda s: (last - s, 0))
+    wide = pl.BlockSpec((STEP, rows), lambda s: (last - s, 0))
     return pl.pallas_call(
         lambda *refs: attn_last_kernel(heads, *refs),
-        grid_spec=pltpu.PrefetchScalarGridSpec(
-            num_scalar_prefetch=1,
-            grid=(steps,),
-            in_specs=[
-                piece,
-                pl.BlockSpec((rows, width), lambda s, i: (0, i[0])),
-                wide,
-                pl.BlockSpec((heads, STEP, depth), lambda s, i: (0, last - s, 0)),
-            ],
-            out_specs=[
-                wide,
-                pl.BlockSpec((blocks, heads, depth, depth), lambda s, i: (last - s, 0, 0, 0)),
-                pl.BlockSpec((heads, depth, depth), lambda s, i: (0, 0, 0)),
-            ],
-            scratch_shapes=[pltpu.VMEM((heads, depth, depth), F32)],
-        ),
+        grid=(steps,),
+        in_specs=[
+            piece,
+            pl.BlockSpec((rows, width), lambda s: (0, column_at(*place))),
+            wide,
+            pl.BlockSpec((heads, STEP, depth), lambda s: (0, last - s, 0)),
+        ],
+        out_specs=[
+            wide,
+            pl.BlockSpec((blocks, heads, depth, depth), lambda s: (last - s, 0, 0, 0)),
+            pl.BlockSpec((heads, depth, depth), lambda s: (0, 0, 0)),
+        ],
+        scratch_shapes=[pltpu.VMEM((heads, depth, depth), F32)],
         out_shape=[
             pltpu.HBM((tokens, rows), BF16),
             pltpu.HBM((tokens // BLOCK, heads, depth, depth), BF16),
@@ -147,7 +148,7 @@
         compiler_params=params(18),
         cost_estimate=cost(5 * tokens * rows * width, 4 * tokens * rows),
         name="attn_last",
-    )(index, a, w, acc, q)
+    )(a, w, acc, q)
 
 
 def inner_kernel(heads, q_ref, k_ref, v_ref, g_ref, local_ref, qi_ref, ki_ref, vi_ref):
@@ -273,23 +274,10 @@
     right, left = along(1), along(-1)
     half = tokens // 2
 
-    me = lax.axis_index("head")
-    chip, core = me // 2, me % 2
-
-    def column(shift, other):
-        return 2 * ((chip + shift) % chips) + (1 - core if other else core)
-
     w = out_weight.reshape(heads * depth, -1)
 
-    def columns_of(*shifts):
-        return jnp.stack([column(s, other) for s in shifts for other in (False, True)]).astype(jnp.int32)
-
-    near_columns, far_columns, out_grad = lax.optimization_barrier(
-        (columns_of(0, -1, 1), (columns_of(2)[:1], columns_of(2)[1:]), out_grad)
-    )
     from_left = send(out_grad, right)
     from_right = send(out_grad, left)
-    twin = send(out_grad, swap)
 
     k = key_rows.transpose(1, 0, 2)
     v = value_rows.transpose(1, 0, 2)
@@ -298,8 +286,8 @@
     order = jnp.arange(shards)
     later = (order[:, None] < order[None, :]).astype(BF16)
     earlier = (order[:, None] > order[None, :]).astype(BF16)
-    kv_total, k, v, later, earlier, queries, twin = lax.optimization_barrier(
-        (kv_total, k, v, later, earlier, queries, twin)
+    kv_total, k, v, later, earlier, queries = lax.optimization_barrier(
+        (kv_total, k, v, later, earlier, queries)
     )
     rows = heads * depth // shards
     kv_pieces = lax.all_to_all(kv_total.reshape(shards, rows, depth), "seq", 0, 0, tiled=True)
@@ -309,8 +297,8 @@
         return sums.astype(BF16).reshape(shards, rows, depth)
 
     kv_sums = scan(earlier, kv_pieces)
-    from_left, from_right, kv_sums, queries, k, v = lax.optimization_barrier(
-        (from_left, from_right, kv_sums, queries, k, v)
+    from_left, from_right, kv_sums, queries, k, v, out_grad = lax.optimization_barrier(
+        (from_left, from_right, kv_sums, queries, k, v, out_grad)
     )
     q = queries.transpose(1, 0, 2)
     to_right, to_left, near_left, near_right = lax.optimization_barrier(
@@ -318,21 +306,22 @@
     )
     far_top = send(to_right, right)
     far_bottom = send(to_left, left)
+    twin = send(out_grad, swap)
     from_left_twin = send(near_left, swap)
     from_right_twin = send(near_right, swap)
     acc = attn_add(
         None,
         [out_grad, twin, from_left, from_left_twin, from_right, from_right_twin],
-        near_columns,
+        [(shift, other) for shift in (0, -1, 1) for other in (False, True)],
         w,
         "attn_near",
     )
     far_top, far_bottom, acc, q = lax.optimization_barrier((far_top, far_bottom, acc, q))
     far = jnp.concatenate([far_top, far_bottom], 0)
     far_twin = send(far, swap)
-    acc = attn_add(acc, [far], far_columns[0], w, "attn_far")
+    acc = attn_add(acc, [far], [(2, False)], w, "attn_far")
     far_twin, acc = lax.optimization_barrier((far_twin, acc))
-    grad, qg_local, qg_total = attn_last(far_twin, far_columns[1], w, acc, q)
+    grad, qg_local, qg_total = attn_last(far_twin, (2, True), w, acc, q)
 
     both = jnp.concatenate([qg_total.reshape(shards, rows, depth), kv_sums], 1)
     both = lax.all_to_all(both, "seq", 0, 0, tiled=True)

time: 92.4 us -> 92 us (level)
  transfers between devices with their start and end apart: 9 -> 9, of which waited for: 3 -> 4; matrix products, arithmetic and copies ran while one was open for 2% -> 2% of each run, Pallas kernels for 17% -> 17%
where the time goes in v4:
time: 92 us; the launch traced here: 90.8 us
  blocking collectives  41.9 us (46%)
  Pallas kernels  21 us (23%)
  starting transfers between devices  12.9 us (14%)
  waiting for transfers between devices  8.76 us (10%)
  local copies, waits for them, and re-layouts  5.09 us (6%)
    all_to_all x1, blocking collectives, body(): both = lax.all_to_all(both, 'seq', 0, 0, tiled=True)  21.1 us
    all_to_all x1, blocking collectives, body(): lax.all_to_all(kv_total.reshape(shards, rows, depth), 'seq', 0, 0, tiled=...  20.8 us
    ppermute x8, waiting for transfers between devices, send(): return lax.ppermute(array, 'head', pairs)  8.76 us
    ppermute x8, starting transfers between devices, send(): return lax.ppermute(array, 'head', pairs)  7.33 us
    pallas_call x2, Pallas kernels, attn_add(): pl.pallas_call(lambda *refs: attn_add_kernel(count, *(refs if first else...  5.96 us
    pallas_call x1, Pallas kernels, inner(): pl.pallas_call(lambda *refs: inner_kernel(heads, *refs), grid=(tokens //...  5.78 us
    all_to_all x1, starting transfers between devices, body(): lax.all_to_all(qg_sums, 'seq', 0, 0, tiled=True)  5.61 us
    pallas_call x1, Pallas kernels, key_value_out(): pl.pallas_call(lambda *refs: key_value_kernel(heads, factor, *refs), grid...  3.25 us
  transfers between devices with their start and end apart: 9, of which 4 were waited for; matrix products, arithmetic and copies ran while one was open for 2% of the time, Pallas kernels for 17%

profile of v4, /device:TPU:8, one launch (start us, length us, event | category | flops | bytes accessed | tf_op | source)
XLA Modules:
  0.0 90.8 jit_solution(17038177155458223064)
XLA Ops:
  0.6 1.6 %collective-permute-start = (bf16[1024,512]{1,0:T(8,128)(2,1)}, bf16[1024,512]{1,0:T(8,128)(2,1)S(1)}, u32[]{:S(2)}, u32[]{:S(2)}) collective-permute-start(bf16[1024,512]{1,0:T(8,128)(2,1)} %refs_0_), channel_id=1, source_target_pairs={{0,2},{1,3},{2,4},{3,5},{4,6},{5,7},{6,0},{7,1},{8,10},{9,11},{10,... | collective-permute-start | bytes 3145736 | tf_op jit(solution)/shard_map/ppermute | solution.py:271
  2.2 1.7 %collective-permute-start.1 = (bf16[1024,512]{1,0:T(8,128)(2,1)}, bf16[1024,512]{1,0:T(8,128)(2,1)S(1)}, u32[]{:S(2)}, u32[]{:S(2)}) collective-permute-start(bf16[1024,512]{1,0:T(8,128)(2,1)} %refs_0_), channel_id=1, source_target_pairs={{0,6},{1,7},{2,0},{3,1},{4,2},{5,3},{6,4},{7,5},{8,14},{9,15},{10,... | collective-permute-start | bytes 3145736 | tf_op jit(solution)/shard_map/ppermute | solution.py:271
  3.9 1.8 %copy_bitcast_fusion.1 = (bf16[4,1024,128]{2,1,0:T(8,128)(2,1)S(1)}, bf16[4,1024,128]{2,1,0:T(8,128)(2,1)S(1)}) fusion(bf16[1024,4,128]{2,1,0:T(4,128)(2,1)} %param.7, bf16[1024,4,128]{2,1,0:T(4,128)(2,1)} %param.6), kind=kLoop, calls=%fused_computation.5 | loop fusion | bytes 4194304 | tf_op jit(solution)/shard_map/transpose | solution.py:283
  5.8 0.0 copy-start.3
  5.8 0.0 copy-start.6
  5.8 2.2 %kv_states.1 = (f32[4,4,128,128]{3,2,1,0:T(8,128)}, bf16[4,128,128]{2,1,0:T(8,128)(2,1)S(1)}) custom-call(bf16[4,1024,128]{2,1,0:T(8,128)(2,1)S(1)} %get-tuple-element.57.refs_0_.refs_1_, bf16[4,1024,128]{2,1,0:T(8,128)(2,1)S(1)} %get-tuple-element.58.refs_1_.refs_2_), custom_call_target="tpu_custom_call" | custom-call | tf_op jit(solution)/shard_map/kv_states/pallas_call | solution.py:49
  8.0 20.8 %all_to_all.15 = bf16[32,16,128]{2,1,0:T(8,128)(2,1)S(1)} all-to-all(bf16[32,16,128]{2,1,0:T(8,128)(2,1)S(1)} %bitcast.40), channel_id=1, replica_groups=mesh['seq'=32,'head'=8] {'seq'}, dimensions={0} | all-to-all | bytes 262144 | tf_op jit(solution)/shard_map/all_to_all | solution.py:293
  28.7 0.2 fusion
  28.9 0.0 collective-permute-done.refs_2_
  28.9 0.0 collective-permute-done.1.refs_4_
  29.0 0.0 copy-start
  29.1 0.0 copy-done.3
  29.1 0.1 collective-permute-start.4
  29.2 0.5 collective-permute-start.5
  29.7 0.1 collective-permute-start.6
  29.8 0.3 collective-permute-start.2
  30.0 3.0 %collective-permute-start.3 = (bf16[512,512]{1,0:T(8,128)(2,1)S(1)}, bf16[512,512]{1,0:T(8,128)(2,1)S(1)}, u32[]{:S(2)}, u32[]{:S(2)}) collective-permute-start(bf16[512,512]{1,0:T(8,128)(2,1)S(1)} %slice.13), channel_id=1, source_target_pairs={{0,6},{1,7},{2,0},{3,1},{4,2},{5,3},{6,4},{7,5},{8,14},{9,15},{10,... | collective-permute-start | bytes 1572872 | tf_op jit(solution)/shard_map/ppermute | solution.py:271
  33.0 0.0 copy-done.6
  33.0 0.1 copy.26
  33.1 0.0 collective-permute-done.4.refs_1_
  33.2 0.2 collective-permute-done.5.refs_3_
  33.3 1.5 %collective-permute-done.6.refs_5_ = bf16[1024,512]{1,0:T(8,128)(2,1)S(1)} collective-permute-done((bf16[1024,512]{1,0:T(8,128)(2,1)S(1)}, bf16[1024,512]{1,0:T(8,128)(2,1)S(1)}, u32[]{:S(2)}, u32[]{:S(2)}) %collective-permute-start.6) | collective-permute-done | bytes 1048608 | tf_op jit(solution)/shard_map/ppermute | solution.py:271
  34.8 0.0 copy-done
  34.8 4.5 %attn_near.1.refs_0_ = f32[1024,512]{1,0:T(8,128)S(1)} custom-call(bf16[1024,512]{1,0:T(8,128)(2,1)S(1)} %copy-done.3, bf16[1024,512]{1,0:T(8,128)(2,1)S(1)} %collective-permute-done.4.refs_1_, bf16[1024,512]{1,0:T(8,128)(2,1)S(1)} %collective-permute-done.refs_2_, bf16[1024,512]{1,0:T(8,128)(2,1)S(1)} %collective-permute-done.5.refs_3_, ...), custom_call_target="tpu_custom_call" | custom-call | flops 3221225472 | bytes 2097152 | tf_op jit(solution)/shard_map/attn_near/pallas_call | solution.py:90
  39.3 5.9 %collective-permute-done.2 = bf16[512,512]{1,0:T(8,128)(2,1)S(1)} collective-permute-done((bf16[512,512]{1,0:T(8,128)(2,1)S(1)}, bf16[512,512]{1,0:T(8,128)(2,1)S(1)}, u32[]{:S(2)}, u32[]{:S(2)}) %collective-permute-start.2) | collective-permute-done | bytes 524320 | tf_op jit(solution)/shard_map/ppermute | solution.py:271
  45.2 0.0 collective-permute-done.3
  45.3 0.1 collective-permute-start.7
  45.4 1.5 %attn_far.1.refs_2_ = f32[1024,512]{1,0:T(8,128)S(1)} custom-call(f32[1024,512]{1,0:T(8,128)S(1)} %attn_near.1.refs_0_, bf16[1024,512]{1,0:T(8,128)(2,1)S(1)} %constant_dynamic-update-slice_fusion.refs_1_, bf16[512,4096]{1,0:T(8,128)(2,1)S(1)} %bitcast.34), custom_call_target="tpu_custom_call" | custom-call | flops 536870912 | bytes 2097152 | tf_op jit(solution)/shard_map/attn_far/pallas_call | solution.py:90
  46.9 1.2 %collective-permute-done.7.refs_0_ = bf16[1024,512]{1,0:T(8,128)(2,1)S(1)} collective-permute-done((bf16[1024,512]{1,0:T(8,128)(2,1)S(1)}, bf16[1024,512]{1,0:T(8,128)(2,1)S(1)}, u32[]{:S(2)}, u32[]{:S(2)}) %collective-permute-start.7) | collective-permute-done | bytes 1048608 | tf_op jit(solution)/shard_map/ppermute | solution.py:271
  48.1 2.4 %attn_last.1 = (bf16[1024,512]{1,0:T(8,128)(2,1)}, bf16[4,4,128,128]{3,2,1,0:T(8,128)(2,1)}, bf16[4,128,128]{2,1,0:T(8,128)(2,1)S(1)}) custom-call(bf16[1024,512]{1,0:T(8,128)(2,1)S(1)} %collective-permute-done.7.refs_0_, bf16[512,4096]{1,0:T(8,128)(2,1)S(1)} %bitcast.35, f32[1024,512]{1,0:T(8,128)S(1)} %attn_far.1.refs_2_, bf16[4,1024,128]{2,1,0:T(8,128)(2,1)S(1)} %bitcast.36), custom_call_target="tpu_custom_call" | custom-call | flops 1342177280 | bytes 2097152 | tf_op jit(solution)/shard_map/attn_last/pallas_call | solution.py:128
  50.5 21.1 %all_to_all.16 = bf16[32,32,128]{2,1,0:T(8,128)(2,1)S(1)} all-to-all(bf16[32,32,128]{2,1,0:T(8,128)(2,1)S(1)} %pad_maximum_fusion), channel_id=1, replica_groups=mesh['seq'=32,'head'=8] {'seq'}, dimensions={0} | all-to-all | bytes 524288 | tf_op jit(solution)/shard_map/all_to_all | solution.py:327
  71.6 0.2 fusion.1
  71.8 0.7 copy.14
  72.4 5.6 %all-to-all-start.2 = ((bf16[32,16,128]{2,1,0:T(8,128)(2,1)}), bf16[32,16,128]{2,1,0:T(8,128)(2,1)S(1)}, u32[]{:S(2)}, u32[]{:S(2)}) async-start(bf16[32,16,128]{2,1,0:T(8,128)(2,1)} %bitcast.15), calls=%async_computation.2 | async-start | bytes 262144 | tf_op jit(solution)/shard_map/all_to_all | solution.py:330
  78.1 0.0 copy-start.1
  78.1 1.2 %copy-done.1 = bf16[1024,512]{1,0:T(8,128)(2,1)S(1)} copy-done((bf16[1024,512]{1,0:T(8,128)(2,1)S(1)}, bf16[1024,512]{1,0:T(8,128)(2,1)}, u32[]{:S(2)}) %copy-start.1) | copy-done | bytes 1048600
  79.3 0.0 copy-start.5
  79.3 1.0 %copy-done.5 = bf16[4,4,128,128]{3,2,1,0:T(8,128)(2,1)S(1)} copy-done((bf16[4,4,128,128]{3,2,1,0:T(8,128)(2,1)S(1)}, bf16[4,4,128,128]{3,2,1,0:T(8,128)(2,1)}, u32[]{:S(2)}) %copy-start.5) | copy-done | bytes 524312
  80.3 0.0 copy-start.2
  80.3 0.0 copy-start.4
  80.3 5.8 %inner.1 = (f32[1024,512]{1,0:T(8,128)S(1)}, bf16[1024,512]{1,0:T(8,128)(2,1)}, bf16[1024,512]{1,0:T(8,128)(2,1)}) custom-call(bf16[4,1024,128]{2,1,0:T(8,128)(2,1)S(1)} %bitcast.37, bf16[4,1024,128]{2,1,0:T(8,128)(2,1)S(1)} %get-tuple-element.57.refs_0_.refs_1_, bf16[4,1024,128]{2,1,0:T(8,128)(2,1)S(1)} %get-tuple-element.58.refs_1_.refs_2_, ...), custom_call_target="tpu_custom_call" | custom-call | tf_op jit(solution)/shard_map/inner/pallas_call | solution.py:175
  86.1 0.0 copy-done.2
  86.1 0.0 copy-done.4
  86.1 1.4 %query_out.1 = bf16[1024,4,128]{2,1,0:T(4,128)(2,1)} custom-call(bf16[1024,512]{1,0:T(8,128)(2,1)S(1)} %copy-done.2, f32[1024,512]{1,0:T(8,128)S(1)} %get-tuple-element.60.refs_1_, f32[4,4,128,128]{3,2,1,0:T(8,128)S(1)} %copy-done.4, bf16[4,128,128]{2,1,0:T(8,128)(2,1)S(1)} %bitcast.39), custom_call_target="tpu_custom_call" | custom-call | tf_op jit(solution)/shard_map/query_out/pallas_call | solution.py:209
  87.6 0.0 all-to-all-done.2
  87.6 3.3 %key_value_out.1 = (bf16[1024,4,128]{2,1,0:T(4,128)(2,1)}, bf16[1024,4,128]{2,1,0:T(4,128)(2,1)}) custom-call(bf16[4,1024,128]{2,1,0:T(8,128)(2,1)S(1)} %get-tuple-element.57.refs_0_.refs_1_, bf16[4,1024,128]{2,1,0:T(8,128)(2,1)S(1)} %get-tuple-element.58.refs_1_.refs_2_, bf16[1024,512]{1,0:T(8,128)(2,1)} %get-tuple-element.64.refs_2_, ...), custom_call_target="tpu_custom_call" | custom-call | tf_op jit(solution)/shard_map/key_value_out/pallas_call | solution.py:243
  (8 shorter events, 0.2 us)
Async XLA Ops:
  0.6 28.3 %collective-permute-start = (bf16[1024,512]{1,0:T(8,128)(2,1)}, bf16[1024,512]{1,0:T(8,128)(2,1)S(1)}, u32[]{:S(2)}, u32[]{:S(2)}) collective-permute-start(bf16[1024,512]{1,0:T(8,128)(2,1)} %refs_0_), channel_id=1, source_target_pairs={{0,2},{1,3},{2,4},{3,5},{4,6},{5,7},{6,0},{7,1},{8,10},{9,11},{10,... | collective-permute-start | bytes 3145736 | tf_op jit(solution)/shard_map/ppermute | solution.py:271
  2.2 26.8 %collective-permute-start.1 = (bf16[1024,512]{1,0:T(8,128)(2,1)}, bf16[1024,512]{1,0:T(8,128)(2,1)S(1)}, u32[]{:S(2)}, u32[]{:S(2)}) collective-permute-start(bf16[1024,512]{1,0:T(8,128)(2,1)} %refs_0_), channel_id=1, source_target_pairs={{0,6},{1,7},{2,0},{3,1},{4,2},{5,3},{6,4},{7,5},{8,14},{9,15},{10,... | collective-permute-start | bytes 3145736 | tf_op jit(solution)/shard_map/ppermute | solution.py:271
  5.8 23.3 %copy-start.3 = (bf16[1024,512]{1,0:T(8,128)(2,1)S(1)}, bf16[1024,512]{1,0:T(8,128)(2,1)}, u32[]{:S(2)}) copy-start(bf16[1024,512]{1,0:T(8,128)(2,1)} %refs_0_) | copy-start | bytes 3145732
  5.8 27.2 %copy-start.6 = (bf16[1024,4,128]{2,1,0:T(4,128)(2,1)S(1)}, bf16[1024,4,128]{2,1,0:T(4,128)(2,1)}, u32[]{:S(2)}) copy-start(bf16[1024,4,128]{2,1,0:T(4,128)(2,1)} %param.5) | copy-start | bytes 3145732
  29.0 5.9 %copy-start = (bf16[4,128,4096]{2,1,0:T(8,128)(2,1)S(1)}, bf16[4,128,4096]{2,1,0:T(8,128)(2,1)}, u32[]{:S(2)}) copy-start(bf16[4,128,4096]{2,1,0:T(8,128)(2,1)} %param.9) | copy-start | bytes 12582916
  29.1 4.1 %collective-permute-start.4 = (bf16[1024,512]{1,0:T(8,128)(2,1)S(1)}, bf16[1024,512]{1,0:T(8,128)(2,1)S(1)}, u32[]{:S(2)}, u32[]{:S(2)}) collective-permute-start(bf16[1024,512]{1,0:T(8,128)(2,1)S(1)} %copy-done.3), channel_id=1, source_target_pairs={{0,1},{1,0},{2,3},{3,2},{4,5},{5,4},{6,7},{7,6},{8,9},{9,8},{10,11... | collective-permute-start | bytes 3145736 | tf_op jit(solution)/shard_map/ppermute | solution.py:271
  29.2 4.1 %collective-permute-start.5 = (bf16[1024,512]{1,0:T(8,128)(2,1)S(1)}, bf16[1024,512]{1,0:T(8,128)(2,1)S(1)}, u32[]{:S(2)}, u32[]{:S(2)}) collective-permute-start(bf16[1024,512]{1,0:T(8,128)(2,1)S(1)} %collective-permute-done.refs_2_), channel_id=1, source_target_pairs={{0,1},{1,0},{2,3},{3,2},{4,5},{5,4},{6,7},{7,6},{8,9},{9,8},{10,11... | collective-permute-start | bytes 3145736 | tf_op jit(solution)/shard_map/ppermute | solution.py:271
  29.7 5.1 %collective-permute-start.6 = (bf16[1024,512]{1,0:T(8,128)(2,1)S(1)}, bf16[1024,512]{1,0:T(8,128)(2,1)S(1)}, u32[]{:S(2)}, u32[]{:S(2)}) collective-permute-start(bf16[1024,512]{1,0:T(8,128)(2,1)S(1)} %collective-permute-done.1.refs_4_), channel_id=1, source_target_pairs={{0,1},{1,0},{2,3},{3,2},{4,5},{5,4},{6,7},{7,6},{8,9},{9,8},{10,11... | collective-permute-start | bytes 3145736 | tf_op jit(solution)/shard_map/ppermute | solution.py:271
  29.8 15.5 %collective-permute-start.2 = (bf16[512,512]{1,0:T(8,128)(2,1)S(1)}, bf16[512,512]{1,0:T(8,128)(2,1)S(1)}, u32[]{:S(2)}, u32[]{:S(2)}) collective-permute-start(bf16[512,512]{1,0:T(8,128)(2,1)S(1)} %slice.12), channel_id=1, source_target_pairs={{0,2},{1,3},{2,4},{3,5},{4,6},{5,7},{6,0},{7,1},{8,10},{9,11},{10,... | collective-permute-start | bytes 1572872 | tf_op jit(solution)/shard_map/ppermute | solution.py:271
  30.0 15.2 %collective-permute-start.3 = (bf16[512,512]{1,0:T(8,128)(2,1)S(1)}, bf16[512,512]{1,0:T(8,128)(2,1)S(1)}, u32[]{:S(2)}, u32[]{:S(2)}) collective-permute-start(bf16[512,512]{1,0:T(8,128)(2,1)S(1)} %slice.13), channel_id=1, source_target_pairs={{0,6},{1,7},{2,0},{3,1},{4,2},{5,3},{6,4},{7,5},{8,14},{9,15},{10,... | collective-permute-start | bytes 1572872 | tf_op jit(solution)/shard_map/ppermute | solution.py:271
  45.3 2.7 %collective-permute-start.7 = (bf16[1024,512]{1,0:T(8,128)(2,1)S(1)}, bf16[1024,512]{1,0:T(8,128)(2,1)S(1)}, u32[]{:S(2)}, u32[]{:S(2)}) collective-permute-start(bf16[1024,512]{1,0:T(8,128)(2,1)S(1)} %constant_dynamic-update-slice_fusion.refs_1_), channel_id=1, source_target_pairs={{0,1},{1,0},{2,3},{3,2},{4,5},{5,4},{6,7},{7,6},{8,9},{9,8},{10,11... | collective-permute-start | bytes 3145736 | tf_op jit(solution)/shard_map/ppermute | solution.py:271
  72.4 15.1 %all-to-all-start.2 = ((bf16[32,16,128]{2,1,0:T(8,128)(2,1)}), bf16[32,16,128]{2,1,0:T(8,128)(2,1)S(1)}, u32[]{:S(2)}, u32[]{:S(2)}) async-start(bf16[32,16,128]{2,1,0:T(8,128)(2,1)} %bitcast.15), calls=%async_computation.2 | async-start | bytes 262144 | tf_op jit(solution)/shard_map/all_to_all | solution.py:330
  78.1 1.2 %copy-start.1 = (bf16[1024,512]{1,0:T(8,128)(2,1)S(1)}, bf16[1024,512]{1,0:T(8,128)(2,1)}, u32[]{:S(2)}) copy-start(bf16[1024,512]{1,0:T(8,128)(2,1)} %get-tuple-element.56.refs_3_.refs_0_) | copy-start | bytes 3145732
  79.3 1.0 %copy-start.5 = (bf16[4,4,128,128]{3,2,1,0:T(8,128)(2,1)S(1)}, bf16[4,4,128,128]{3,2,1,0:T(8,128)(2,1)}, u32[]{:S(2)}) copy-start(bf16[4,4,128,128]{3,2,1,0:T(8,128)(2,1)} %get-tuple-element.59.refs_4_) | copy-start | bytes 1572868
  80.3 5.8 %copy-start.2 = (bf16[1024,512]{1,0:T(8,128)(2,1)S(1)}, bf16[1024,512]{1,0:T(8,128)(2,1)}, u32[]{:S(2)}) copy-start(bf16[1024,512]{1,0:T(8,128)(2,1)} %get-tuple-element.56.refs_3_.refs_0_) | copy-start | bytes 3145732
  80.3 5.8 %copy-start.4 = (f32[4,4,128,128]{3,2,1,0:T(8,128)S(1)}, f32[4,4,128,128]{3,2,1,0:T(8,128)}, u32[]{:S(2)}) copy-start(f32[4,4,128,128]{3,2,1,0:T(8,128)} %get-tuple-element.61.refs_2_) | copy-start | bytes 3145732

commit v5 on v4

--- a/solution.py
+++ b/solution.py
@@ -272,7 +272,7 @@
 
     swap = [(i, i ^ 1) for i in range(columns)]
     right, left = along(1), along(-1)
-    half = tokens // 2
+    edge = 17 * tokens // 32
 
     w = out_weight.reshape(heads * depth, -1)
 
@@ -302,7 +302,7 @@
     )
     q = queries.transpose(1, 0, 2)
     to_right, to_left, near_left, near_right = lax.optimization_barrier(
-        (from_left[:half], from_right[half:], from_left, from_right)
+        (from_left[:edge], from_right[edge:], from_left, from_right)
     )
     far_top = send(to_right, right)
     far_bottom = send(to_left, left)

time: 92 us -> 91.9 us (level)
  transfers between devices with their start and end apart: 9 -> 9, of which waited for: 4 -> 5; matrix products, arithmetic and copies ran while one was open for 2% -> 2% of each run, Pallas kernels for 17% -> 17%
where the time goes in v5:
time: 91.9 us; the launch traced here: 91.5 us
  blocking collectives  41.9 us (46%)
  Pallas kernels  21 us (23%)
  starting transfers between devices  12.9 us (14%)
  waiting for transfers between devices  9.46 us (10%)
  local copies, waits for them, and re-layouts  5.09 us (6%)
    all_to_all x1, blocking collectives, body(): both = lax.all_to_all(both, 'seq', 0, 0, tiled=True)  21.1 us
    all_to_all x1, blocking collectives, body(): lax.all_to_all(kv_total.reshape(shards, rows, depth), 'seq', 0, 0, tiled=...  20.8 us
    ppermute x8, waiting for transfers between devices, send(): return lax.ppermute(array, 'head', pairs)  9.46 us
    ppermute x8, starting transfers between devices, send(): return lax.ppermute(array, 'head', pairs)  7.33 us
    pallas_call x2, Pallas kernels, attn_add(): pl.pallas_call(lambda *refs: attn_add_kernel(count, *(refs if first else...  5.96 us
    pallas_call x1, Pallas kernels, inner(): pl.pallas_call(lambda *refs: inner_kernel(heads, *refs), grid=(tokens //...  5.78 us
    all_to_all x1, starting transfers between devices, body(): lax.all_to_all(qg_sums, 'seq', 0, 0, tiled=True)  5.61 us
    pallas_call x1, Pallas kernels, key_value_out(): pl.pallas_call(lambda *refs: key_value_kernel(heads, factor, *refs), grid...  3.25 us
  transfers between devices with their start and end apart: 9, of which 5 were waited for; matrix products, arithmetic and copies ran while one was open for 2% of the time, Pallas kernels for 17%

profile of v5, /device:TPU:8, one launch (start us, length us, event | category | flops | bytes accessed | tf_op | source)
XLA Modules:
  0.0 91.5 jit_solution(4027590796055956846)
XLA Ops:
  0.6 1.6 %collective-permute-start = (bf16[1024,512]{1,0:T(8,128)(2,1)}, bf16[1024,512]{1,0:T(8,128)(2,1)S(1)}, u32[]{:S(2)}, u32[]{:S(2)}) collective-permute-start(bf16[1024,512]{1,0:T(8,128)(2,1)} %refs_0_), channel_id=1, source_target_pairs={{0,2},{1,3},{2,4},{3,5},{4,6},{5,7},{6,0},{7,1},{8,10},{9,11},{10,... | collective-permute-start | bytes 3145736 | tf_op jit(solution)/shard_map/ppermute | solution.py:271
  2.2 1.7 %collective-permute-start.1 = (bf16[1024,512]{1,0:T(8,128)(2,1)}, bf16[1024,512]{1,0:T(8,128)(2,1)S(1)}, u32[]{:S(2)}, u32[]{:S(2)}) collective-permute-start(bf16[1024,512]{1,0:T(8,128)(2,1)} %refs_0_), channel_id=1, source_target_pairs={{0,6},{1,7},{2,0},{3,1},{4,2},{5,3},{6,4},{7,5},{8,14},{9,15},{10,... | collective-permute-start | bytes 3145736 | tf_op jit(solution)/shard_map/ppermute | solution.py:271
  3.9 1.8 %copy_bitcast_fusion.1 = (bf16[4,1024,128]{2,1,0:T(8,128)(2,1)S(1)}, bf16[4,1024,128]{2,1,0:T(8,128)(2,1)S(1)}) fusion(bf16[1024,4,128]{2,1,0:T(4,128)(2,1)} %param.7, bf16[1024,4,128]{2,1,0:T(4,128)(2,1)} %param.6), kind=kLoop, calls=%fused_computation.5 | loop fusion | bytes 4194304 | tf_op jit(solution)/shard_map/transpose | solution.py:283
  5.8 0.0 copy-start.3
  5.8 0.0 copy-start.6
  5.8 2.2 %kv_states.1 = (f32[4,4,128,128]{3,2,1,0:T(8,128)}, bf16[4,128,128]{2,1,0:T(8,128)(2,1)S(1)}) custom-call(bf16[4,1024,128]{2,1,0:T(8,128)(2,1)S(1)} %get-tuple-element.57.refs_0_.refs_1_, bf16[4,1024,128]{2,1,0:T(8,128)(2,1)S(1)} %get-tuple-element.58.refs_1_.refs_2_), custom_call_target="tpu_custom_call" | custom-call | tf_op jit(solution)/shard_map/kv_states/pallas_call | solution.py:49
  8.0 20.8 %all_to_all.15 = bf16[32,16,128]{2,1,0:T(8,128)(2,1)S(1)} all-to-all(bf16[32,16,128]{2,1,0:T(8,128)(2,1)S(1)} %bitcast.40), channel_id=1, replica_groups=mesh['seq'=32,'head'=8] {'seq'}, dimensions={0} | all-to-all | bytes 262144 | tf_op jit(solution)/shard_map/all_to_all | solution.py:293
  28.7 0.2 fusion
  28.9 0.0 collective-permute-done.refs_2_
  28.9 0.0 collective-permute-done.1.refs_4_
  29.0 0.0 copy-start
  29.1 0.0 copy-done.3
  29.1 0.1 collective-permute-start.4
  29.2 0.5 collective-permute-start.5
  29.7 0.1 collective-permute-start.6
  29.8 0.3 collective-permute-start.2
  30.0 3.0 %collective-permute-start.3 = (bf16[480,512]{1,0:T(8,128)(2,1)S(1)}, bf16[480,512]{1,0:T(8,128)(2,1)S(1)}, u32[]{:S(2)}, u32[]{:S(2)}) collective-permute-start(bf16[480,512]{1,0:T(8,128)(2,1)S(1)} %slice.13), channel_id=1, source_target_pairs={{0,6},{1,7},{2,0},{3,1},{4,2},{5,3},{6,4},{7,5},{8,14},{9,15},{10,... | collective-permute-start | bytes 1474568 | tf_op jit(solution)/shard_map/ppermute | solution.py:271
  33.0 0.0 copy-done.6
  33.0 0.1 copy.26
  33.1 0.0 collective-permute-done.4.refs_1_
  33.2 0.2 collective-permute-done.5.refs_3_
  33.3 1.5 %collective-permute-done.6.refs_5_ = bf16[1024,512]{1,0:T(8,128)(2,1)S(1)} collective-permute-done((bf16[1024,512]{1,0:T(8,128)(2,1)S(1)}, bf16[1024,512]{1,0:T(8,128)(2,1)S(1)}, u32[]{:S(2)}, u32[]{:S(2)}) %collective-permute-start.6) | collective-permute-done | bytes 1048608 | tf_op jit(solution)/shard_map/ppermute | solution.py:271
  34.8 0.0 copy-done
  34.8 4.5 %attn_near.1.refs_0_ = f32[1024,512]{1,0:T(8,128)S(1)} custom-call(bf16[1024,512]{1,0:T(8,128)(2,1)S(1)} %copy-done.3, bf16[1024,512]{1,0:T(8,128)(2,1)S(1)} %collective-permute-done.4.refs_1_, bf16[1024,512]{1,0:T(8,128)(2,1)S(1)} %collective-permute-done.refs_2_, bf16[1024,512]{1,0:T(8,128)(2,1)S(1)} %collective-permute-done.5.refs_3_, ...), custom_call_target="tpu_custom_call" | custom-call | flops 3221225472 | bytes 2097152 | tf_op jit(solution)/shard_map/attn_near/pallas_call | solution.py:90
  39.3 4.5 %collective-permute-done.3 = bf16[480,512]{1,0:T(8,128)(2,1)S(1)} collective-permute-done((bf16[480,512]{1,0:T(8,128)(2,1)S(1)}, bf16[480,512]{1,0:T(8,128)(2,1)S(1)}, u32[]{:S(2)}, u32[]{:S(2)}) %collective-permute-start.3) | collective-permute-done | bytes 491552 | tf_op jit(solution)/shard_map/ppermute | solution.py:271
  43.8 2.1 %collective-permute-done.2 = bf16[544,512]{1,0:T(8,128)(2,1)S(1)} collective-permute-done((bf16[544,512]{1,0:T(8,128)(2,1)S(1)}, bf16[544,512]{1,0:T(8,128)(2,1)S(1)}, u32[]{:S(2)}, u32[]{:S(2)}) %collective-permute-start.2) | collective-permute-done | bytes 557088 | tf_op jit(solution)/shard_map/ppermute | solution.py:271
  46.0 0.1 collective-permute-start.7
  46.1 1.5 %attn_far.1.refs_2_ = f32[1024,512]{1,0:T(8,128)S(1)} custom-call(f32[1024,512]{1,0:T(8,128)S(1)} %attn_near.1.refs_0_, bf16[1024,512]{1,0:T(8,128)(2,1)S(1)} %constant_dynamic-update-slice_fusion.refs_1_, bf16[512,4096]{1,0:T(8,128)(2,1)S(1)} %bitcast.34), custom_call_target="tpu_custom_call" | custom-call | flops 536870912 | bytes 2097152 | tf_op jit(solution)/shard_map/attn_far/pallas_call | solution.py:90
  47.6 1.2 %collective-permute-done.7.refs_0_ = bf16[1024,512]{1,0:T(8,128)(2,1)S(1)} collective-permute-done((bf16[1024,512]{1,0:T(8,128)(2,1)S(1)}, bf16[1024,512]{1,0:T(8,128)(2,1)S(1)}, u32[]{:S(2)}, u32[]{:S(2)}) %collective-permute-start.7) | collective-permute-done | bytes 1048608 | tf_op jit(solution)/shard_map/ppermute | solution.py:271
  48.8 2.4 %attn_last.1 = (bf16[1024,512]{1,0:T(8,128)(2,1)}, bf16[4,4,128,128]{3,2,1,0:T(8,128)(2,1)}, bf16[4,128,128]{2,1,0:T(8,128)(2,1)S(1)}) custom-call(bf16[1024,512]{1,0:T(8,128)(2,1)S(1)} %collective-permute-done.7.refs_0_, bf16[512,4096]{1,0:T(8,128)(2,1)S(1)} %bitcast.35, f32[1024,512]{1,0:T(8,128)S(1)} %attn_far.1.refs_2_, bf16[4,1024,128]{2,1,0:T(8,128)(2,1)S(1)} %bitcast.36), custom_call_target="tpu_custom_call" | custom-call | flops 1342177280 | bytes 2097152 | tf_op jit(solution)/shard_map/attn_last/pallas_call | solution.py:128
  51.2 21.1 %all_to_all.16 = bf16[32,32,128]{2,1,0:T(8,128)(2,1)S(1)} all-to-all(bf16[32,32,128]{2,1,0:T(8,128)(2,1)S(1)} %pad_maximum_fusion), channel_id=1, replica_groups=mesh['seq'=32,'head'=8] {'seq'}, dimensions={0} | all-to-all | bytes 524288 | tf_op jit(solution)/shard_map/all_to_all | solution.py:327
  72.3 0.2 fusion.1
  72.5 0.7 copy.14
  73.1 5.6 %all-to-all-start.2 = ((bf16[32,16,128]{2,1,0:T(8,128)(2,1)}), bf16[32,16,128]{2,1,0:T(8,128)(2,1)S(1)}, u32[]{:S(2)}, u32[]{:S(2)}) async-start(bf16[32,16,128]{2,1,0:T(8,128)(2,1)} %bitcast.15), calls=%async_computation.2 | async-start | bytes 262144 | tf_op jit(solution)/shard_map/all_to_all | solution.py:330
  78.8 0.0 copy-start.1
  78.8 1.2 %copy-done.1 = bf16[1024,512]{1,0:T(8,128)(2,1)S(1)} copy-done((bf16[1024,512]{1,0:T(8,128)(2,1)S(1)}, bf16[1024,512]{1,0:T(8,128)(2,1)}, u32[]{:S(2)}) %copy-start.1) | copy-done | bytes 1048600
  80.0 0.0 copy-start.5
  80.0 1.0 %copy-done.5 = bf16[4,4,128,128]{3,2,1,0:T(8,128)(2,1)S(1)} copy-done((bf16[4,4,128,128]{3,2,1,0:T(8,128)(2,1)S(1)}, bf16[4,4,128,128]{3,2,1,0:T(8,128)(2,1)}, u32[]{:S(2)}) %copy-start.5) | copy-done | bytes 524312
  81.0 0.0 copy-start.2
  81.0 0.0 copy-start.4
  81.0 5.8 %inner.1 = (f32[1024,512]{1,0:T(8,128)S(1)}, bf16[1024,512]{1,0:T(8,128)(2,1)}, bf16[1024,512]{1,0:T(8,128)(2,1)}) custom-call(bf16[4,1024,128]{2,1,0:T(8,128)(2,1)S(1)} %bitcast.37, bf16[4,1024,128]{2,1,0:T(8,128)(2,1)S(1)} %get-tuple-element.57.refs_0_.refs_1_, bf16[4,1024,128]{2,1,0:T(8,128)(2,1)S(1)} %get-tuple-element.58.refs_1_.refs_2_, ...), custom_call_target="tpu_custom_call" | custom-call | tf_op jit(solution)/shard_map/inner/pallas_call | solution.py:175
  86.8 0.0 copy-done.2
  86.8 0.0 copy-done.4
  86.8 1.4 %query_out.1 = bf16[1024,4,128]{2,1,0:T(4,128)(2,1)} custom-call(bf16[1024,512]{1,0:T(8,128)(2,1)S(1)} %copy-done.2, f32[1024,512]{1,0:T(8,128)S(1)} %get-tuple-element.60.refs_1_, f32[4,4,128,128]{3,2,1,0:T(8,128)S(1)} %copy-done.4, bf16[4,128,128]{2,1,0:T(8,128)(2,1)S(1)} %bitcast.39), custom_call_target="tpu_custom_call" | custom-call | tf_op jit(solution)/shard_map/query_out/pallas_call | solution.py:209
  88.3 0.0 all-to-all-done.2
  88.3 3.3 %key_value_out.1 = (bf16[1024,4,128]{2,1,0:T(4,128)(2,1)}, bf16[1024,4,128]{2,1,0:T(4,128)(2,1)}) custom-call(bf16[4,1024,128]{2,1,0:T(8,128)(2,1)S(1)} %get-tuple-element.57.refs_0_.refs_1_, bf16[4,1024,128]{2,1,0:T(8,128)(2,1)S(1)} %get-tuple-element.58.refs_1_.refs_2_, bf16[1024,512]{1,0:T(8,128)(2,1)} %get-tuple-element.64.refs_2_, ...), custom_call_target="tpu_custom_call" | custom-call | tf_op jit(solution)/shard_map/key_value_out/pallas_call | solution.py:243
  (8 shorter events, 0.2 us)
Async XLA Ops:
  0.6 28.3 %collective-permute-start = (bf16[1024,512]{1,0:T(8,128)(2,1)}, bf16[1024,512]{1,0:T(8,128)(2,1)S(1)}, u32[]{:S(2)}, u32[]{:S(2)}) collective-permute-start(bf16[1024,512]{1,0:T(8,128)(2,1)} %refs_0_), channel_id=1, source_target_pairs={{0,2},{1,3},{2,4},{3,5},{4,6},{5,7},{6,0},{7,1},{8,10},{9,11},{10,... | collective-permute-start | bytes 3145736 | tf_op jit(solution)/shard_map/ppermute | solution.py:271
  2.2 26.8 %collective-permute-start.1 = (bf16[1024,512]{1,0:T(8,128)(2,1)}, bf16[1024,512]{1,0:T(8,128)(2,1)S(1)}, u32[]{:S(2)}, u32[]{:S(2)}) collective-permute-start(bf16[1024,512]{1,0:T(8,128)(2,1)} %refs_0_), channel_id=1, source_target_pairs={{0,6},{1,7},{2,0},{3,1},{4,2},{5,3},{6,4},{7,5},{8,14},{9,15},{10,... | collective-permute-start | bytes 3145736 | tf_op jit(solution)/shard_map/ppermute | solution.py:271
  5.8 23.3 %copy-start.3 = (bf16[1024,512]{1,0:T(8,128)(2,1)S(1)}, bf16[1024,512]{1,0:T(8,128)(2,1)}, u32[]{:S(2)}) copy-start(bf16[1024,512]{1,0:T(8,128)(2,1)} %refs_0_) | copy-start | bytes 3145732
  5.8 27.2 %copy-start.6 = (bf16[1024,4,128]{2,1,0:T(4,128)(2,1)S(1)}, bf16[1024,4,128]{2,1,0:T(4,128)(2,1)}, u32[]{:S(2)}) copy-start(bf16[1024,4,128]{2,1,0:T(4,128)(2,1)} %param.5) | copy-start | bytes 3145732
  29.0 5.9 %copy-start = (bf16[4,128,4096]{2,1,0:T(8,128)(2,1)S(1)}, bf16[4,128,4096]{2,1,0:T(8,128)(2,1)}, u32[]{:S(2)}) copy-start(bf16[4,128,4096]{2,1,0:T(8,128)(2,1)} %param.9) | copy-start | bytes 12582916
  29.1 4.1 %collective-permute-start.4 = (bf16[1024,512]{1,0:T(8,128)(2,1)S(1)}, bf16[1024,512]{1,0:T(8,128)(2,1)S(1)}, u32[]{:S(2)}, u32[]{:S(2)}) collective-permute-start(bf16[1024,512]{1,0:T(8,128)(2,1)S(1)} %copy-done.3), channel_id=1, source_target_pairs={{0,1},{1,0},{2,3},{3,2},{4,5},{5,4},{6,7},{7,6},{8,9},{9,8},{10,11... | collective-permute-start | bytes 3145736 | tf_op jit(solution)/shard_map/ppermute | solution.py:271
  29.2 4.1 %collective-permute-start.5 = (bf16[1024,512]{1,0:T(8,128)(2,1)S(1)}, bf16[1024,512]{1,0:T(8,128)(2,1)S(1)}, u32[]{:S(2)}, u32[]{:S(2)}) collective-permute-start(bf16[1024,512]{1,0:T(8,128)(2,1)S(1)} %collective-permute-done.refs_2_), channel_id=1, source_target_pairs={{0,1},{1,0},{2,3},{3,2},{4,5},{5,4},{6,7},{7,6},{8,9},{9,8},{10,11... | collective-permute-start | bytes 3145736 | tf_op jit(solution)/shard_map/ppermute | solution.py:271
  29.7 5.1 %collective-permute-start.6 = (bf16[1024,512]{1,0:T(8,128)(2,1)S(1)}, bf16[1024,512]{1,0:T(8,128)(2,1)S(1)}, u32[]{:S(2)}, u32[]{:S(2)}) collective-permute-start(bf16[1024,512]{1,0:T(8,128)(2,1)S(1)} %collective-permute-done.1.refs_4_), channel_id=1, source_target_pairs={{0,1},{1,0},{2,3},{3,2},{4,5},{5,4},{6,7},{7,6},{8,9},{9,8},{10,11... | collective-permute-start | bytes 3145736 | tf_op jit(solution)/shard_map/ppermute | solution.py:271
  29.8 16.2 %collective-permute-start.2 = (bf16[544,512]{1,0:T(8,128)(2,1)S(1)}, bf16[544,512]{1,0:T(8,128)(2,1)S(1)}, u32[]{:S(2)}, u32[]{:S(2)}) collective-permute-start(bf16[544,512]{1,0:T(8,128)(2,1)S(1)} %slice.12), channel_id=1, source_target_pairs={{0,2},{1,3},{2,4},{3,5},{4,6},{5,7},{6,0},{7,1},{8,10},{9,11},{10,... | collective-permute-start | bytes 1671176 | tf_op jit(solution)/shard_map/ppermute | solution.py:271
  30.0 13.8 %collective-permute-start.3 = (bf16[480,512]{1,0:T(8,128)(2,1)S(1)}, bf16[480,512]{1,0:T(8,128)(2,1)S(1)}, u32[]{:S(2)}, u32[]{:S(2)}) collective-permute-start(bf16[480,512]{1,0:T(8,128)(2,1)S(1)} %slice.13), channel_id=1, source_target_pairs={{0,6},{1,7},{2,0},{3,1},{4,2},{5,3},{6,4},{7,5},{8,14},{9,15},{10,... | collective-permute-start | bytes 1474568 | tf_op jit(solution)/shard_map/ppermute | solution.py:271
  46.0 2.7 %collective-permute-start.7 = (bf16[1024,512]{1,0:T(8,128)(2,1)S(1)}, bf16[1024,512]{1,0:T(8,128)(2,1)S(1)}, u32[]{:S(2)}, u32[]{:S(2)}) collective-permute-start(bf16[1024,512]{1,0:T(8,128)(2,1)S(1)} %constant_dynamic-update-slice_fusion.refs_1_), channel_id=1, source_target_pairs={{0,1},{1,0},{2,3},{3,2},{4,5},{5,4},{6,7},{7,6},{8,9},{9,8},{10,11... | collective-permute-start | bytes 3145736 | tf_op jit(solution)/shard_map/ppermute | solution.py:271
  73.1 15.1 %all-to-all-start.2 = ((bf16[32,16,128]{2,1,0:T(8,128)(2,1)}), bf16[32,16,128]{2,1,0:T(8,128)(2,1)S(1)}, u32[]{:S(2)}, u32[]{:S(2)}) async-start(bf16[32,16,128]{2,1,0:T(8,128)(2,1)} %bitcast.15), calls=%async_computation.2 | async-start | bytes 262144 | tf_op jit(solution)/shard_map/all_to_all | solution.py:330
  78.8 1.2 %copy-start.1 = (bf16[1024,512]{1,0:T(8,128)(2,1)S(1)}, bf16[1024,512]{1,0:T(8,128)(2,1)}, u32[]{:S(2)}) copy-start(bf16[1024,512]{1,0:T(8,128)(2,1)} %get-tuple-element.56.refs_3_.refs_0_) | copy-start | bytes 3145732
  80.0 1.0 %copy-start.5 = (bf16[4,4,128,128]{3,2,1,0:T(8,128)(2,1)S(1)}, bf16[4,4,128,128]{3,2,1,0:T(8,128)(2,1)}, u32[]{:S(2)}) copy-start(bf16[4,4,128,128]{3,2,1,0:T(8,128)(2,1)} %get-tuple-element.59.refs_4_) | copy-start | bytes 1572868
  81.0 5.8 %copy-start.2 = (bf16[1024,512]{1,0:T(8,128)(2,1)S(1)}, bf16[1024,512]{1,0:T(8,128)(2,1)}, u32[]{:S(2)}) copy-start(bf16[1024,512]{1,0:T(8,128)(2,1)} %get-tuple-element.56.refs_3_.refs_0_) | copy-start | bytes 3145732
  81.0 5.8 %copy-start.4 = (f32[4,4,128,128]{3,2,1,0:T(8,128)S(1)}, f32[4,4,128,128]{3,2,1,0:T(8,128)}, u32[]{:S(2)}) copy-start(f32[4,4,128,128]{3,2,1,0:T(8,128)} %get-tuple-element.61.refs_2_) | copy-start | bytes 3145732

commit v6 on v4

--- a/solution.py
+++ b/solution.py
@@ -120,11 +120,11 @@
     tokens, width = a.shape
     rows = w.shape[0]
     heads, _, depth = q.shape
-    steps = tokens // STEP
+    steps = tokens // BLOCK
     last = steps - 1
-    blocks = STEP // BLOCK
-    piece = pl.BlockSpec((STEP, width), lambda s: (last - s, 0))
-    wide = pl.BlockSpec((STEP, rows), lambda s: (last - s, 0))
+    blocks = 1
+    piece = pl.BlockSpec((BLOCK, width), lambda s: (last - s, 0))
+    wide = pl.BlockSpec((BLOCK, rows), lambda s: (last - s, 0))
     return pl.pallas_call(
         lambda *refs: attn_last_kernel(heads, *refs),
         grid=(steps,),
@@ -132,7 +132,7 @@
             piece,
             pl.BlockSpec((rows, width), lambda s: (0, column_at(*place))),
             wide,
-            pl.BlockSpec((heads, STEP, depth), lambda s: (0, last - s, 0)),
+            pl.BlockSpec((heads, BLOCK, depth), lambda s: (0, last - s, 0)),
         ],
         out_specs=[
             wide,

time: 92 us -> 92.7 us (level)
  no operation moved by 1% of the time
where the time goes in v6:
time: 92.7 us; the launch traced here: 91.5 us
  blocking collectives  41.9 us (45%)
  Pallas kernels  21.6 us (23%)
  starting transfers between devices  12.9 us (14%)
  waiting for transfers between devices  8.76 us (9%)
  local copies, waits for them, and re-layouts  5.09 us (5%)
    all_to_all x1, blocking collectives, body(): both = lax.all_to_all(both, 'seq', 0, 0, tiled=True)  21.1 us
    all_to_all x1, blocking collectives, body(): lax.all_to_all(kv_total.reshape(shards, rows, depth), 'seq', 0, 0, tiled=...  20.8 us
    ppermute x8, waiting for transfers between devices, send(): return lax.ppermute(array, 'head', pairs)  8.76 us
    ppermute x8, starting transfers between devices, send(): return lax.ppermute(array, 'head', pairs)  7.33 us
    pallas_call x2, Pallas kernels, attn_add(): pl.pallas_call(lambda *refs: attn_add_kernel(count, *(refs if first else...  5.96 us
    pallas_call x1, Pallas kernels, inner(): pl.pallas_call(lambda *refs: inner_kernel(heads, *refs), grid=(tokens //...  5.79 us
    all_to_all x1, starting transfers between devices, body(): lax.all_to_all(qg_sums, 'seq', 0, 0, tiled=True)  5.61 us
    pallas_call x1, Pallas kernels, key_value_out(): pl.pallas_call(lambda *refs: key_value_kernel(heads, factor, *refs), grid...  3.25 us
  transfers between devices with their start and end apart: 9, of which 4 were waited for; matrix products, arithmetic and copies ran while one was open for 2% of the time, Pallas kernels for 17%

profile of v6, /device:TPU:8, one launch (start us, length us, event | category | flops | bytes accessed | tf_op | source)
XLA Modules:
  0.0 91.5 jit_solution(2625418050956908779)
XLA Ops:
  0.6 1.6 %collective-permute-start = (bf16[1024,512]{1,0:T(8,128)(2,1)}, bf16[1024,512]{1,0:T(8,128)(2,1)S(1)}, u32[]{:S(2)}, u32[]{:S(2)}) collective-permute-start(bf16[1024,512]{1,0:T(8,128)(2,1)} %refs_0_), channel_id=1, source_target_pairs={{0,2},{1,3},{2,4},{3,5},{4,6},{5,7},{6,0},{7,1},{8,10},{9,11},{10,... | collective-permute-start | bytes 3145736 | tf_op jit(solution)/shard_map/ppermute | solution.py:271
  2.2 1.7 %collective-permute-start.1 = (bf16[1024,512]{1,0:T(8,128)(2,1)}, bf16[1024,512]{1,0:T(8,128)(2,1)S(1)}, u32[]{:S(2)}, u32[]{:S(2)}) collective-permute-start(bf16[1024,512]{1,0:T(8,128)(2,1)} %refs_0_), channel_id=1, source_target_pairs={{0,6},{1,7},{2,0},{3,1},{4,2},{5,3},{6,4},{7,5},{8,14},{9,15},{10,... | collective-permute-start | bytes 3145736 | tf_op jit(solution)/shard_map/ppermute | solution.py:271
  3.9 1.8 %copy_bitcast_fusion.1 = (bf16[4,1024,128]{2,1,0:T(8,128)(2,1)S(1)}, bf16[4,1024,128]{2,1,0:T(8,128)(2,1)S(1)}) fusion(bf16[1024,4,128]{2,1,0:T(4,128)(2,1)} %param.7, bf16[1024,4,128]{2,1,0:T(4,128)(2,1)} %param.6), kind=kLoop, calls=%fused_computation.5 | loop fusion | bytes 4194304 | tf_op jit(solution)/shard_map/transpose | solution.py:283
  5.8 0.0 copy-start.3
  5.8 0.0 copy-start.6
  5.8 2.2 %kv_states.1 = (f32[4,4,128,128]{3,2,1,0:T(8,128)}, bf16[4,128,128]{2,1,0:T(8,128)(2,1)S(1)}) custom-call(bf16[4,1024,128]{2,1,0:T(8,128)(2,1)S(1)} %get-tuple-element.57.refs_0_.refs_1_, bf16[4,1024,128]{2,1,0:T(8,128)(2,1)S(1)} %get-tuple-element.58.refs_1_.refs_2_), custom_call_target="tpu_custom_call" | custom-call | tf_op jit(solution)/shard_map/kv_states/pallas_call | solution.py:49
  8.0 20.8 %all_to_all.15 = bf16[32,16,128]{2,1,0:T(8,128)(2,1)S(1)} all-to-all(bf16[32,16,128]{2,1,0:T(8,128)(2,1)S(1)} %bitcast.40), channel_id=1, replica_groups=mesh['seq'=32,'head'=8] {'seq'}, dimensions={0} | all-to-all | bytes 262144 | tf_op jit(solution)/shard_map/all_to_all | solution.py:293
  28.7 0.2 fusion
  28.9 0.0 collective-permute-done.refs_2_
  28.9 0.0 collective-permute-done.1.refs_4_
  29.0 0.0 copy-start
  29.1 0.0 copy-done.3
  29.1 0.1 collective-permute-start.4
  29.2 0.5 collective-permute-start.5
  29.7 0.1 collective-permute-start.6
  29.8 0.3 collective-permute-start.2
  30.0 3.0 %collective-permute-start.3 = (bf16[512,512]{1,0:T(8,128)(2,1)S(1)}, bf16[512,512]{1,0:T(8,128)(2,1)S(1)}, u32[]{:S(2)}, u32[]{:S(2)}) collective-permute-start(bf16[512,512]{1,0:T(8,128)(2,1)S(1)} %slice.13), channel_id=1, source_target_pairs={{0,6},{1,7},{2,0},{3,1},{4,2},{5,3},{6,4},{7,5},{8,14},{9,15},{10,... | collective-permute-start | bytes 1572872 | tf_op jit(solution)/shard_map/ppermute | solution.py:271
  33.0 0.0 copy-done.6
  33.0 0.1 copy.26
  33.1 0.0 collective-permute-done.4.refs_1_
  33.2 0.2 collective-permute-done.5.refs_3_
  33.3 1.5 %collective-permute-done.6.refs_5_ = bf16[1024,512]{1,0:T(8,128)(2,1)S(1)} collective-permute-done((bf16[1024,512]{1,0:T(8,128)(2,1)S(1)}, bf16[1024,512]{1,0:T(8,128)(2,1)S(1)}, u32[]{:S(2)}, u32[]{:S(2)}) %collective-permute-start.6) | collective-permute-done | bytes 1048608 | tf_op jit(solution)/shard_map/ppermute | solution.py:271
  34.8 0.0 copy-done
  34.8 4.5 %attn_near.1.refs_0_ = f32[1024,512]{1,0:T(8,128)S(1)} custom-call(bf16[1024,512]{1,0:T(8,128)(2,1)S(1)} %copy-done.3, bf16[1024,512]{1,0:T(8,128)(2,1)S(1)} %collective-permute-done.4.refs_1_, bf16[1024,512]{1,0:T(8,128)(2,1)S(1)} %collective-permute-done.refs_2_, bf16[1024,512]{1,0:T(8,128)(2,1)S(1)} %collective-permute-done.5.refs_3_, ...), custom_call_target="tpu_custom_call" | custom-call | flops 3221225472 | bytes 2097152 | tf_op jit(solution)/shard_map/attn_near/pallas_call | solution.py:90
  39.3 5.9 %collective-permute-done.2 = bf16[512,512]{1,0:T(8,128)(2,1)S(1)} collective-permute-done((bf16[512,512]{1,0:T(8,128)(2,1)S(1)}, bf16[512,512]{1,0:T(8,128)(2,1)S(1)}, u32[]{:S(2)}, u32[]{:S(2)}) %collective-permute-start.2) | collective-permute-done | bytes 524320 | tf_op jit(solution)/shard_map/ppermute | solution.py:271
  45.2 0.0 collective-permute-done.3
  45.3 0.1 collective-permute-start.7
  45.4 1.5 %attn_far.1.refs_2_ = f32[1024,512]{1,0:T(8,128)S(1)} custom-call(f32[1024,512]{1,0:T(8,128)S(1)} %attn_near.1.refs_0_, bf16[1024,512]{1,0:T(8,128)(2,1)S(1)} %constant_dynamic-update-slice_fusion.refs_1_, bf16[512,4096]{1,0:T(8,128)(2,1)S(1)} %bitcast.34), custom_call_target="tpu_custom_call" | custom-call | flops 536870912 | bytes 2097152 | tf_op jit(solution)/shard_map/attn_far/pallas_call | solution.py:90
  46.9 1.2 %collective-permute-done.7.refs_0_ = bf16[1024,512]{1,0:T(8,128)(2,1)S(1)} collective-permute-done((bf16[1024,512]{1,0:T(8,128)(2,1)S(1)}, bf16[1024,512]{1,0:T(8,128)(2,1)S(1)}, u32[]{:S(2)}, u32[]{:S(2)}) %collective-permute-start.7) | collective-permute-done | bytes 1048608 | tf_op jit(solution)/shard_map/ppermute | solution.py:271
  48.1 3.0 %attn_last.1 = (bf16[1024,512]{1,0:T(8,128)(2,1)}, bf16[4,4,128,128]{3,2,1,0:T(8,128)(2,1)}, bf16[4,128,128]{2,1,0:T(8,128)(2,1)S(1)}) custom-call(bf16[1024,512]{1,0:T(8,128)(2,1)S(1)} %collective-permute-done.7.refs_0_, bf16[512,4096]{1,0:T(8,128)(2,1)S(1)} %bitcast.35, f32[1024,512]{1,0:T(8,128)S(1)} %attn_far.1.refs_2_, bf16[4,1024,128]{2,1,0:T(8,128)(2,1)S(1)} %bitcast.36), custom_call_target="tpu_custom_call" | custom-call | flops 1342177280 | bytes 2097152 | tf_op jit(solution)/shard_map/attn_last/pallas_call | solution.py:128
  51.1 21.1 %all_to_all.16 = bf16[32,32,128]{2,1,0:T(8,128)(2,1)S(1)} all-to-all(bf16[32,32,128]{2,1,0:T(8,128)(2,1)S(1)} %pad_maximum_fusion), channel_id=1, replica_groups=mesh['seq'=32,'head'=8] {'seq'}, dimensions={0} | all-to-all | bytes 524288 | tf_op jit(solution)/shard_map/all_to_all | solution.py:327
  72.2 0.2 fusion.1
  72.4 0.7 copy.14
  73.1 5.6 %all-to-all-start.2 = ((bf16[32,16,128]{2,1,0:T(8,128)(2,1)}), bf16[32,16,128]{2,1,0:T(8,128)(2,1)S(1)}, u32[]{:S(2)}, u32[]{:S(2)}) async-start(bf16[32,16,128]{2,1,0:T(8,128)(2,1)} %bitcast.15), calls=%async_computation.2 | async-start | bytes 262144 | tf_op jit(solution)/shard_map/all_to_all | solution.py:330
  78.7 0.0 copy-start.1
  78.7 1.2 %copy-done.1 = bf16[1024,512]{1,0:T(8,128)(2,1)S(1)} copy-done((bf16[1024,512]{1,0:T(8,128)(2,1)S(1)}, bf16[1024,512]{1,0:T(8,128)(2,1)}, u32[]{:S(2)}) %copy-start.1) | copy-done | bytes 1048600
  79.9 0.0 copy-start.5
  79.9 1.0 %copy-done.5 = bf16[4,4,128,128]{3,2,1,0:T(8,128)(2,1)S(1)} copy-done((bf16[4,4,128,128]{3,2,1,0:T(8,128)(2,1)S(1)}, bf16[4,4,128,128]{3,2,1,0:T(8,128)(2,1)}, u32[]{:S(2)}) %copy-start.5) | copy-done | bytes 524312
  80.9 0.0 copy-start.2
  80.9 0.0 copy-start.4
  80.9 5.8 %inner.1 = (f32[1024,512]{1,0:T(8,128)S(1)}, bf16[1024,512]{1,0:T(8,128)(2,1)}, bf16[1024,512]{1,0:T(8,128)(2,1)}) custom-call(bf16[4,1024,128]{2,1,0:T(8,128)(2,1)S(1)} %bitcast.37, bf16[4,1024,128]{2,1,0:T(8,128)(2,1)S(1)} %get-tuple-element.57.refs_0_.refs_1_, bf16[4,1024,128]{2,1,0:T(8,128)(2,1)S(1)} %get-tuple-element.58.refs_1_.refs_2_, ...), custom_call_target="tpu_custom_call" | custom-call | tf_op jit(solution)/shard_map/inner/pallas_call | solution.py:175
  86.7 0.0 copy-done.2
  86.7 0.0 copy-done.4
  86.7 1.4 %query_out.1 = bf16[1024,4,128]{2,1,0:T(4,128)(2,1)} custom-call(bf16[1024,512]{1,0:T(8,128)(2,1)S(1)} %copy-done.2, f32[1024,512]{1,0:T(8,128)S(1)} %get-tuple-element.60.refs_1_, f32[4,4,128,128]{3,2,1,0:T(8,128)S(1)} %copy-done.4, bf16[4,128,128]{2,1,0:T(8,128)(2,1)S(1)} %bitcast.39), custom_call_target="tpu_custom_call" | custom-call | tf_op jit(solution)/shard_map/query_out/pallas_call | solution.py:209
  88.2 0.0 all-to-all-done.2
  88.2 3.3 %key_value_out.1 = (bf16[1024,4,128]{2,1,0:T(4,128)(2,1)}, bf16[1024,4,128]{2,1,0:T(4,128)(2,1)}) custom-call(bf16[4,1024,128]{2,1,0:T(8,128)(2,1)S(1)} %get-tuple-element.57.refs_0_.refs_1_, bf16[4,1024,128]{2,1,0:T(8,128)(2,1)S(1)} %get-tuple-element.58.refs_1_.refs_2_, bf16[1024,512]{1,0:T(8,128)(2,1)} %get-tuple-element.64.refs_2_, ...), custom_call_target="tpu_custom_call" | custom-call | tf_op jit(solution)/shard_map/key_value_out/pallas_call | solution.py:243
  (8 shorter events, 0.2 us)
Async XLA Ops:
  0.6 28.3 %collective-permute-start = (bf16[1024,512]{1,0:T(8,128)(2,1)}, bf16[1024,512]{1,0:T(8,128)(2,1)S(1)}, u32[]{:S(2)}, u32[]{:S(2)}) collective-permute-start(bf16[1024,512]{1,0:T(8,128)(2,1)} %refs_0_), channel_id=1, source_target_pairs={{0,2},{1,3},{2,4},{3,5},{4,6},{5,7},{6,0},{7,1},{8,10},{9,11},{10,... | collective-permute-start | bytes 3145736 | tf_op jit(solution)/shard_map/ppermute | solution.py:271
  2.2 26.8 %collective-permute-start.1 = (bf16[1024,512]{1,0:T(8,128)(2,1)}, bf16[1024,512]{1,0:T(8,128)(2,1)S(1)}, u32[]{:S(2)}, u32[]{:S(2)}) collective-permute-start(bf16[1024,512]{1,0:T(8,128)(2,1)} %refs_0_), channel_id=1, source_target_pairs={{0,6},{1,7},{2,0},{3,1},{4,2},{5,3},{6,4},{7,5},{8,14},{9,15},{10,... | collective-permute-start | bytes 3145736 | tf_op jit(solution)/shard_map/ppermute | solution.py:271
  5.8 23.3 %copy-start.3 = (bf16[1024,512]{1,0:T(8,128)(2,1)S(1)}, bf16[1024,512]{1,0:T(8,128)(2,1)}, u32[]{:S(2)}) copy-start(bf16[1024,512]{1,0:T(8,128)(2,1)} %refs_0_) | copy-start | bytes 3145732
  5.8 27.2 %copy-start.6 = (bf16[1024,4,128]{2,1,0:T(4,128)(2,1)S(1)}, bf16[1024,4,128]{2,1,0:T(4,128)(2,1)}, u32[]{:S(2)}) copy-start(bf16[1024,4,128]{2,1,0:T(4,128)(2,1)} %param.5) | copy-start | bytes 3145732
  29.0 5.9 %copy-start = (bf16[4,128,4096]{2,1,0:T(8,128)(2,1)S(1)}, bf16[4,128,4096]{2,1,0:T(8,128)(2,1)}, u32[]{:S(2)}) copy-start(bf16[4,128,4096]{2,1,0:T(8,128)(2,1)} %param.9) | copy-start | bytes 12582916
  29.1 4.1 %collective-permute-start.4 = (bf16[1024,512]{1,0:T(8,128)(2,1)S(1)}, bf16[1024,512]{1,0:T(8,128)(2,1)S(1)}, u32[]{:S(2)}, u32[]{:S(2)}) collective-permute-start(bf16[1024,512]{1,0:T(8,128)(2,1)S(1)} %copy-done.3), channel_id=1, source_target_pairs={{0,1},{1,0},{2,3},{3,2},{4,5},{5,4},{6,7},{7,6},{8,9},{9,8},{10,11... | collective-permute-start | bytes 3145736 | tf_op jit(solution)/shard_map/ppermute | solution.py:271
  29.2 4.1 %collective-permute-start.5 = (bf16[1024,512]{1,0:T(8,128)(2,1)S(1)}, bf16[1024,512]{1,0:T(8,128)(2,1)S(1)}, u32[]{:S(2)}, u32[]{:S(2)}) collective-permute-start(bf16[1024,512]{1,0:T(8,128)(2,1)S(1)} %collective-permute-done.refs_2_), channel_id=1, source_target_pairs={{0,1},{1,0},{2,3},{3,2},{4,5},{5,4},{6,7},{7,6},{8,9},{9,8},{10,11... | collective-permute-start | bytes 3145736 | tf_op jit(solution)/shard_map/ppermute | solution.py:271
  29.7 5.1 %collective-permute-start.6 = (bf16[1024,512]{1,0:T(8,128)(2,1)S(1)}, bf16[1024,512]{1,0:T(8,128)(2,1)S(1)}, u32[]{:S(2)}, u32[]{:S(2)}) collective-permute-start(bf16[1024,512]{1,0:T(8,128)(2,1)S(1)} %collective-permute-done.1.refs_4_), channel_id=1, source_target_pairs={{0,1},{1,0},{2,3},{3,2},{4,5},{5,4},{6,7},{7,6},{8,9},{9,8},{10,11... | collective-permute-start | bytes 3145736 | tf_op jit(solution)/shard_map/ppermute | solution.py:271
  29.8 15.5 %collective-permute-start.2 = (bf16[512,512]{1,0:T(8,128)(2,1)S(1)}, bf16[512,512]{1,0:T(8,128)(2,1)S(1)}, u32[]{:S(2)}, u32[]{:S(2)}) collective-permute-start(bf16[512,512]{1,0:T(8,128)(2,1)S(1)} %slice.12), channel_id=1, source_target_pairs={{0,2},{1,3},{2,4},{3,5},{4,6},{5,7},{6,0},{7,1},{8,10},{9,11},{10,... | collective-permute-start | bytes 1572872 | tf_op jit(solution)/shard_map/ppermute | solution.py:271
  30.0 15.2 %collective-permute-start.3 = (bf16[512,512]{1,0:T(8,128)(2,1)S(1)}, bf16[512,512]{1,0:T(8,128)(2,1)S(1)}, u32[]{:S(2)}, u32[]{:S(2)}) collective-permute-start(bf16[512,512]{1,0:T(8,128)(2,1)S(1)} %slice.13), channel_id=1, source_target_pairs={{0,6},{1,7},{2,0},{3,1},{4,2},{5,3},{6,4},{7,5},{8,14},{9,15},{10,... | collective-permute-start | bytes 1572872 | tf_op jit(solution)/shard_map/ppermute | solution.py:271
  45.3 2.7 %collective-permute-start.7 = (bf16[1024,512]{1,0:T(8,128)(2,1)S(1)}, bf16[1024,512]{1,0:T(8,128)(2,1)S(1)}, u32[]{:S(2)}, u32[]{:S(2)}) collective-permute-start(bf16[1024,512]{1,0:T(8,128)(2,1)S(1)} %constant_dynamic-update-slice_fusion.refs_1_), channel_id=1, source_target_pairs={{0,1},{1,0},{2,3},{3,2},{4,5},{5,4},{6,7},{7,6},{8,9},{9,8},{10,11... | collective-permute-start | bytes 3145736 | tf_op jit(solution)/shard_map/ppermute | solution.py:271
  73.1 15.1 %all-to-all-start.2 = ((bf16[32,16,128]{2,1,0:T(8,128)(2,1)}), bf16[32,16,128]{2,1,0:T(8,128)(2,1)S(1)}, u32[]{:S(2)}, u32[]{:S(2)}) async-start(bf16[32,16,128]{2,1,0:T(8,128)(2,1)} %bitcast.15), calls=%async_computation.2 | async-start | bytes 262144 | tf_op jit(solution)/shard_map/all_to_all | solution.py:330
  78.7 1.2 %copy-start.1 = (bf16[1024,512]{1,0:T(8,128)(2,1)S(1)}, bf16[1024,512]{1,0:T(8,128)(2,1)}, u32[]{:S(2)}) copy-start(bf16[1024,512]{1,0:T(8,128)(2,1)} %get-tuple-element.56.refs_3_.refs_0_) | copy-start | bytes 3145732
  79.9 1.0 %copy-start.5 = (bf16[4,4,128,128]{3,2,1,0:T(8,128)(2,1)S(1)}, bf16[4,4,128,128]{3,2,1,0:T(8,128)(2,1)}, u32[]{:S(2)}) copy-start(bf16[4,4,128,128]{3,2,1,0:T(8,128)(2,1)} %get-tuple-element.59.refs_4_) | copy-start | bytes 1572868
  80.9 5.8 %copy-start.2 = (bf16[1024,512]{1,0:T(8,128)(2,1)S(1)}, bf16[1024,512]{1,0:T(8,128)(2,1)}, u32[]{:S(2)}) copy-start(bf16[1024,512]{1,0:T(8,128)(2,1)} %get-tuple-element.56.refs_3_.refs_0_) | copy-start | bytes 3145732
  80.9 5.8 %copy-start.4 = (f32[4,4,128,128]{3,2,1,0:T(8,128)S(1)}, f32[4,4,128,128]{3,2,1,0:T(8,128)}, u32[]{:S(2)}) copy-start(f32[4,4,128,128]{3,2,1,0:T(8,128)} %get-tuple-element.61.refs_2_) | copy-start | bytes 3145732
